TPU v7x, 32 devices: a whole 2x2x4 slice. The times are simulated.
32 devices in a mesh: resp: 8 (over z, core), seq: 4 (over y, x).
Axes of the slice: x: 2, y: 2, z: 4, core: 2. Of those that a mesh axis runs over, the one named last changes fastest.
Arguments:
- prompt_cache: bfloat16 [512, 576], P('seq'), may hold values from -8 to 8
- channel_scale: float32 [576], replicated, may hold values from 0.5 to 2
- span_cache: bfloat16 [512, 576], P('resp'), may hold values from -6 to 6
- q_latent: bfloat16 [512, 128, 512], P('resp', 'seq'), may hold values from -6 to 6
- q_rope: bfloat16 [512, 8192], P('resp', 'seq'), may hold values from -512 to 512
- d_out: bfloat16 [512, 128, 512], P('resp', 'seq'), may hold values from -6 to 6
- resp_length: int32 [16], replicated, may hold values from 1 to 16384
- span_response: int32 [8], replicated, may hold values from 0 to 15
- span_index: int32 [8], replicated, may hold values from 0 to 255
Outputs:
- grad_q_latent: bfloat16 [512, 128, 512], P('resp', 'seq')
- grad_q_rope: bfloat16 [512, 8192], P('resp', 'seq')
- grad_prompt: float32 [512, 576], P('seq', 'resp')
- grad_span: float32 [512, 576], P(('resp', 'seq'))
All inputs are finite; a program needn't handle non-finite values.
Results may differ from a plain program's by a relative error of at most 0.029.
Values may be sent and summed in bfloat16 or wider, within the bound.
No kernel may reach another device: no remote copies, remote signals or barrier semaphores. Data moves between devices by JAX's collectives and lax.ppermute only.
A program may use at most 64 MiB of HBM per device.

v0:
```python
import math

import jax
import jax.numpy as jnp
from jax import lax
from jax.sharding import PartitionSpec as P

SIGMA = 1.0 / math.sqrt(192.0)


def on_device(
    prompt_cache,
    channel_scale,
    span_cache,
    q_latent,
    q_rope,
    d_out,
    resp_length,
    span_response,
    span_index,
):
    tok_rows, head_local, latent_width = q_latent.shape
    full_width = prompt_cache.shape[1]
    rotary_width = full_width - latent_width
    scaled_cache = (prompt_cache.astype(jnp.float32) * channel_scale).astype(jnp.bfloat16)
    prompt_keys = lax.all_gather(scaled_cache, "seq", axis=0, tiled=True)
    prompt_rows = prompt_keys.shape[0]
    all_keys = jnp.concatenate([prompt_keys, span_cache], axis=0)
    latent_keys = all_keys[:, :latent_width]
    rotary_keys = all_keys[:, latent_width:]
    block_slot = lax.axis_index("resp")
    live_count = jnp.clip(
        resp_length[span_response[block_slot]] - span_index[block_slot] * tok_rows, 0, tok_rows
    )
    query_pos = lax.broadcasted_iota(jnp.int32, (tok_rows, tok_rows), 0)
    key_pos = lax.broadcasted_iota(jnp.int32, (tok_rows, tok_rows), 1)
    block_seen = (key_pos <= query_pos) & (key_pos < live_count)
    visible = jnp.concatenate([jnp.ones((tok_rows, prompt_rows), bool), block_seen], axis=1)
    rotary_query = q_rope.reshape(tok_rows, head_local, rotary_width)
    logits = SIGMA * (
        jnp.einsum("thc,kc->thk", q_latent, latent_keys, preferred_element_type=jnp.float32)
        + jnp.einsum("thc,kc->thk", rotary_query, rotary_keys, preferred_element_type=jnp.float32)
    )
    masked = jnp.where(visible[:, None, :], logits, -jnp.inf)
    highest = jnp.max(masked, axis=2, keepdims=True)
    expo = jnp.where(visible[:, None, :], jnp.exp(logits - highest), 0.0)
    probs = expo / jnp.sum(expo, axis=2, keepdims=True)
    probs_half = probs.astype(jnp.bfloat16)
    valid = lax.iota(jnp.int32, tok_rows) < live_count
    upstream = jnp.where(valid[:, None, None], d_out, jnp.zeros_like(d_out))
    attended = jnp.einsum(
        "thk,kc->thc", probs_half, latent_keys, preferred_element_type=jnp.float32
    )
    delta = jnp.sum(upstream.astype(jnp.float32) * attended, axis=2, keepdims=True)
    dprob = jnp.einsum("thc,kc->thk", upstream, latent_keys, preferred_element_type=jnp.float32)
    dscore = (probs * (dprob - delta)).astype(jnp.bfloat16)
    grad_latent = (
        SIGMA * jnp.einsum("thk,kc->thc", dscore, latent_keys, preferred_element_type=jnp.float32)
    ).astype(jnp.bfloat16)
    grad_rotary = (
        SIGMA * jnp.einsum("thk,kc->thc", dscore, rotary_keys, preferred_element_type=jnp.float32)
    ).astype(jnp.bfloat16)
    grad_rotary = grad_rotary.reshape(tok_rows, head_local * rotary_width)

    def key_grads(lower, count):
        score_part = lax.dynamic_slice_in_dim(dscore, lower, count, 2)
        prob_part = lax.dynamic_slice_in_dim(probs_half, lower, count, 2)
        latent_part = SIGMA * jnp.einsum(
            "thk,thc->kc", score_part, q_latent, preferred_element_type=jnp.float32
        )
        latent_part = latent_part + jnp.einsum(
            "thk,thc->kc", prob_part, upstream, preferred_element_type=jnp.float32
        )
        rotary_part = SIGMA * jnp.einsum(
            "thk,thc->kc", score_part, rotary_query, preferred_element_type=jnp.float32
        )
        return jnp.concatenate([latent_part, rotary_part], axis=1)

    block_terms = key_grads(prompt_rows, tok_rows)
    grad_span = lax.psum_scatter(
        block_terms.astype(jnp.bfloat16), "seq", scatter_dimension=0, tiled=True
    ).astype(jnp.float32)
    resp_count = lax.axis_size("resp")
    column_count = full_width // resp_count
    prompt_terms = key_grads(0, prompt_rows)
    partial_sum = lax.psum_scatter(
        prompt_terms.astype(jnp.bfloat16), "resp", scatter_dimension=1, tiled=True
    )
    summed = lax.psum_scatter(partial_sum, "seq", scatter_dimension=0, tiled=True).astype(
        jnp.float32
    )
    column_scale = lax.dynamic_slice_in_dim(
        channel_scale, lax.axis_index("resp") * column_count, column_count
    )
    grad_prompt = summed * column_scale
    return (grad_latent, grad_rotary, grad_prompt, grad_span)


def solution(mesh):
    return jax.shard_map(
        on_device,
        mesh=mesh,
        in_specs=(
            P("seq", None),
            P(),
            P("resp", None),
            P("resp", "seq", None),
            P("resp", "seq"),
            P("resp", "seq", None),
            P(),
            P(),
            P(),
        ),
        out_specs=(
            P("resp", "seq", None),
            P("resp", "seq"),
            P("seq", "resp"),
            P(("resp", "seq"), None),
        ),
        check_vma=False,
    )
```

profile of v0, /device:TPU:0, one launch (start us, length us, event | category | flops | bytes accessed | tf_op | source)
XLA Modules:
  0.0 142.6 jit_solution(10037975802702702468)
XLA Ops:
  8.1 1.2 multiply_convert_fusion.2
  9.3 11.8 %all_gather.3 = bf16[512,576]{0,1:T(8,128)(2,1)S(1)} all-gather(bf16[128,576]{0,1:T(8,128)(2,1)S(1)} %multiply_convert_fusion.2), channel_id=1, replica_groups=mesh['resp'=8,'seq'=4] {'seq'}, dimensions={0}, use_global_device_ids=true | all-gather | bytes 737280 | tf_op jit(solution)/shard_map/all_gather | solution.py:26
  21.0 1.0 copy.70
  22.1 0.7 fusion.90
  27.9 1.5 %reshape.31 = bf16[64,32,64]{2,1,0:T(8,128)(2,1)S(1)} reshape(bf16[64,2048]{1,0:T(8,128)(2,1)} %param.13) | data formatting | bytes 524288 | tf_op jit(solution)/shard_map/reshape | solution.py:39
  29.4 1.8 %broadcast_select_fusion = bf16[64,32,512]{2,1,0:T(8,128)(2,1)S(1)} fusion(bf16[64,32,512]{2,1,0:T(8,128)(2,1)} %param.14, pred[64]{0:T(512)(128)(4,1)S(1)} %iota_compare_fusion.1), kind=kLoop, calls=%fused_computation.20 | loop fusion | flops 1048576 | bytes 4194368 | tf_op jit(solution)/shard_map/jit(_where)/select_n | solution.py:50
  31.2 0.8 fusion.88
  32.0 2.6 %add_multiply_fusion = f32[576,64,32]{0,1,2:T(8,128)S(1)} fusion(f32[576,64,32]{0,1,2:T(8,128)S(1)} %fusion.88, bf16[576,512,1]{0,1,2:T(8,128)(2,1)S(1)} %fusion.82, bf16[64,32,512]{2,1,0:T(8,128)(2,1)S(1)} %copy-done), kind=kOutput, calls=%fused_computation.6 | convolution fusion | flops 1210318848 | bytes 12124160 | tf_op jit(solution)/shard_map/thc,kc->thk/dot_general | solution.py:41
  34.6 1.9 %fusion.93 = (f32[64,32]{0,1:T(8,128)S(1)}, f32[64,32,576]{2,0,1:T(8,128)S(1)}) fusion(f32[576,64,32]{0,1,2:T(8,128)S(1)} %add_multiply_fusion, pred[64,576]{1,0:T(8,128)(4,1)S(1)} %concatenate.14), kind=kOutput, calls=%fused_computation.73 | output fusion | flops 4719167 | bytes 9482240 | tf_op jit(solution)/shard_map/sub | solution.py:46
  36.9 1.9 %copy-done.1 = f32[64,32,576]{2,0,1:T(8,128)} copy-done((f32[64,32,576]{2,0,1:T(8,128)}, f32[64,32,576]{2,0,1:T(8,128)S(1)}, u32[]{:S(2)}) %copy-start.1) | copy-done | bytes 4718616
  38.8 1.5 %copy-done.6 = bf16[64,32,576]{2,0,1:T(8,128)(2,1)} copy-done((bf16[64,32,576]{2,0,1:T(8,128)(2,1)}, bf16[64,32,576]{2,0,1:T(8,128)(2,1)S(1)}, u32[]{:S(2)}) %copy-start.6) | copy-done | bytes 2359320
  40.3 2.6 %multiply_reduce_fusion = f32[64,32]{1,0:T(8,128)S(1)} fusion(bf16[64,32,512]{2,1,0:T(8,128)(2,1)S(1)} %broadcast_select_fusion, bf16[576,512,1]{0,1,2:T(8,128)(2,1)S(1)} %fusion.82, bf16[64,32,576]{2,0,1:T(8,128)(2,1)S(1)} %fusion.10), kind=kOutput, calls=%fused_computation.9 | convolution fusion | flops 1211103232 | bytes 5054464 | tf_op jit(solution)/shard_map/thk,kc->thc/dot_general | solution.py:51
  42.9 7.1 %multiply_convert_fusion = bf16[64,32,576]{2,0,1:T(8,128)(2,1)S(1)} fusion(f32[64,32]{0,1:T(8,128)S(1)} %copy.77, bf16[576,512,1]{0,1,2:T(8,128)(2,1)S(1)} %fusion.82, f32[64,32,576]{2,0,1:T(8,128)} %copy-done.1, f32[64,32]{0,1:T(8,128)S(1)} %get-tuple-element.4, bf16[64,32,512]{2,1,0:T(8,128)(2,1)} %copy-done.2), kind=kOutput, calls=%fused_computation.5 | convolution fusion | flops 1212678144 | bytes 9781248 | tf_op jit(solution)/shard_map/thc,kc->thk/dot_general | solution.py:55
  50.0 1.6 %fusion.44 = f32[512,512]{0,1:T(8,128)S(1)} fusion(bf16[64,32,512]{2,1,0:T(8,128)(2,1)S(1)} %copy-done, bf16[64,32,576]{2,0,1:T(8,128)(2,1)S(1)} %multiply_convert_fusion), kind=kOutput, calls=%fused_computation.37 | convolution fusion | flops 1074003968 | bytes 5242880 | tf_op jit(solution)/shard_map/thk,thc->kc/dot_general | solution.py:68
  52.7 0.8 copy-done.3
  53.5 1.6 %fusion.49 = bf16[512,512]{0,1:T(8,128)(2,1)S(1)} fusion(f32[512,512]{0,1:T(8,128)S(1)} %fusion.44, bf16[64,32,512]{2,1,0:T(8,128)(2,1)S(1)} %copy-done.3, bf16[64,32,576]{2,0,1:T(8,128)(2,1)S(1)} %copy-done.7), kind=kOutput, calls=%fused_computation.38 | convolution fusion | flops 1074266112 | bytes 5767168 | tf_op jit(solution)/shard_map/thk,thc->kc/dot_general | solution.py:71
  55.1 0.9 pad_maximum_fusion
  56.0 1.5 %fusion.80 = bf16[64,64]{1,0:T(8,128)(2,1)S(1)} fusion(bf16[64,32,576]{2,0,1:T(8,128)(2,1)} %copy-done.5, bf16[64,32,64]{2,1,0:T(8,128)(2,1)S(1)} %reshape.31), kind=kOutput, calls=%fused_computation.50 | convolution fusion | flops 16785408 | bytes 794624 | tf_op jit(solution)/shard_map/thk,thc->kc/dot_general | solution.py:74
  57.6 3.4 %fusion.70 = f32[64,512]{1,0:T(8,128)S(1)} fusion(bf16[64,32,512]{2,1,0:T(8,128)(2,1)S(1)} %copy-done, bf16[64,32,576]{2,0,1:T(8,128)(2,1)} %copy-done.5), kind=kOutput, calls=%fused_computation.45 | convolution fusion | flops 134250496 | bytes 2752512 | tf_op jit(solution)/shard_map/thk,thc->kc/dot_general | solution.py:68
  61.0 3.4 %fusion.73 = bf16[64,512]{1,0:T(8,128)(2,1)S(1)} fusion(f32[64,512]{1,0:T(8,128)S(1)} %fusion.70, bf16[64,32,512]{2,1,0:T(8,128)(2,1)S(1)} %copy-done.4, bf16[64,32,576]{2,0,1:T(8,128)(2,1)} %copy-done.6), kind=kOutput, calls=%fused_computation.46 | convolution fusion | flops 134283264 | bytes 2818048 | tf_op jit(solution)/shard_map/thk,thc->kc/dot_general | solution.py:71
  64.4 0.6 pad_maximum_fusion.2
  65.3 5.2 %multiply_convert_fusion.1 = bf16[64,32,512]{2,1,0:T(8,128)(2,1)} fusion(bf16[576,512,1]{0,1,2:T(8,128)(2,1)S(1)} %fusion.82, bf16[64,32,576]{2,0,1:T(8,128)(2,1)} %copy-done.5), kind=kOutput, calls=%fused_computation.8 | convolution fusion | flops 1210056704 | bytes 5046272 | tf_op jit(solution)/shard_map/thk,kc->thc/dot_general | solution.py:58
  70.5 17.1 %reduce-scatter.5.cloned.1.call-done = bf16[512,72]{0,1:T(8,128)(2,1)} async-done(((bf16[512,576]{0,1:T(8,128)(2,1)}), bf16[512,72]{0,1:T(8,128)(2,1)}) %reduce-scatter.5.cloned.1.call-update) | async-done | bytes 73744 | tf_op jit(solution)/shard_map/reduce_scatter | solution.py:86
  87.6 1.6 %copy.103 = bf16[512,72]{1,0:T(8,128)(2,1)} copy(bf16[512,72]{0,1:T(8,128)(2,1)} %reduce-scatter.5.cloned.1.call-done) | data formatting | bytes 147456
  89.2 2.6 %fusion.54 = bf16[64,32,64]{2,0,1:T(8,128)(2,1)S(1)} fusion(bf16[64,32,576]{2,0,1:T(8,128)(2,1)} %copy-done.5, bf16[576,64,1]{0,1,2:T(8,128)(2,1)S(1)} %copy-done.8), kind=kOutput, calls=%fused_computation.39 | convolution fusion | flops 151257088 | bytes 2695168 | tf_op jit(solution)/shard_map/thk,kc->thc/dot_general | solution.py:61
  91.9 0.8 dynamic_slice.29
  93.0 1.2 reshape.32
  95.4 10.9 %all-reduce.4.cloned.1.call-done = bf16[64,576]{1,0:T(8,128)(2,1)} async-done(((bf16[64,576]{1,0:T(8,128)(2,1)}), bf16[64,576]{1,0:T(8,128)(2,1)}) %all-reduce.4.cloned.1.call-update) | async-done | bytes 73744
  106.2 1.3 dynamic-slice_convert_fusion
  107.6 26.0 %reduce-scatter.7.cloned.1.call-done = bf16[128,72]{1,0:T(8,128)(2,1)} async-done(((bf16[512,72]{1,0:T(8,128)(2,1)}), bf16[128,72]{1,0:T(8,128)(2,1)}) %reduce-scatter.7.cloned.1.call-update) | async-done | bytes 18448
  133.6 0.8 copy.104
  134.5 0.7 convert_multiply_fusion
  (41 shorter events, 4.7 us)
Async XLA Ops:
  8.0 24.0 %copy-start = (bf16[64,32,512]{2,1,0:T(8,128)(2,1)S(1)}, bf16[64,32,512]{2,1,0:T(8,128)(2,1)}, u32[]{:S(2)}) copy-start(bf16[64,32,512]{2,1,0:T(8,128)(2,1)} %param.12) | copy-start | bytes 6291460
  8.0 14.8 %copy-start.9 = (s32[8]{0:T(128)S(1)}, s32[8]{0:T(128)}, u32[]{:S(2)}) copy-start(s32[8]{0:T(128)} %param.16) | copy-start | bytes 100
  8.0 16.7 %copy-start.10 = (s32[8]{0:T(128)S(1)}, s32[8]{0:T(128)}, u32[]{:S(2)}) copy-start(s32[8]{0:T(128)} %param.17) | copy-start | bytes 100
  8.0 17.9 %copy-start.11 = (s32[16]{0:T(128)S(1)}, s32[16]{0:T(128)}, u32[]{:S(2)}) copy-start(s32[16]{0:T(128)} %param.15) | copy-start | bytes 196
  8.0 79.5 %reduce-scatter.5.cloned.1.call-start = ((), (), s32[]{:S(2)}) async-start(), calls=%async_computation.2 | async-start | bytes 663552 | tf_op jit(solution)/shard_map/reduce_scatter | solution.py:86
  22.8 8.4 %copy-start.8 = (bf16[576,64,1]{0,1,2:T(8,128)(2,1)S(1)}, bf16[576,64,1]{0,1,2:T(8,128)(2,1)}, u32[]{:S(2)}) copy-start(bf16[576,64,1]{0,1,2:T(8,128)(2,1)} %fusion.90) | copy-start | bytes 221188
  31.2 5.8 %copy-start.2 = (bf16[64,32,512]{2,1,0:T(8,128)(2,1)}, bf16[64,32,512]{2,1,0:T(8,128)(2,1)S(1)}, u32[]{:S(2)}) copy-start(bf16[64,32,512]{2,1,0:T(8,128)(2,1)S(1)} %broadcast_select_fusion) | copy-start | bytes 6291460
  36.5 2.3 %copy-start.1 = (f32[64,32,576]{2,0,1:T(8,128)}, f32[64,32,576]{2,0,1:T(8,128)S(1)}, u32[]{:S(2)}) copy-start(f32[64,32,576]{2,0,1:T(8,128)S(1)} %get-tuple-element.5) | copy-start | bytes 14155780
  38.8 1.5 %copy-start.6 = (bf16[64,32,576]{2,0,1:T(8,128)(2,1)}, bf16[64,32,576]{2,0,1:T(8,128)(2,1)S(1)}, u32[]{:S(2)}) copy-start(bf16[64,32,576]{2,0,1:T(8,128)(2,1)S(1)} %fusion.10) | copy-start | bytes 7077892
  50.0 1.6 %copy-start.5 = (bf16[64,32,576]{2,0,1:T(8,128)(2,1)}, bf16[64,32,576]{2,0,1:T(8,128)(2,1)S(1)}, u32[]{:S(2)}) copy-start(bf16[64,32,576]{2,0,1:T(8,128)(2,1)S(1)} %multiply_convert_fusion) | copy-start | bytes 7077892
  50.0 2.7 %copy-start.7 = (bf16[64,32,576]{2,0,1:T(8,128)(2,1)S(1)}, bf16[64,32,576]{2,0,1:T(8,128)(2,1)}, u32[]{:S(2)}) copy-start(bf16[64,32,576]{2,0,1:T(8,128)(2,1)} %copy-done.6) | copy-start | bytes 7077892
  51.6 1.9 %copy-start.3 = (bf16[64,32,512]{2,1,0:T(8,128)(2,1)S(1)}, bf16[64,32,512]{2,1,0:T(8,128)(2,1)}, u32[]{:S(2)}) copy-start(bf16[64,32,512]{2,1,0:T(8,128)(2,1)} %copy-done.2) | copy-start | bytes 6291460
  55.9 50.3 %all-reduce.4.cloned.1.call-start = ((), (), s32[]{:S(2)}) async-start(), calls=%async_computation.4 | async-start | bytes 163840
  56.0 5.0 %copy-start.4 = (bf16[64,32,512]{2,1,0:T(8,128)(2,1)S(1)}, bf16[64,32,512]{2,1,0:T(8,128)(2,1)}, u32[]{:S(2)}) copy-start(bf16[64,32,512]{2,1,0:T(8,128)(2,1)} %copy-done.2) | copy-start | bytes 6291460
  65.0 68.6 %reduce-scatter.7.cloned.1.call-start = ((), (), s32[]{:S(2)}) async-start(), calls=%async_computation.3 | async-start | bytes 163840
  89.2 4.9 %copy-start.12 = (u32[32]{0:T(128)S(1)}, u32[32]{0:T(128)}, u32[]{:S(2)}) copy-start(u32[32]{0:T(128)} %constant.42) | copy-start | bytes 388
Sparse Core Ops, SparseCore 0:
  56.1 31.4 reduce-scatter.4
Sparse Core Ops, SparseCore 1:
  65.1 41.1 all-reduce.3
  109.1 24.5 reduce-scatter.6
where the time goes:
time: 143 us
  waiting for transfers between devices  54 us (38%)
  matrix products  32.9 us (23%)
  between operations  19.7 us (14%)
  local copies, waits for them, and re-layouts  14.3 us (10%)
  blocking collectives  11.8 us (8%)
  other arithmetic  9.54 us (7%)
    unnamed x5, waiting for transfers between devices  37 us
    reduce_scatter x1, waiting for transfers between devices, on_device(): lax.psum_scatter(prompt_terms.astype(jnp.bfloat16), 'resp', scatter_dimen...  17.1 us
    all_gather x1, blocking collectives, on_device(): prompt_keys = lax.all_gather(scaled_cache, 'seq', axis=0, tiled=True)  11.8 us
    unnamed x30, local copies, waits for them, and re-layouts  8.75 us
    dot_general x1, matrix products, on_device(): jnp.einsum('thc,kc->thk', upstream, latent_keys, preferred_element_type=j...  7.08 us
    dot_general x1, matrix products, on_device(): jnp.einsum('thk,kc->thc', dscore, latent_keys, preferred_element_type=jnp...  5.21 us
    dot_general x2, matrix products, key_grads(): jnp.einsum('thk,thc->kc', score_part, q_latent, preferred_element_type=jn...  5.01 us
    dot_general x2, matrix products, key_grads(): jnp.einsum('thk,thc->kc', prob_part, upstream, preferred_element_type=jnp...  4.96 us
  transfers between devices with their start and end apart: 3, of which 3 were waited for; matrix products, arithmetic and copies ran while one was open for 16% of the time, Pallas kernels for 0%

commit v1 on v0

v1 whole, which is shorter than its diff:
```python
import functools
import math

import jax
import jax.numpy as jnp
from jax import lax
from jax.experimental import pallas as pl
from jax.experimental.pallas import tpu as pltpu
from jax.sharding import PartitionSpec as P

SIGMA = 1.0 / math.sqrt(192.0)
LOG2E = math.log2(math.e)
F32 = jnp.float32
BF16 = jnp.bfloat16
NT = (((1,), (1,)), ((), ()))
NN = (((1,), (0,)), ((), ()))
TN = (((0,), (0,)), ((), ()))


def dot(a, b, dims):
    return lax.dot_general(a, b, dims, preferred_element_type=F32)


def low_half(shape, half):
    return lax.broadcasted_iota(jnp.int32, shape, len(shape) - 1) < half


def keys_kernel(
    n_resp,
    n_seq,
    heads,
    resp_length,
    span_response,
    span_index,
    scale_ref,
    span_ref,
    q_ref,
    qrope_ref,
    up_ref,
    *refs,
):
    shard_refs = refs[:n_seq]
    mine_ref, theirs_ref, span_out, ds_ref, keys_ref = refs[n_seq : n_seq + 5]
    rope_scr, p_scr, qr_ref = refs[n_seq + 5 :]
    tok, full = span_ref.shape
    rows, latent = q_ref.shape
    rope = full - latent
    shard = shard_refs[0].shape[0]
    prompt = shard * n_seq
    keys = prompt + tok
    my_resp = lax.axis_index("resp")
    my_seq = lax.axis_index("seq")
    live = jnp.clip(
        resp_length[span_response[my_resp]] - span_index[my_resp] * tok, 0, tok
    )

    scale = scale_ref[...]
    for d in range(n_seq):
        k = (shard_refs[d][...].astype(F32) * scale).astype(BF16)
        keys_ref[pl.ds(d * shard, shard), :full] = k
        keys_ref[pl.ds(d * shard, shard), full:] = k[:, latent:]
    keys_ref[pl.ds(prompt, tok), :full] = span_ref[...]
    keys_ref[pl.ds(prompt, tok), full:] = span_ref[:, latent:]

    low = low_half((tok, 2 * rope), rope)
    for j in range(heads // 2):
        x = qrope_ref[:, pl.ds(2 * rope * j, 2 * rope)].astype(F32)
        rope_scr[pl.ds(2 * j, tok, stride=heads), :] = jnp.where(low, x, 0.0)
        rope_scr[pl.ds(2 * j + 1, tok, stride=heads), :] = jnp.where(low, 0.0, x)
    qr_ref[...] = rope_scr[...].astype(BF16)

    step = 256
    for i in range(rows // step):
        at = pl.ds(i * step, step)
        logits = dot(keys_ref[:, :latent], q_ref[at, :], NT) + dot(
            keys_ref[:, latent:], qr_ref[at, :], NT
        )
        dprob = dot(keys_ref[:, :latent], up_ref[at, :], NT)
        key_pos = lax.broadcasted_iota(jnp.int32, (tok, step), 0)
        query_pos = (lax.broadcasted_iota(jnp.int32, (tok, step), 1) + i * step) // heads
        seen = (key_pos <= query_pos) & (key_pos < live)
        own = jnp.where(seen, logits[prompt:], -jnp.inf)
        logits = jnp.concatenate([logits[:prompt], own], axis=0)
        top = jnp.max(logits, axis=0, keepdims=True)
        expo = jnp.exp2((logits - top) * (SIGMA * LOG2E))
        total = jnp.sum(expo, axis=0, keepdims=True)
        weighed = jnp.sum(expo * dprob, axis=0, keepdims=True)
        row_pos = (lax.broadcasted_iota(jnp.int32, (1, step), 1) + i * step) // heads
        inverse = 1.0 / total
        delta = weighed * inverse
        inverse = jnp.where(row_pos < live, inverse, 0.0)
        probs = expo * inverse
        p_scr[:, at] = probs.astype(BF16)
        ds_ref[:, at] = (probs * ((dprob - delta) * SIGMA)).astype(BF16)

    grad_latent = dot(ds_ref[...], q_ref[...], NN) + dot(p_scr[...], up_ref[...], NN)
    grad_rope = dot(ds_ref[...], qr_ref[...], NN)

    piece = tok // n_seq
    own_rope = grad_rope[prompt:]
    own_rope = own_rope + pltpu.roll(own_rope, rope, 1)
    for s in range(n_seq):
        parts = [
            grad_latent[prompt + s * piece : prompt + (s + 1) * piece, c : c + 2 * rope]
            for c in range(0, latent, 2 * rope)
        ]
        parts.append(own_rope[s * piece : (s + 1) * piece])
        span_out[s ^ my_seq] = jnp.concatenate(parts, axis=0).astype(BF16)

    cols = full // n_resp
    odd = (my_resp % 2) == 1
    my_pair = my_resp // 2
    for d in range(n_seq):
        at = slice(d * shard, (d + 1) * shard)
        lat = grad_latent[at].T
        rot = grad_rope[at].T
        whole = jnp.concatenate([lat, rot[:rope] + rot[rope:]], axis=0)
        for z in range(n_resp // 2):
            even_part = whole[2 * z * cols : (2 * z + 1) * cols]
            odd_part = whole[(2 * z + 1) * cols : (2 * z + 2) * cols]
            mine_ref[d, z ^ my_pair] = jnp.where(odd, odd_part, even_part).astype(BF16)
            theirs_ref[d, z ^ my_pair] = jnp.where(odd, even_part, odd_part).astype(BF16)


def query_kernel(heads, ds_ref, keys_ref, out_ref, rope_out, rope_scr):
    rows, latent = out_ref.shape
    width = keys_ref.shape[1]
    rope = (width - latent) // 2
    step = 16 * heads
    for i in range(rows // step):
        at = pl.ds(i * step, step)
        out_ref[at, :] = dot(ds_ref[:, at], keys_ref[:, :latent], TN).astype(BF16)
        rope_scr[...] = dot(ds_ref[:, at], keys_ref[:, latent:], TN)
        low = low_half((16, 2 * rope), rope)
        for j in range(heads // 2):
            even = rope_scr[pl.ds(2 * j, 16, stride=heads), :]
            odd = rope_scr[pl.ds(2 * j + 1, 16, stride=heads), :]
            rope_out[pl.ds(i * 16, 16), pl.ds(2 * rope * j, 2 * rope)] = jnp.where(
                low, even, odd
            ).astype(BF16)


def on_device(
    n_resp,
    n_seq,
    prompt_cache,
    channel_scale,
    span_cache,
    q_latent,
    q_rope,
    d_out,
    resp_length,
    span_response,
    span_index,
):
    tok, heads, latent = q_latent.shape
    shard, full = prompt_cache.shape
    rope = full - latent
    rows = tok * heads
    prompt = shard * n_seq
    keys = prompt + tok
    width = latent + 2 * rope
    cols = full // n_resp
    pairs = n_resp // 2
    piece = tok // n_seq
    span_rows = piece * (latent // (2 * rope) + 1)

    def over_seq(x, d):
        return lax.ppermute(x, "seq", [(i, i ^ d) for i in range(n_seq)])

    def over_resp(x, d):
        return lax.ppermute(x, "resp", [(i, i ^ d) for i in range(n_resp)])

    order = sorted(range(1, n_seq), key=lambda d: -bin(d).count("1"))
    got = {d: over_seq(prompt_cache, d) for d in order}
    shards = [prompt_cache] + [got[d] for d in range(1, n_seq)]

    vmem = pl.BlockSpec(memory_space=pltpu.VMEM)
    smem = pl.BlockSpec(memory_space=pltpu.SMEM)
    q_rows = q_latent.reshape(rows, latent)
    up_rows = d_out.reshape(rows, latent)
    mine, theirs, span, dscore, keys_all = pl.pallas_call(
        functools.partial(keys_kernel, n_resp, n_seq, heads),
        out_shape=(
            jax.ShapeDtypeStruct((n_seq, pairs, cols, shard), BF16),
            jax.ShapeDtypeStruct((n_seq, pairs, cols, shard), BF16),
            jax.ShapeDtypeStruct((n_seq, span_rows, 2 * rope), BF16),
            jax.ShapeDtypeStruct((keys, rows), BF16),
            jax.ShapeDtypeStruct((keys, width), BF16),
        ),
        in_specs=[smem] * 3 + [vmem] * (5 + n_seq),
        out_specs=(vmem,) * 5,
        scratch_shapes=[
            pltpu.VMEM((rows, 2 * rope), F32),
            pltpu.VMEM((keys, rows), BF16),
            pltpu.VMEM((rows, 2 * rope), BF16),
        ],
        compiler_params=pltpu.CompilerParams(vmem_limit_bytes=48 * 1024 * 1024),
        cost_estimate=pl.CostEstimate(
            flops=2 * keys * rows * 4 * latent, bytes_accessed=6 * rows * latent, transcendentals=0
        ),
        name="keys",
    )(
        resp_length,
        span_response,
        span_index,
        channel_scale.reshape(1, full),
        span_cache,
        q_rows,
        q_rope,
        up_rows,
        *shards,
    )

    grad_latent, grad_rope = pl.pallas_call(
        functools.partial(query_kernel, heads),
        out_shape=(
            jax.ShapeDtypeStruct((rows, latent), BF16),
            jax.ShapeDtypeStruct((tok, heads * rope), BF16),
        ),
        in_specs=[vmem] * 2,
        out_specs=(vmem,) * 2,
        scratch_shapes=[pltpu.VMEM((16 * heads, 2 * rope), F32)],
        compiler_params=pltpu.CompilerParams(vmem_limit_bytes=32 * 1024 * 1024),
        cost_estimate=pl.CostEstimate(
            flops=2 * keys * rows * width, bytes_accessed=6 * rows * latent, transcendentals=0
        ),
        name="queries",
    )(dscore, keys_all)

    summed = mine.astype(F32) + over_resp(theirs, 1).astype(F32)
    held = summed.astype(BF16).reshape(n_seq, pairs * cols, shard)
    moved = {
        d: over_seq(
            jnp.concatenate(
                [held[d].reshape(-1, 2 * rope), span[d]], axis=0
            ),
            d,
        )
        for d in order
    }
    split = pairs * cols * shard // (2 * rope)
    block = summed[0].reshape(pairs, cols, shard)
    own = span[0].astype(F32)
    for d in order:
        block = block + moved[d][:split].reshape(pairs, cols, shard).astype(F32)
        own = own + moved[d][split:].astype(F32)
    block_half = block.astype(BF16)
    total = block[0]
    for d in range(pairs - 1, 0, -1):
        total = total + over_resp(block_half[d], 2 * d).astype(F32)
    column = lax.dynamic_slice_in_dim(
        channel_scale, lax.axis_index("resp") * cols, cols
    )
    grad_prompt = (total * column[:, None]).T

    parts = own.reshape(-1, piece, 2 * rope)
    grad_span = jnp.concatenate(
        [parts[i] for i in range(latent // (2 * rope))] + [parts[-1][:, :rope]], axis=1
    )
    return (
        grad_latent.reshape(tok, heads, latent),
        grad_rope,
        grad_prompt,
        grad_span,
    )


def solution(mesh):
    return jax.shard_map(
        functools.partial(on_device, mesh.shape["resp"], mesh.shape["seq"]),
        mesh=mesh,
        in_specs=(
            P("seq", None),
            P(),
            P("resp", None),
            P("resp", "seq", None),
            P("resp", "seq"),
            P("resp", "seq", None),
            P(),
            P(),
            P(),
        ),
        out_specs=(
            P("resp", "seq", None),
            P("resp", "seq"),
            P("seq", "resp"),
            P(("resp", "seq"), None),
        ),
        check_vma=False,
    )
```

time: 143 us -> 51.4 us (0.36)
  waiting for transfers between devices: 54 us -> 11.5 us
  matrix products: 32.9 us -> 0 us
  between operations: 19.7 us -> 0.75 us
  Pallas kernels: 0 us -> 15.1 us
  starting transfers between devices: 0.35 us -> 12.7 us
  blocking collectives: 11.8 us -> 0 us
  other arithmetic: 9.54 us -> 0.86 us
  local copies, waits for them, and re-layouts: 14.3 us -> 10.1 us
    unnamed x5 -> x0, waiting for transfers between devices: 37 us -> none
    dot_general x12 -> x0, matrix products: 32.9 us -> none  [the longest x1 7.08 us: on_device(): jnp.einsum('thc,kc->thk', upstream, latent_keys, preferred_element_type=j...]
    reduce_scatter x1 -> x0, waiting for transfers between devices: 17.1 us -> none  [on_device(): lax.psum_scatter(prompt_terms.astype(jnp.bfloat16), 'resp', scatter_dimen...]
    pallas_call x0 -> x2, Pallas kernels: none -> 15.1 us  [the longest x1 11 us: on_device(): pl.pallas_call(functools.partial(keys_kernel, n_resp, n_seq, heads), out_...]
    ppermute x0 -> x10, starting transfers between devices: none -> 12.7 us  [the longest x6 8.22 us: over_seq(): return lax.ppermute(x, 'seq', [(i, i ^ d) for i in range(n_seq)])]
    all_gather x1 -> x0, blocking collectives: 11.8 us -> none  [on_device(): prompt_keys = lax.all_gather(scaled_cache, 'seq', axis=0, tiled=True)]
    ppermute x0 -> x10, waiting for transfers between devices: none -> 11.5 us  [the longest x6 6.95 us: over_seq(): return lax.ppermute(x, 'seq', [(i, i ^ d) for i in range(n_seq)])]
    convert_element_type x3 -> x1, other arithmetic: 2.95 us -> 0.04 us  [on_device(): block_half = block.astype(BF16)]
  transfers between devices with their start and end apart: 3 -> 10, of which waited for: 3 -> 5; matrix products, arithmetic and copies ran while one was open for 16% -> 3% of each run, Pallas kernels for 0% -> 8%
where the time goes in v1:
time: 51.4 us; the launch traced here: 51 us
  Pallas kernels  15.1 us (29%)
  starting transfers between devices  12.7 us (25%)
  waiting for transfers between devices  11.5 us (22%)
  local copies, waits for them, and re-layouts  10.1 us (20%)
  other arithmetic  0.86 us (2%)
  between operations  0.75 us (1%)
    pallas_call x1, Pallas kernels, on_device(): pl.pallas_call(functools.partial(keys_kernel, n_resp, n_seq, heads), out_...  11 us
    unnamed x25, local copies, waits for them, and re-layouts  8.45 us
    ppermute x6, starting transfers between devices, over_seq(): return lax.ppermute(x, 'seq', [(i, i ^ d) for i in range(n_seq)])  8.22 us
    ppermute x6, waiting for transfers between devices, over_seq(): return lax.ppermute(x, 'seq', [(i, i ^ d) for i in range(n_seq)])  6.95 us
    ppermute x4, waiting for transfers between devices, over_resp(): return lax.ppermute(x, 'resp', [(i, i ^ d) for i in range(n_resp)])  4.53 us
    ppermute x4, starting transfers between devices, over_resp(): return lax.ppermute(x, 'resp', [(i, i ^ d) for i in range(n_resp)])  4.46 us
    pallas_call x1, Pallas kernels, on_device(): pl.pallas_call(functools.partial(query_kernel, heads), out_shape=(jax.Sha...  4.15 us
  transfers between devices with their start and end apart: 10, of which 5 were waited for; matrix products, arithmetic and copies ran while one was open for 3% of the time, Pallas kernels for 8%

profile of v1, /device:TPU:0, one launch (start us, length us, event | category | flops | bytes accessed | tf_op | source)
XLA Modules:
  0.0 51.0 jit_solution(6598270737385319575)
XLA Ops:
  0.6 1.1 %copy.16.refs_0_ = bf16[128,576]{1,0:T(8,128)(2,1)S(1)} copy(bf16[128,576]{0,1:T(8,128)(2,1)} %param.9) | data formatting | bytes 294912 | tf_op args[0]
  1.7 3.0 %collective-permute-start = (bf16[128,576]{1,0:T(8,128)(2,1)S(1)}, bf16[128,576]{1,0:T(8,128)(2,1)S(1)}, u32[]{:S(2)}, u32[]{:S(2)}) collective-permute-start(bf16[128,576]{1,0:T(8,128)(2,1)S(1)} %copy.16.refs_0_), channel_id=1, source_target_pairs={{0,1},{1,0},{2,3},{3,2},{4,5},{5,4},{6,7},{7,6},{8,9},{9,8},{10,11... | collective-permute-start | bytes 442376 | tf_op jit(solution)/shard_map/ppermute | solution.py:169
  4.7 1.5 %collective-permute-start.1 = (bf16[128,576]{1,0:T(8,128)(2,1)S(1)}, bf16[128,576]{1,0:T(8,128)(2,1)S(1)}, u32[]{:S(2)}, u32[]{:S(2)}) collective-permute-start(bf16[128,576]{1,0:T(8,128)(2,1)S(1)} %copy.16.refs_0_), channel_id=1, source_target_pairs={{0,2},{1,3},{2,0},{3,1},{4,6},{5,7},{6,4},{7,5},{8,10},{9,11},{10,... | collective-permute-start | bytes 442376 | tf_op jit(solution)/shard_map/ppermute | solution.py:169
  6.2 0.0 collective-permute-start.2
  6.2 0.7 %reshape.50.scale_ref = f32[1,576]{1,0:T(1,128)S(1)} reshape(f32[576]{0:T(1024)} %param.10) | data formatting | bytes 4608 | tf_op jit(solution)/shard_map/reshape | solution.py:207
  6.9 2.8 %collective-permute-done.refs_1_ = bf16[128,576]{1,0:T(8,128)(2,1)S(1)} collective-permute-done((bf16[128,576]{1,0:T(8,128)(2,1)S(1)}, bf16[128,576]{1,0:T(8,128)(2,1)S(1)}, u32[]{:S(2)}, u32[]{:S(2)}) %collective-permute-start) | collective-permute-done | bytes 147488 | tf_op jit(solution)/shard_map/ppermute | solution.py:169
  9.7 4.1 %collective-permute-done.1.refs_2_ = bf16[128,576]{1,0:T(8,128)(2,1)S(1)} collective-permute-done((bf16[128,576]{1,0:T(8,128)(2,1)S(1)}, bf16[128,576]{1,0:T(8,128)(2,1)S(1)}, u32[]{:S(2)}, u32[]{:S(2)}) %collective-permute-start.1) | collective-permute-done | bytes 147488 | tf_op jit(solution)/shard_map/ppermute | solution.py:169
  13.9 0.0 collective-permute-done.2.refs_3_
  13.9 1.6 %copy-done = bf16[64,32,512]{2,1,0:T(8,128)(2,1)S(1)} copy-done((bf16[64,32,512]{2,1,0:T(8,128)(2,1)S(1)}, bf16[64,32,512]{2,1,0:T(8,128)(2,1)}, u32[]{:S(2)}) %copy-start) | copy-done | bytes 2097176
  15.5 0.9 %copy-done.1 = bf16[64,2048]{1,0:T(8,128)(2,1)S(1)} copy-done((bf16[64,2048]{1,0:T(8,128)(2,1)S(1)}, bf16[64,2048]{1,0:T(8,128)(2,1)}, u32[]{:S(2)}) %copy-start.1) | copy-done | bytes 262168
  16.4 0.9 %copy-done.2 = bf16[64,576]{1,0:T(8,128)(2,1)S(1)} copy-done((bf16[64,576]{1,0:T(8,128)(2,1)S(1)}, bf16[64,576]{1,0:T(8,128)(2,1)}, u32[]{:S(2)}) %copy-start.2) | copy-done | bytes 73752
  17.3 0.7 %copy-done.3 = s32[16]{0:T(128)S(1)} copy-done((s32[16]{0:T(128)S(1)}, s32[16]{0:T(128)}, u32[]{:S(2)}) %copy-start.3) | copy-done | bytes 88
  18.0 0.7 %copy-done.4 = s32[8]{0:T(128)S(1)} copy-done((s32[8]{0:T(128)S(1)}, s32[8]{0:T(128)}, u32[]{:S(2)}) %copy-start.4) | copy-done | bytes 56
  18.6 0.7 %copy-done.5 = s32[8]{0:T(128)S(1)} copy-done((s32[8]{0:T(128)S(1)}, s32[8]{0:T(128)}, u32[]{:S(2)}) %copy-start.5) | copy-done | bytes 56
  19.3 11.0 %keys.1 = (bf16[4,4,72,128]{3,2,1,0:T(8,128)(2,1)S(1)}, bf16[4,4,72,128]{3,2,1,0:T(8,128)(2,1)S(1)}, bf16[4,80,128]{2,1,0:T(8,128)(2,1)S(1)}, bf16[576,2048]{1,0:T(8,128)(2,1)}, bf16[576,640]{1,0:T(8,128)(2,1)S(1)}) custom-call(s32[16]{0:T(128)S(1)} %copy-done.3, s32[8]{0:T(128)S(1)} %copy-done.4, s32[8]{0:T(128)S(1)} %copy-done.5, ...), custom_call_target="tpu_custom_call" | custom-call | flops 4831838208 | bytes 6291456 | tf_op jit(solution)/shard_map/keys/pallas_call | solution.py:182
  30.3 0.9 %copy-done.7 = bf16[576,640]{1,0:T(8,128)(2,1)} copy-done((bf16[576,640]{1,0:T(8,128)(2,1)}, bf16[576,640]{1,0:T(8,128)(2,1)S(1)}, u32[]{:S(2)}) %copy-start.7) | copy-done | bytes 737304
  31.1 0.9 %dynamic_slice.3 = f32[72]{0:T(128)S(1)} dynamic-slice(f32[576]{0:T(1024)} %param.10, s32[]{:T(128)S(6)} %select_n.3), dynamic_slice_sizes={72} | dynamic-slice | bytes 580 | tf_op jit(solution)/shard_map/dynamic_slice | solution.py:252
  32.0 0.7 %collective-permute-done.3 = bf16[4,4,72,128]{3,2,1,0:T(8,128)(2,1)S(1)} collective-permute-done((bf16[4,4,72,128]{3,2,1,0:T(8,128)(2,1)S(1)}, bf16[4,4,72,128]{3,2,1,0:T(8,128)(2,1)S(1)}, u32[]{:S(2)}, u32[]{:S(2)}) %collective-permute-start.3) | collective-permute-done | bytes 294944 | tf_op jit(solution)/shard_map/ppermute | solution.py:172
  32.7 0.1 convert_add_fusion
  32.8 1.5 %collective-permute-start.4 = (bf16[368,128]{1,0:T(8,128)(2,1)S(1)}, bf16[368,128]{1,0:T(8,128)(2,1)S(1)}, u32[]{:S(2)}, u32[]{:S(2)}) collective-permute-start(bf16[368,128]{1,0:T(8,128)(2,1)S(1)} %pad_maximum_fusion), channel_id=1, source_target_pairs={{0,3},{1,2},{2,1},{3,0},{4,7},{5,6},{6,5},{7,4},{8,11},{9,10},{10,... | collective-permute-start | bytes 282632 | tf_op jit(solution)/shard_map/ppermute | solution.py:169
  34.4 1.6 %collective-permute-start.5 = (bf16[368,128]{1,0:T(8,128)(2,1)S(1)}, bf16[368,128]{1,0:T(8,128)(2,1)S(1)}, u32[]{:S(2)}, u32[]{:S(2)}) collective-permute-start(bf16[368,128]{1,0:T(8,128)(2,1)S(1)} %pad_maximum_fusion.1), channel_id=1, source_target_pairs={{0,1},{1,0},{2,3},{3,2},{4,5},{5,4},{6,7},{7,6},{8,9},{9,8},{10,11... | collective-permute-start | bytes 282632 | tf_op jit(solution)/shard_map/ppermute | solution.py:169
  36.0 0.6 %collective-permute-start.6 = (bf16[368,128]{1,0:T(8,128)(2,1)S(1)}, bf16[368,128]{1,0:T(8,128)(2,1)S(1)}, u32[]{:S(2)}, u32[]{:S(2)}) collective-permute-start(bf16[368,128]{1,0:T(8,128)(2,1)S(1)} %pad_maximum_fusion.2), channel_id=1, source_target_pairs={{0,2},{1,3},{2,0},{3,1},{4,6},{5,7},{6,4},{7,5},{8,10},{9,11},{10,... | collective-permute-start | bytes 282632 | tf_op jit(solution)/shard_map/ppermute | solution.py:169
  36.5 1.1 %copy-done.8 = bf16[576,640]{1,0:T(8,128)(2,1)S(1)} copy-done((bf16[576,640]{1,0:T(8,128)(2,1)S(1)}, bf16[576,640]{1,0:T(8,128)(2,1)}, u32[]{:S(2)}) %copy-start.8) | copy-done | bytes 737304
  37.6 4.1 %queries.1 = (bf16[2048,512]{1,0:T(8,128)(2,1)}, bf16[64,2048]{1,0:T(8,128)(2,1)}) custom-call(bf16[576,2048]{1,0:T(8,128)(2,1)S(1)} %copy-done.6, bf16[576,640]{1,0:T(8,128)(2,1)S(1)} %copy-done.8), custom_call_target="tpu_custom_call" | custom-call | flops 1509949440 | bytes 6291456 | tf_op jit(solution)/shard_map/queries/pallas_call | solution.py:215
  41.8 0.0 collective-permute-done.4
  41.8 0.0 collective-permute-done.5
  41.8 0.0 collective-permute-done.6
  42.0 3.7 %collective-permute-start.7 = (bf16[72,128]{1,0:T(8,128)(2,1)S(1)}, bf16[72,128]{1,0:T(8,128)(2,1)S(1)}, u32[]{:S(2)}, u32[]{:S(2)}) collective-permute-start(bf16[72,128]{1,0:T(8,128)(2,1)S(1)} %get-tuple-element.28), channel_id=1, source_target_pairs={{0,24},{4,28},{8,16},{12,20},{16,8},{20,12},{24,0},{28,4},{1,25},{... | collective-permute-start | bytes 55304 | tf_op jit(solution)/shard_map/ppermute | solution.py:172
  45.6 0.8 %collective-permute-start.9 = (bf16[72,128]{1,0:T(8,128)(2,1)S(1)}, bf16[72,128]{1,0:T(8,128)(2,1)S(1)}, u32[]{:S(2)}, u32[]{:S(2)}) collective-permute-start(bf16[72,128]{1,0:T(8,128)(2,1)S(1)} %get-tuple-element.29), channel_id=1, source_target_pairs={{0,8},{4,12},{8,0},{12,4},{16,24},{20,28},{24,16},{28,20},{1,9},{5... | collective-permute-start | bytes 55304 | tf_op jit(solution)/shard_map/ppermute | solution.py:172
  46.4 1.2 %collective-permute-done.7 = bf16[72,128]{1,0:T(8,128)(2,1)S(1)} collective-permute-done((bf16[72,128]{1,0:T(8,128)(2,1)S(1)}, bf16[72,128]{1,0:T(8,128)(2,1)S(1)}, u32[]{:S(2)}, u32[]{:S(2)}) %collective-permute-start.7) | collective-permute-done | bytes 18464 | tf_op jit(solution)/shard_map/ppermute | solution.py:172
  47.6 2.7 %collective-permute-done.8 = bf16[72,128]{1,0:T(8,128)(2,1)S(1)} collective-permute-done((bf16[72,128]{1,0:T(8,128)(2,1)S(1)}, bf16[72,128]{1,0:T(8,128)(2,1)S(1)}, u32[]{:S(2)}, u32[]{:S(2)}) %collective-permute-start.8) | collective-permute-done | bytes 18464 | tf_op jit(solution)/shard_map/ppermute | solution.py:172
  50.3 0.7 %fusion.9 = f32[128,72]{0,1:T(8,128)} fusion(f32[4,72,128]{2,1,0:T(8,128)S(1)} %get-tuple-element.19, bf16[72,128]{1,0:T(8,128)(2,1)S(1)} %collective-permute-done.9, bf16[72,128]{1,0:T(8,128)(2,1)S(1)} %collective-permute-done.8, bf16[72,128]{1,0:T(8,128)(2,1)S(1)} %collective-permute-done.7, f32[72]{0:T(128)S(1)} %dynamic_slice.3), kind=kLoop, calls=%fused_computation.16 | loop fusion | flops 64512 | bytes 129312 | tf_op jit(solution)/shard_map/transpose | solution.py:255
  (31 shorter events, 0.2 us)
Async XLA Ops:
  1.7 8.0 %collective-permute-start = (bf16[128,576]{1,0:T(8,128)(2,1)S(1)}, bf16[128,576]{1,0:T(8,128)(2,1)S(1)}, u32[]{:S(2)}, u32[]{:S(2)}) collective-permute-start(bf16[128,576]{1,0:T(8,128)(2,1)S(1)} %copy.16.refs_0_), channel_id=1, source_target_pairs={{0,1},{1,0},{2,3},{3,2},{4,5},{5,4},{6,7},{7,6},{8,9},{9,8},{10,11... | collective-permute-start | bytes 442376 | tf_op jit(solution)/shard_map/ppermute | solution.py:169
  4.7 9.2 %collective-permute-start.1 = (bf16[128,576]{1,0:T(8,128)(2,1)S(1)}, bf16[128,576]{1,0:T(8,128)(2,1)S(1)}, u32[]{:S(2)}, u32[]{:S(2)}) collective-permute-start(bf16[128,576]{1,0:T(8,128)(2,1)S(1)} %copy.16.refs_0_), channel_id=1, source_target_pairs={{0,2},{1,3},{2,0},{3,1},{4,6},{5,7},{6,4},{7,5},{8,10},{9,11},{10,... | collective-permute-start | bytes 442376 | tf_op jit(solution)/shard_map/ppermute | solution.py:169
  6.2 7.7 %collective-permute-start.2 = (bf16[128,576]{1,0:T(8,128)(2,1)S(1)}, bf16[128,576]{1,0:T(8,128)(2,1)S(1)}, u32[]{:S(2)}, u32[]{:S(2)}) collective-permute-start(bf16[128,576]{1,0:T(8,128)(2,1)S(1)} %copy.16.refs_0_), channel_id=1, source_target_pairs={{0,3},{1,2},{2,1},{3,0},{4,7},{5,6},{6,5},{7,4},{8,11},{9,10},{10,... | collective-permute-start | bytes 442376 | tf_op jit(solution)/shard_map/ppermute | solution.py:169
  13.9 1.6 %copy-start = (bf16[64,32,512]{2,1,0:T(8,128)(2,1)S(1)}, bf16[64,32,512]{2,1,0:T(8,128)(2,1)}, u32[]{:S(2)}) copy-start(bf16[64,32,512]{2,1,0:T(8,128)(2,1)} %param.12) | copy-start | bytes 6291460
  15.5 0.9 %copy-start.1 = (bf16[64,2048]{1,0:T(8,128)(2,1)S(1)}, bf16[64,2048]{1,0:T(8,128)(2,1)}, u32[]{:S(2)}) copy-start(bf16[64,2048]{1,0:T(8,128)(2,1)} %qrope_ref.1) | copy-start | bytes 786436
  16.4 0.9 %copy-start.2 = (bf16[64,576]{1,0:T(8,128)(2,1)S(1)}, bf16[64,576]{1,0:T(8,128)(2,1)}, u32[]{:S(2)}) copy-start(bf16[64,576]{1,0:T(8,128)(2,1)} %span_ref.1) | copy-start | bytes 221188
  17.3 0.7 %copy-start.3 = (s32[16]{0:T(128)S(1)}, s32[16]{0:T(128)}, u32[]{:S(2)}) copy-start(s32[16]{0:T(128)} %resp_length.1) | copy-start | bytes 196
  18.0 0.7 %copy-start.4 = (s32[8]{0:T(128)S(1)}, s32[8]{0:T(128)}, u32[]{:S(2)}) copy-start(s32[8]{0:T(128)} %span_response.1) | copy-start | bytes 100
  18.6 0.7 %copy-start.5 = (s32[8]{0:T(128)S(1)}, s32[8]{0:T(128)}, u32[]{:S(2)}) copy-start(s32[8]{0:T(128)} %span_index.1) | copy-start | bytes 100
  30.3 0.9 %copy-start.7 = (bf16[576,640]{1,0:T(8,128)(2,1)}, bf16[576,640]{1,0:T(8,128)(2,1)S(1)}, u32[]{:S(2)}) copy-start(bf16[576,640]{1,0:T(8,128)(2,1)S(1)} %get-tuple-element.12.keys_ref) | copy-start | bytes 2211844
  31.1 5.4 %copy-start.6 = (bf16[576,2048]{1,0:T(8,128)(2,1)S(1)}, bf16[576,2048]{1,0:T(8,128)(2,1)}, u32[]{:S(2)}) copy-start(bf16[576,2048]{1,0:T(8,128)(2,1)} %get-tuple-element.11.ds_ref) | copy-start | bytes 7077892
  31.1 1.6 %collective-permute-start.3 = (bf16[4,4,72,128]{3,2,1,0:T(8,128)(2,1)S(1)}, bf16[4,4,72,128]{3,2,1,0:T(8,128)(2,1)S(1)}, u32[]{:S(2)}, u32[]{:S(2)}) collective-permute-start(bf16[4,4,72,128]{3,2,1,0:T(8,128)(2,1)S(1)} %get-tuple-element.16), channel_id=1, source_target_pairs={{0,4},{4,0},{8,12},{12,8},{16,20},{20,16},{24,28},{28,24},{1,5},{5... | collective-permute-start | bytes 884744 | tf_op jit(solution)/shard_map/ppermute | solution.py:172
  32.8 9.0 %collective-permute-start.4 = (bf16[368,128]{1,0:T(8,128)(2,1)S(1)}, bf16[368,128]{1,0:T(8,128)(2,1)S(1)}, u32[]{:S(2)}, u32[]{:S(2)}) collective-permute-start(bf16[368,128]{1,0:T(8,128)(2,1)S(1)} %pad_maximum_fusion), channel_id=1, source_target_pairs={{0,3},{1,2},{2,1},{3,0},{4,7},{5,6},{6,5},{7,4},{8,11},{9,10},{10,... | collective-permute-start | bytes 282632 | tf_op jit(solution)/shard_map/ppermute | solution.py:169
  34.4 7.4 %collective-permute-start.5 = (bf16[368,128]{1,0:T(8,128)(2,1)S(1)}, bf16[368,128]{1,0:T(8,128)(2,1)S(1)}, u32[]{:S(2)}, u32[]{:S(2)}) collective-permute-start(bf16[368,128]{1,0:T(8,128)(2,1)S(1)} %pad_maximum_fusion.1), channel_id=1, source_target_pairs={{0,1},{1,0},{2,3},{3,2},{4,5},{5,4},{6,7},{7,6},{8,9},{9,8},{10,11... | collective-permute-start | bytes 282632 | tf_op jit(solution)/shard_map/ppermute | solution.py:169
  36.0 5.8 %collective-permute-start.6 = (bf16[368,128]{1,0:T(8,128)(2,1)S(1)}, bf16[368,128]{1,0:T(8,128)(2,1)S(1)}, u32[]{:S(2)}, u32[]{:S(2)}) collective-permute-start(bf16[368,128]{1,0:T(8,128)(2,1)S(1)} %pad_maximum_fusion.2), channel_id=1, source_target_pairs={{0,2},{1,3},{2,0},{3,1},{4,6},{5,7},{6,4},{7,5},{8,10},{9,11},{10,... | collective-permute-start | bytes 282632 | tf_op jit(solution)/shard_map/ppermute | solution.py:169
  36.5 1.1 %copy-start.8 = (bf16[576,640]{1,0:T(8,128)(2,1)S(1)}, bf16[576,640]{1,0:T(8,128)(2,1)}, u32[]{:S(2)}) copy-start(bf16[576,640]{1,0:T(8,128)(2,1)} %copy-done.7) | copy-start | bytes 2211844
  42.0 5.7 %collective-permute-start.7 = (bf16[72,128]{1,0:T(8,128)(2,1)S(1)}, bf16[72,128]{1,0:T(8,128)(2,1)S(1)}, u32[]{:S(2)}, u32[]{:S(2)}) collective-permute-start(bf16[72,128]{1,0:T(8,128)(2,1)S(1)} %get-tuple-element.28), channel_id=1, source_target_pairs={{0,24},{4,28},{8,16},{12,20},{16,8},{20,12},{24,0},{28,4},{1,25},{... | collective-permute-start | bytes 55304 | tf_op jit(solution)/shard_map/ppermute | solution.py:172
  45.6 4.7 %collective-permute-start.8 = (bf16[72,128]{1,0:T(8,128)(2,1)S(1)}, bf16[72,128]{1,0:T(8,128)(2,1)S(1)}, u32[]{:S(2)}, u32[]{:S(2)}) collective-permute-start(bf16[72,128]{1,0:T(8,128)(2,1)S(1)} %get-tuple-element.30), channel_id=1, source_target_pairs={{0,16},{4,20},{8,24},{12,28},{16,0},{20,4},{24,8},{28,12},{1,17},{... | collective-permute-start | bytes 55304 | tf_op jit(solution)/shard_map/ppermute | solution.py:172
  45.6 4.7 %collective-permute-start.9 = (bf16[72,128]{1,0:T(8,128)(2,1)S(1)}, bf16[72,128]{1,0:T(8,128)(2,1)S(1)}, u32[]{:S(2)}, u32[]{:S(2)}) collective-permute-start(bf16[72,128]{1,0:T(8,128)(2,1)S(1)} %get-tuple-element.29), channel_id=1, source_target_pairs={{0,8},{4,12},{8,0},{12,4},{16,24},{20,28},{24,16},{28,20},{1,9},{5... | collective-permute-start | bytes 55304 | tf_op jit(solution)/shard_map/ppermute | solution.py:172
  46.4 4.6 %copy-start.9 = (f32[16,576]{1,0:T(8,128)}, f32[16,576]{1,0:T(8,128)S(1)}, u32[]{:S(2)}) copy-start(f32[16,576]{1,0:T(8,128)S(1)} %constant_dynamic-update-slice_fusion) | copy-start | bytes 110596

commit v2 on v1

v2 whole, which is shorter than its diff:
```python
import functools
import math

import jax
import jax.numpy as jnp
from jax import lax
from jax.experimental import pallas as pl
from jax.experimental.pallas import tpu as pltpu
from jax.sharding import PartitionSpec as P

SIGMA = 1.0 / math.sqrt(192.0)
EXP_SCALE = SIGMA * math.log2(math.e)
F32 = jnp.float32
BF16 = jnp.bfloat16
NT = (((1,), (1,)), ((), ()))
NN = (((1,), (0,)), ((), ()))
TN = (((0,), (0,)), ((), ()))
MIB = 1024 * 1024
STEP = 256


def dot(a, b, dims):
    return lax.dot_general(a, b, dims, preferred_element_type=F32)


def low_half(shape, half):
    return lax.broadcasted_iota(jnp.int32, shape, len(shape) - 1) < half


def put_keys(keys_ref, start, latent, values):
    rows, full = values.shape
    keys_ref[pl.ds(start, rows), :full] = values
    keys_ref[pl.ds(start, rows), full:] = values[:, latent:]


def scaled_rows(shard, scale):
    return (shard.astype(F32).T * scale).astype(BF16)


def mask_kernel(heads, mask_ref):
    key_pos = lax.broadcasted_iota(jnp.int32, mask_ref.shape, 0)
    row = lax.broadcasted_iota(jnp.int32, mask_ref.shape, 1)
    mask_ref[...] = jnp.where(key_pos * heads <= row, 1.0, 0.0)


def early_kernel(
    heads,
    length_s,
    response_s,
    index_s,
    mask_ref,
    scale_ref,
    prompt_ref,
    span_ref,
    q_ref,
    qrope_v,
    up_ref,
    qr_ref,
    expo_ref,
    dprob_ref,
    stat_ref,
    keys_ref,
    rope_scr,
):
    full, shard = prompt_ref.shape
    tok = span_ref.shape[0]
    rows, latent = q_ref.shape
    rope = full - latent
    my_resp = lax.axis_index("resp")
    live = jnp.clip(
        length_s[response_s[my_resp]] - index_s[my_resp] * tok, 0, tok
    )
    low = low_half((tok, 2 * rope), rope)
    for j in range(heads // 2):
        x = qrope_v[:, pl.ds(2 * rope * j, 2 * rope)].astype(F32)
        rope_scr[pl.ds(2 * j, tok, stride=heads), :] = jnp.where(low, x, 0.0)
        rope_scr[pl.ds(2 * j + 1, tok, stride=heads), :] = jnp.where(low, 0.0, x)
    qr_ref[...] = rope_scr[...].astype(BF16)

    put_keys(keys_ref, 0, latent, scaled_rows(prompt_ref[...], scale_ref[...]))
    put_keys(keys_ref, shard, latent, span_ref[...])

    for i in range(rows // STEP):
        at = pl.ds(i * STEP, STEP)
        logits = dot(keys_ref[:, :latent], q_ref[at, :], NT) + dot(
            keys_ref[:, latent:], qr_ref[at, :], NT
        )
        dprob = dot(keys_ref[:, :latent], up_ref[at, :], NT)
        key_pos = lax.broadcasted_iota(jnp.int32, (tok, STEP), 0)
        seen = (mask_ref[:, at] > 0.5) & (key_pos < live)
        own = jnp.where(seen, logits[shard:], -jnp.inf)
        logits = jnp.concatenate([logits[:shard], own], axis=0)
        top = jnp.max(logits, axis=0, keepdims=True)
        expo = jnp.exp2((logits - top) * EXP_SCALE)
        row_pos = (lax.broadcasted_iota(jnp.int32, (1, STEP), 1) + i * STEP) // heads
        expo_ref[:, at] = expo
        dprob_ref[:, at] = dprob
        stat_ref[0:1, at] = top
        stat_ref[1:2, at] = jnp.sum(expo, axis=0, keepdims=True)
        stat_ref[2:3, at] = jnp.sum(expo * dprob, axis=0, keepdims=True)
        stat_ref[3:4, at] = jnp.where(row_pos < live, SIGMA, 0.0)


def keys_kernel(
    n_resp,
    n_seq,
    scale_ref,
    q_ref,
    up_ref,
    qr_ref,
    expo_ref,
    dprob_ref,
    stat_ref,
    early_ref,
    *refs,
):
    shard_refs = refs[: n_seq - 1]
    mine_ref, theirs_ref, span_out, ds_ref, keys_ref, t_scr = refs[n_seq - 1 :]
    rows, latent = q_ref.shape
    full, shard = shard_refs[0].shape
    rope = full - latent
    prompt = shard * n_seq
    tok = early_ref.shape[0] - shard
    my_resp = lax.axis_index("resp")
    my_seq = lax.axis_index("seq")
    odd = (my_resp % 2) == 1

    scale = scale_ref[...]
    keys_ref[:shard] = early_ref[:shard]
    keys_ref[prompt:] = early_ref[shard:]
    for d in range(1, n_seq):
        value = shard_refs[d - 1][...]
        if d < n_seq - 1:
            other = shard_refs[(d - 1) ^ 1][...]
            value = jnp.where(odd, other, value)
        put_keys(keys_ref, d * shard, latent, scaled_rows(value, scale))

    late = slice(shard, prompt)
    for i in range(rows // STEP):
        at = pl.ds(i * STEP, STEP)
        logits = dot(keys_ref[late, :latent], q_ref[at, :], NT) + dot(
            keys_ref[late, latent:], qr_ref[at, :], NT
        )
        dprob = dot(keys_ref[late, :latent], up_ref[at, :], NT)
        early_top = stat_ref[0:1, at]
        top = jnp.maximum(early_top, jnp.max(logits, axis=0, keepdims=True))
        expo = jnp.exp2((logits - top) * EXP_SCALE)
        again = jnp.exp2((early_top - top) * EXP_SCALE)
        total = stat_ref[1:2, at] * again + jnp.sum(expo, axis=0, keepdims=True)
        weighed = stat_ref[2:3, at] * again + jnp.sum(expo * dprob, axis=0, keepdims=True)
        inverse = 1.0 / total
        delta = weighed * inverse
        factor = inverse * stat_ref[3:4, at]
        probs = expo * factor
        t_scr[late, at] = probs.astype(BF16)
        ds_ref[late, at] = (probs * (dprob - delta)).astype(BF16)
        probs = expo_ref[:, at] * (factor * again)
        dscore = probs * (dprob_ref[:, at] - delta)
        t_scr[:shard, at] = probs[:shard].astype(BF16)
        ds_ref[:shard, at] = dscore[:shard].astype(BF16)
        t_scr[prompt:, at] = probs[shard:].astype(BF16)
        ds_ref[prompt:, at] = dscore[shard:].astype(BF16)

    grad_latent = dot(ds_ref[...], q_ref[...], NN) + dot(t_scr[...], up_ref[...], NN) * (
        1.0 / SIGMA
    )
    grad_rope = dot(ds_ref[...], qr_ref[...], NN)

    piece = tok // n_seq
    own_rope = grad_rope[prompt:]
    own_rope = own_rope + pltpu.roll(own_rope, rope, 1)
    for s in range(n_seq):
        parts = [
            grad_latent[prompt + s * piece : prompt + (s + 1) * piece, c : c + 2 * rope]
            for c in range(0, latent, 2 * rope)
        ]
        parts.append(own_rope[s * piece : (s + 1) * piece])
        span_out[s ^ my_seq] = jnp.concatenate(parts, axis=0).astype(BF16)

    cols = full // n_resp
    my_pair = my_resp // 2
    scale_twice = jnp.concatenate([scale[:, latent:]] * 2, axis=1)
    for d in range(n_seq):
        at = slice(d * shard, (d + 1) * shard)
        lat = (grad_latent[at] * scale[:, :latent]).T
        rot = (grad_rope[at] * scale_twice).T
        whole = jnp.concatenate([lat, rot[:rope] + rot[rope:]], axis=0)
        for z in range(n_resp // 2):
            even_part = whole[2 * z * cols : (2 * z + 1) * cols]
            odd_part = whole[(2 * z + 1) * cols : (2 * z + 2) * cols]
            mine_ref[d, z ^ my_pair] = jnp.where(odd, odd_part, even_part).astype(BF16)
            theirs_ref[d, z ^ my_pair] = jnp.where(odd, even_part, odd_part).astype(BF16)


def query_kernel(heads, first, count, ds_ref, keys_ref, *refs):
    out_hbm, rope_hbm, out_v, rope_v, rope_scr, out_sems, rope_sems = refs[-7:]
    latent = out_v.shape[1]
    rope = (keys_ref.shape[1] - latent) // 2
    step = 16 * heads
    low = low_half((16, 2 * rope), rope)
    copies = []
    for i in range(count):
        at = pl.ds((first + i) * step, step)
        here = pl.ds(i * step, step)
        out_v[here, :] = dot(ds_ref[:, at], keys_ref[:, :latent], TN).astype(BF16)
        copies.append(pltpu.make_async_copy(out_v.at[here], out_hbm.at[at], out_sems.at[i]))
        copies[-1].start()
        rope_scr[...] = dot(ds_ref[:, at], keys_ref[:, latent:], TN)
        for j in range(heads // 2):
            even = rope_scr[pl.ds(2 * j, 16, stride=heads), :]
            odd = rope_scr[pl.ds(2 * j + 1, 16, stride=heads), :]
            rope_v[pl.ds(i * 16, 16), pl.ds(2 * rope * j, 2 * rope)] = jnp.where(
                low, even, odd
            ).astype(BF16)
        copies.append(
            pltpu.make_async_copy(
                rope_v.at[pl.ds(i * 16, 16)],
                rope_hbm.at[pl.ds((first + i) * 16, 16)],
                rope_sems.at[i],
            )
        )
        copies[-1].start()
    for copy in copies:
        copy.wait()


def on_device(
    n_resp,
    n_seq,
    prompt_cache,
    channel_scale,
    span_cache,
    q_latent,
    q_rope,
    d_out,
    resp_length,
    span_response,
    span_index,
):
    tok, heads, latent = q_latent.shape
    shard, full = prompt_cache.shape
    rope = full - latent
    rows = tok * heads
    prompt = shard * n_seq
    keys = prompt + tok
    early = shard + tok
    width = latent + 2 * rope
    cols = full // n_resp
    pairs = n_resp // 2
    piece = tok // n_seq
    span_rows = piece * (latent // (2 * rope) + 1)
    vmem = pl.BlockSpec(memory_space=pltpu.VMEM)
    hbm = pl.BlockSpec(memory_space=pl.ANY)

    def shape(dims, dtype=BF16):
        return jax.ShapeDtypeStruct(dims, dtype)

    def over_seq(x, d):
        return lax.ppermute(x, "seq", [(i, i ^ d) for i in range(n_seq)])

    def over_resp(x, d):
        return lax.ppermute(x, "resp", [(i, i ^ d) for i in range(n_resp)])

    def by_core(x, d):
        moves = [
            (r * n_seq + s, r * n_seq + (s ^ (d + r % 2)))
            for r in range(n_resp)
            for s in range(n_seq)
        ]
        return lax.ppermute(x, ("resp", "seq"), moves)

    prompt_t = prompt_cache.T
    fetched = [by_core(prompt_t, d) for d in range(1, n_seq - 1, 2)]
    last = over_seq(prompt_t, n_seq - 1)

    scale_row = channel_scale.reshape(1, full)
    smem = pl.BlockSpec(memory_space=pltpu.SMEM)
    q_rows = q_latent.reshape(rows, latent)
    up_rows = d_out.reshape(rows, latent)
    mask = pl.pallas_call(
        functools.partial(mask_kernel, heads),
        out_shape=shape((tok, rows), F32),
        out_specs=vmem,
        compiler_params=pltpu.CompilerParams(vmem_limit_bytes=4 * MIB),
        cost_estimate=pl.CostEstimate(
            flops=40 * keys * rows * width, bytes_accessed=4 * tok * rows, transcendentals=0
        ),
        name="mask",
    )()
    q_turned, expo, dprob, stats, early_keys = pl.pallas_call(
        functools.partial(early_kernel, heads),
        out_shape=(
            shape((rows, 2 * rope)),
            shape((early, rows), F32),
            shape((early, rows), F32),
            shape((8, rows), F32),
            shape((early, width)),
        ),
        in_specs=[smem] * 3 + [vmem] * 7,
        out_specs=(vmem,) * 5,
        scratch_shapes=[pltpu.VMEM((rows, 2 * rope), F32)],
        compiler_params=pltpu.CompilerParams(vmem_limit_bytes=24 * MIB),
        cost_estimate=pl.CostEstimate(
            flops=2 * early * rows * 2 * latent, bytes_accessed=4 * rows * latent, transcendentals=0
        ),
        name="early",
    )(
        resp_length,
        span_response,
        span_index,
        mask,
        scale_row,
        prompt_t,
        span_cache,
        q_rows,
        q_rope,
        up_rows,
    )

    fetched, stats = lax.optimization_barrier((fetched, stats))
    shards = []
    for value in fetched:
        shards += [value, over_resp(value, 1)]
    shards.append(last)
    mine, theirs, span, dscore, keys_all = pl.pallas_call(
        functools.partial(keys_kernel, n_resp, n_seq),
        out_shape=(
            shape((n_seq, pairs, cols, shard)),
            shape((n_seq, pairs, cols, shard)),
            shape((n_seq, span_rows, 2 * rope)),
            shape((keys, rows)),
            shape((keys, width)),
        ),
        in_specs=[vmem] * (7 + n_seq),
        out_specs=(vmem,) * 5,
        scratch_shapes=[pltpu.VMEM((keys, rows), BF16)],
        compiler_params=pltpu.CompilerParams(vmem_limit_bytes=24 * MIB),
        cost_estimate=pl.CostEstimate(
            flops=2 * keys * rows * 3 * latent, bytes_accessed=4 * rows * latent, transcendentals=0
        ),
        name="keys",
    )(scale_row, q_rows, up_rows, q_turned, expo, dprob, stats, early_keys, *shards)

    steps = tok // 16

    def queries(first, count, dscore, keys_all, before):
        return pl.pallas_call(
            functools.partial(query_kernel, heads, first, count),
            out_shape=(shape((rows, latent)), shape((tok, heads * rope))),
            in_specs=[vmem] * 2 + [hbm] * len(before),
            out_specs=(hbm,) * 2,
            scratch_shapes=[
                pltpu.VMEM((count * 16 * heads, latent), BF16),
                pltpu.VMEM((count * 16, heads * rope), BF16),
                pltpu.VMEM((16 * heads, 2 * rope), F32),
                pltpu.SemaphoreType.DMA((count,)),
                pltpu.SemaphoreType.DMA((count,)),
            ],
            input_output_aliases={2: 0, 3: 1} if before else {},
            compiler_params=pltpu.CompilerParams(vmem_limit_bytes=16 * MIB),
            cost_estimate=pl.CostEstimate(
                flops=2 * keys * count * 16 * heads * width,
                bytes_accessed=count * 32 * heads * latent,
                transcendentals=0,
            ),
            name="queries",
        )(dscore, keys_all, *before)

    summed = mine.astype(F32) + over_resp(theirs, 1).astype(F32)
    held = summed.astype(BF16).reshape(n_seq, pairs * cols, shard)
    moved = {
        d: over_seq(jnp.concatenate([held[d].reshape(-1, 2 * rope), span[d]], axis=0), d)
        for d in range(n_seq - 1, 0, -1)
    }
    half = (steps + 1) // 2
    partly = queries(0, half, dscore, keys_all, ())
    split = pairs * cols * shard // (2 * rope)
    block = summed[0].reshape(pairs, cols, shard)
    own = span[0].astype(F32)
    for d in moved:
        block = block + moved[d][:split].reshape(pairs, cols, shard).astype(F32)
        own = own + moved[d][split:].astype(F32)
    block_half = block.astype(BF16)
    block_half, dscore, keys_all = lax.optimization_barrier((block_half, dscore, keys_all))
    arrived = [over_resp(block_half[d], 2 * d) for d in range(pairs - 1, 0, -1)]
    grad_latent, grad_rope = queries(half, steps - half, dscore, keys_all, partly)
    total = block[0]
    for x in arrived:
        total = total + x.astype(F32)
    grad_prompt = total.T

    parts = own.reshape(-1, piece, 2 * rope)
    grad_span = jnp.concatenate(
        [parts[i] for i in range(latent // (2 * rope))] + [parts[-1][:, :rope]], axis=1
    )
    return (
        grad_latent.reshape(tok, heads, latent),
        grad_rope,
        grad_prompt,
        grad_span,
    )


def solution(mesh):
    return jax.shard_map(
        functools.partial(on_device, mesh.shape["resp"], mesh.shape["seq"]),
        mesh=mesh,
        in_specs=(
            P("seq", None),
            P(),
            P("resp", None),
            P("resp", "seq", None),
            P("resp", "seq"),
            P("resp", "seq", None),
            P(),
            P(),
            P(),
        ),
        out_specs=(
            P("resp", "seq", None),
            P("resp", "seq"),
            P("seq", "resp"),
            P(("resp", "seq"), None),
        ),
        check_vma=False,
    )
```

time: 51.4 us -> 37.8 us (0.74)
  local copies, waits for them, and re-layouts: 10.1 us -> 0.11 us
  waiting for transfers between devices: 11.5 us -> 8.9 us
  Pallas kernels: 15.1 us -> 14 us
    unnamed x25 -> x24, local copies, waits for them, and re-layouts: 8.45 us -> 0.06 us
    ppermute x6 -> x4, waiting for transfers between devices: 6.95 us -> 2.18 us  [over_seq(): return lax.ppermute(x, 'seq', [(i, i ^ d) for i in range(n_seq)])]
    ppermute x0 -> x1, waiting for transfers between devices: none -> 2.37 us  [by_core(): return lax.ppermute(x, ('resp', 'seq'), moves)]
    pallas_call x2 -> x5, Pallas kernels: 15.1 us -> 14 us  [the longest x1 6.53 us: on_device(): pl.pallas_call(functools.partial(keys_kernel, n_resp, n_seq), out_shape=(...]
    dynamic_slice x1 -> x0, local copies, waits for them, and re-layouts: 0.91 us -> none  [on_device(): lax.dynamic_slice_in_dim(channel_scale, lax.axis_index('resp') * cols, cols)]
    reshape x1, local copies, waits for them, and re-layouts: 0.69 us -> 0.01 us  [on_device(): scale_row = channel_scale.reshape(1, full)]
    ppermute x6 -> x4, starting transfers between devices: 8.22 us -> 7.63 us  [over_seq(): return lax.ppermute(x, 'seq', [(i, i ^ d) for i in range(n_seq)])]
    ppermute x0 -> x1, starting transfers between devices: none -> 0.54 us  [by_core(): return lax.ppermute(x, ('resp', 'seq'), moves)]
  transfers between devices with their start and end apart: 10 -> 10, of which waited for: 5 -> 7; matrix products, arithmetic and copies ran while one was open for 3% -> 0% of each run, Pallas kernels for 8% -> 20%
where the time goes in v2:
time: 37.8 us; the launch traced here: 37.6 us
  Pallas kernels  14 us (37%)
  starting transfers between devices  12.8 us (34%)
  waiting for transfers between devices  8.9 us (24%)
  between operations  0.94 us (2%)
  other arithmetic  0.79 us (2%)
    ppermute x4, starting transfers between devices, over_seq(): return lax.ppermute(x, 'seq', [(i, i ^ d) for i in range(n_seq)])  7.63 us
    pallas_call x1, Pallas kernels, on_device(): pl.pallas_call(functools.partial(keys_kernel, n_resp, n_seq), out_shape=(...  6.53 us
    ppermute x5, starting transfers between devices, over_resp(): return lax.ppermute(x, 'resp', [(i, i ^ d) for i in range(n_resp)])  4.67 us
    pallas_call x2, Pallas kernels, queries(): pl.pallas_call(functools.partial(query_kernel, heads, first, count), out_...  4.57 us
    ppermute x5, waiting for transfers between devices, over_resp(): return lax.ppermute(x, 'resp', [(i, i ^ d) for i in range(n_resp)])  4.36 us
    pallas_call x1, Pallas kernels, on_device(): pl.pallas_call(functools.partial(early_kernel, heads), out_shape=(shape((...  2.87 us
    ppermute x1, waiting for transfers between devices, by_core(): return lax.ppermute(x, ('resp', 'seq'), moves)  2.37 us
    ppermute x4, waiting for transfers between devices, over_seq(): return lax.ppermute(x, 'seq', [(i, i ^ d) for i in range(n_seq)])  2.18 us
  transfers between devices with their start and end apart: 10, of which 7 were waited for; matrix products, arithmetic and copies ran while one was open for 0% of the time, Pallas kernels for 20%

profile of v2, /device:TPU:0, one launch (start us, length us, event | category | flops | bytes accessed | tf_op | source)
XLA Modules:
  0.0 37.6 jit_solution(951572946446559445)
XLA Ops:
  0.7 4.0 %collective-permute-start.2 = (bf16[576,128]{1,0:T(8,128)(2,1)}, bf16[576,128]{1,0:T(8,128)(2,1)S(1)}, u32[]{:S(2)}, u32[]{:S(2)}) collective-permute-start(bf16[576,128]{1,0:T(8,128)(2,1)} %bitcast.53), channel_id=1, source_target_pairs={{0,3},{1,2},{2,1},{3,0},{4,7},{5,6},{6,5},{7,4},{8,11},{9,10},{10,... | collective-permute-start | bytes 442376 | tf_op jit(solution)/shard_map/ppermute | solution.py:259
  4.7 0.5 %collective-permute-start = (bf16[576,128]{1,0:T(8,128)(2,1)}, bf16[576,128]{1,0:T(8,128)(2,1)S(1)}, u32[]{:S(2)}, u32[]{:S(2)}) collective-permute-start(bf16[576,128]{1,0:T(8,128)(2,1)} %bitcast.54), channel_id=1, source_target_pairs={{0,1},{1,0},{2,3},{3,2},{4,6},{5,7},{6,4},{7,5},{8,9},{9,8},{10,11... | collective-permute-start | bytes 442376 | tf_op jit(solution)/shard_map/ppermute | solution.py:270
  5.3 0.0 copy-done
  5.3 0.0 copy-done.1
  5.3 0.0 copy-done.2
  5.3 0.0 copy-done.3
  5.3 0.0 copy-done.4
  5.4 2.9 %early.1 = (bf16[2048,128]{1,0:T(8,128)(2,1)S(1)}, f32[192,2048]{1,0:T(8,128)S(1)}, f32[192,2048]{1,0:T(8,128)S(1)}, f32[8,2048]{1,0:T(8,128)S(1)}, bf16[192,640]{1,0:T(8,128)(2,1)S(1)}) custom-call(s32[16]{0:T(128)S(1)} %copy-done.5, s32[8]{0:T(128)S(1)} %copy-done.6, s32[8]{0:T(128)S(1)} %copy-done.7, f32[64,2048]{1,0:T(8,128)S(1)} %mask.1.mask_ref, ...), custom_call_target="tpu_custom_call" | custom-call | flops 805306368 | bytes 4194304 | tf_op jit(solution)/shard_map/early/pallas_call | solution.py:290
  8.2 2.4 %collective-permute-done.refs_0_ = bf16[576,128]{1,0:T(8,128)(2,1)S(1)} collective-permute-done((bf16[576,128]{1,0:T(8,128)(2,1)}, bf16[576,128]{1,0:T(8,128)(2,1)S(1)}, u32[]{:S(2)}, u32[]{:S(2)}) %collective-permute-start) | collective-permute-done | bytes 147488 | tf_op jit(solution)/shard_map/ppermute | solution.py:270
  10.6 0.0 collective-permute-start.1
  10.6 0.0 collective-permute-done.2.refs_2_
  10.6 1.4 %collective-permute-done.1.refs_1_ = bf16[576,128]{1,0:T(8,128)(2,1)S(1)} collective-permute-done((bf16[576,128]{1,0:T(8,128)(2,1)S(1)}, bf16[576,128]{1,0:T(8,128)(2,1)S(1)}, u32[]{:S(2)}, u32[]{:S(2)}) %collective-permute-start.1) | collective-permute-done | bytes 147488 | tf_op jit(solution)/shard_map/ppermute | solution.py:262
  12.0 6.5 %keys.1 = (bf16[4,4,72,128]{3,2,1,0:T(8,128)(2,1)S(1)}, bf16[4,4,72,128]{3,2,1,0:T(8,128)(2,1)S(1)}, bf16[4,80,128]{2,1,0:T(8,128)(2,1)S(1)}, bf16[576,2048]{1,0:T(8,128)(2,1)S(1)}, bf16[576,640]{1,0:T(8,128)(2,1)S(1)}) custom-call(f32[1,576]{1,0:T(1,128)S(1)} %reshape.49.scale_ref, bf16[2048,512]{1,0:T(8,128)(2,1)S(1)} %bitcast.50, ...), custom_call_target="tpu_custom_call" | custom-call | flops 3623878656 | bytes 4194304 | tf_op jit(solution)/shard_map/keys/pallas_call | solution.py:325
  18.5 0.2 collective-permute-start.3
  18.7 1.4 %collective-permute-done.3 = bf16[4,4,72,128]{3,2,1,0:T(8,128)(2,1)S(1)} collective-permute-done((bf16[4,4,72,128]{3,2,1,0:T(8,128)(2,1)S(1)}, bf16[4,4,72,128]{3,2,1,0:T(8,128)(2,1)S(1)}, u32[]{:S(2)}, u32[]{:S(2)}) %collective-permute-start.3) | collective-permute-done | bytes 294944 | tf_op jit(solution)/shard_map/ppermute | solution.py:262
  20.2 0.1 convert_add_fusion
  20.3 1.0 %collective-permute-start.5 = (bf16[368,128]{1,0:T(8,128)(2,1)S(1)}, bf16[368,128]{1,0:T(8,128)(2,1)S(1)}, u32[]{:S(2)}, u32[]{:S(2)}) collective-permute-start(bf16[368,128]{1,0:T(8,128)(2,1)S(1)} %pad_maximum_fusion.1), channel_id=1, source_target_pairs={{0,2},{1,3},{2,0},{3,1},{4,6},{5,7},{6,4},{7,5},{8,10},{9,11},{10,... | collective-permute-start | bytes 282632 | tf_op jit(solution)/shard_map/ppermute | solution.py:259
  21.3 1.2 %collective-permute-start.6 = (bf16[368,128]{1,0:T(8,128)(2,1)S(1)}, bf16[368,128]{1,0:T(8,128)(2,1)S(1)}, u32[]{:S(2)}, u32[]{:S(2)}) collective-permute-start(bf16[368,128]{1,0:T(8,128)(2,1)S(1)} %pad_maximum_fusion.2), channel_id=1, source_target_pairs={{0,1},{1,0},{2,3},{3,2},{4,5},{5,4},{6,7},{7,6},{8,9},{9,8},{10,11... | collective-permute-start | bytes 282632 | tf_op jit(solution)/shard_map/ppermute | solution.py:259
  22.4 1.6 %collective-permute-start.4 = (bf16[368,128]{1,0:T(8,128)(2,1)S(1)}, bf16[368,128]{1,0:T(8,128)(2,1)S(1)}, u32[]{:S(2)}, u32[]{:S(2)}) collective-permute-start(bf16[368,128]{1,0:T(8,128)(2,1)S(1)} %pad_maximum_fusion), channel_id=1, source_target_pairs={{0,3},{1,2},{2,1},{3,0},{4,7},{5,6},{6,5},{7,4},{8,11},{9,10},{10,... | collective-permute-start | bytes 282632 | tf_op jit(solution)/shard_map/ppermute | solution.py:259
  24.0 2.3 %queries.2 = (bf16[2048,512]{1,0:T(8,128)(2,1)}, bf16[64,2048]{1,0:T(8,128)(2,1)}) custom-call(bf16[576,2048]{1,0:T(8,128)(2,1)S(1)} %get-tuple-element.35.ds_ref, bf16[576,640]{1,0:T(8,128)(2,1)S(1)} %get-tuple-element.36.keys_ref), custom_call_target="tpu_custom_call" | custom-call | flops 754974720 | bytes 1048576 | tf_op jit(solution)/shard_map/queries/pallas_call | solution.py:347
  26.3 0.0 collective-permute-done.5
  26.3 0.1 collective-permute-done.6
  26.4 2.1 %collective-permute-done.4 = bf16[368,128]{1,0:T(8,128)(2,1)S(1)} collective-permute-done((bf16[368,128]{1,0:T(8,128)(2,1)S(1)}, bf16[368,128]{1,0:T(8,128)(2,1)S(1)}, u32[]{:S(2)}, u32[]{:S(2)}) %collective-permute-start.4) | collective-permute-done | bytes 94240 | tf_op jit(solution)/shard_map/ppermute | solution.py:259
  28.6 0.0 copy-start.9
  28.6 3.7 %collective-permute-start.7 = (bf16[72,128]{1,0:T(8,128)(2,1)S(1)}, bf16[72,128]{1,0:T(8,128)(2,1)S(1)}, u32[]{:S(2)}, u32[]{:S(2)}) collective-permute-start(bf16[72,128]{1,0:T(8,128)(2,1)S(1)} %get-tuple-element.52), channel_id=1, source_target_pairs={{0,24},{4,28},{8,16},{12,20},{16,8},{20,12},{24,0},{28,4},{1,25},{... | collective-permute-start | bytes 55304 | tf_op jit(solution)/shard_map/ppermute | solution.py:262
  32.3 0.0 collective-permute-start.9
  32.3 0.8 %collective-permute-start.8 = (bf16[72,128]{1,0:T(8,128)(2,1)S(1)}, bf16[72,128]{1,0:T(8,128)(2,1)S(1)}, u32[]{:S(2)}, u32[]{:S(2)}) collective-permute-start(bf16[72,128]{1,0:T(8,128)(2,1)S(1)} %get-tuple-element.54), channel_id=1, source_target_pairs={{0,16},{4,20},{8,24},{12,28},{16,0},{20,4},{24,8},{28,12},{1,17},{... | collective-permute-start | bytes 55304 | tf_op jit(solution)/shard_map/ppermute | solution.py:262
  33.1 2.3 %queries.3 = (bf16[2048,512]{1,0:T(8,128)(2,1)}, bf16[64,2048]{1,0:T(8,128)(2,1)}) custom-call(bf16[576,2048]{1,0:T(8,128)(2,1)S(1)} %get-tuple-element.35.ds_ref, bf16[576,640]{1,0:T(8,128)(2,1)S(1)} %get-tuple-element.36.keys_ref, bf16[2048,512]{1,0:T(8,128)(2,1)} %get-tuple-element.37.refs_0_, ...), custom_call_target="tpu_custom_call", output_to_operand_aliasing={{0}: (2, {}), {1}: (3, {})} | custom-call | flops 754974720 | bytes 1048576 | tf_op jit(solution)/shard_map/queries/pallas_call | solution.py:347
  35.4 0.0 collective-permute-done.7
  35.4 0.7 %collective-permute-done.9 = bf16[72,128]{1,0:T(8,128)(2,1)S(1)} collective-permute-done((bf16[72,128]{1,0:T(8,128)(2,1)S(1)}, bf16[72,128]{1,0:T(8,128)(2,1)S(1)}, u32[]{:S(2)}, u32[]{:S(2)}) %collective-permute-start.9) | collective-permute-done | bytes 18464 | tf_op jit(solution)/shard_map/ppermute | solution.py:262
  36.1 0.9 %collective-permute-done.8 = bf16[72,128]{1,0:T(8,128)(2,1)S(1)} collective-permute-done((bf16[72,128]{1,0:T(8,128)(2,1)S(1)}, bf16[72,128]{1,0:T(8,128)(2,1)S(1)}, u32[]{:S(2)}, u32[]{:S(2)}) %collective-permute-start.8) | collective-permute-done | bytes 18464 | tf_op jit(solution)/shard_map/ppermute | solution.py:262
  37.0 0.6 %fusion.8 = f32[128,72]{0,1:T(8,128)} fusion(f32[4,72,128]{2,1,0:T(8,128)S(1)} %get-tuple-element.43, bf16[72,128]{1,0:T(8,128)(2,1)S(1)} %collective-permute-done.9, bf16[72,128]{1,0:T(8,128)(2,1)S(1)} %collective-permute-done.8, bf16[72,128]{1,0:T(8,128)(2,1)S(1)} %collective-permute-done.7), kind=kLoop, calls=%fused_computation.15 | loop fusion | flops 55296 | bytes 129024 | tf_op jit(solution)/shard_map/transpose | solution.py:390
  (32 shorter events, 0.2 us)
Async XLA Ops:
  0.6 4.6 %copy-start.8 = (f32[576]{0:T(1024)S(1)}, f32[576]{0:T(1024)}, u32[]{:S(2)}) copy-start(f32[576]{0:T(1024)} %param.10) | copy-start | bytes 6916
  0.6 4.6 %copy-start = (bf16[64,32,512]{2,1,0:T(8,128)(2,1)S(1)}, bf16[64,32,512]{2,1,0:T(8,128)(2,1)}, u32[]{:S(2)}) copy-start(bf16[64,32,512]{2,1,0:T(8,128)(2,1)} %param.12) | copy-start | bytes 6291460
  0.7 4.6 %copy-start.1 = (bf16[64,32,512]{2,1,0:T(8,128)(2,1)S(1)}, bf16[64,32,512]{2,1,0:T(8,128)(2,1)}, u32[]{:S(2)}) copy-start(bf16[64,32,512]{2,1,0:T(8,128)(2,1)} %param.14) | copy-start | bytes 6291460
  0.7 4.6 %copy-start.2 = (bf16[64,2048]{1,0:T(8,128)(2,1)S(1)}, bf16[64,2048]{1,0:T(8,128)(2,1)}, u32[]{:S(2)}) copy-start(bf16[64,2048]{1,0:T(8,128)(2,1)} %qrope_v.1) | copy-start | bytes 786436
  0.7 4.6 %copy-start.3 = (bf16[128,576]{0,1:T(8,128)(2,1)S(1)}, bf16[128,576]{0,1:T(8,128)(2,1)}, u32[]{:S(2)}) copy-start(bf16[128,576]{0,1:T(8,128)(2,1)} %param.9) | copy-start | bytes 442372
  0.7 4.6 %copy-start.4 = (bf16[64,576]{1,0:T(8,128)(2,1)S(1)}, bf16[64,576]{1,0:T(8,128)(2,1)}, u32[]{:S(2)}) copy-start(bf16[64,576]{1,0:T(8,128)(2,1)} %span_ref.1) | copy-start | bytes 221188
  0.7 4.6 %copy-start.5 = (s32[16]{0:T(128)S(1)}, s32[16]{0:T(128)}, u32[]{:S(2)}) copy-start(s32[16]{0:T(128)} %length_s.1) | copy-start | bytes 196
  0.7 4.6 %copy-start.6 = (s32[8]{0:T(128)S(1)}, s32[8]{0:T(128)}, u32[]{:S(2)}) copy-start(s32[8]{0:T(128)} %response_s.1) | copy-start | bytes 100
  0.7 4.6 %copy-start.7 = (s32[8]{0:T(128)S(1)}, s32[8]{0:T(128)}, u32[]{:S(2)}) copy-start(s32[8]{0:T(128)} %index_s.1) | copy-start | bytes 100
  0.7 9.9 %collective-permute-start.2 = (bf16[576,128]{1,0:T(8,128)(2,1)}, bf16[576,128]{1,0:T(8,128)(2,1)S(1)}, u32[]{:S(2)}, u32[]{:S(2)}) collective-permute-start(bf16[576,128]{1,0:T(8,128)(2,1)} %bitcast.53), channel_id=1, source_target_pairs={{0,3},{1,2},{2,1},{3,0},{4,7},{5,6},{6,5},{7,4},{8,11},{9,10},{10,... | collective-permute-start | bytes 442376 | tf_op jit(solution)/shard_map/ppermute | solution.py:259
  4.7 5.9 %collective-permute-start = (bf16[576,128]{1,0:T(8,128)(2,1)}, bf16[576,128]{1,0:T(8,128)(2,1)S(1)}, u32[]{:S(2)}, u32[]{:S(2)}) collective-permute-start(bf16[576,128]{1,0:T(8,128)(2,1)} %bitcast.54), channel_id=1, source_target_pairs={{0,1},{1,0},{2,3},{3,2},{4,6},{5,7},{6,4},{7,5},{8,9},{9,8},{10,11... | collective-permute-start | bytes 442376 | tf_op jit(solution)/shard_map/ppermute | solution.py:270
  10.6 1.4 %collective-permute-start.1 = (bf16[576,128]{1,0:T(8,128)(2,1)S(1)}, bf16[576,128]{1,0:T(8,128)(2,1)S(1)}, u32[]{:S(2)}, u32[]{:S(2)}) collective-permute-start(bf16[576,128]{1,0:T(8,128)(2,1)S(1)} %collective-permute-done.refs_0_), channel_id=1, source_target_pairs={{0,4},{4,0},{8,12},{12,8},{16,20},{20,16},{24,28},{28,24},{1,5},{5... | collective-permute-start | bytes 442376 | tf_op jit(solution)/shard_map/ppermute | solution.py:262
  18.5 1.6 %collective-permute-start.3 = (bf16[4,4,72,128]{3,2,1,0:T(8,128)(2,1)S(1)}, bf16[4,4,72,128]{3,2,1,0:T(8,128)(2,1)S(1)}, u32[]{:S(2)}, u32[]{:S(2)}) collective-permute-start(bf16[4,4,72,128]{3,2,1,0:T(8,128)(2,1)S(1)} %get-tuple-element.31), channel_id=1, source_target_pairs={{0,4},{4,0},{8,12},{12,8},{16,20},{20,16},{24,28},{28,24},{1,5},{5... | collective-permute-start | bytes 884744 | tf_op jit(solution)/shard_map/ppermute | solution.py:262
  20.3 6.0 %collective-permute-start.5 = (bf16[368,128]{1,0:T(8,128)(2,1)S(1)}, bf16[368,128]{1,0:T(8,128)(2,1)S(1)}, u32[]{:S(2)}, u32[]{:S(2)}) collective-permute-start(bf16[368,128]{1,0:T(8,128)(2,1)S(1)} %pad_maximum_fusion.1), channel_id=1, source_target_pairs={{0,2},{1,3},{2,0},{3,1},{4,6},{5,7},{6,4},{7,5},{8,10},{9,11},{10,... | collective-permute-start | bytes 282632 | tf_op jit(solution)/shard_map/ppermute | solution.py:259
  21.3 5.2 %collective-permute-start.6 = (bf16[368,128]{1,0:T(8,128)(2,1)S(1)}, bf16[368,128]{1,0:T(8,128)(2,1)S(1)}, u32[]{:S(2)}, u32[]{:S(2)}) collective-permute-start(bf16[368,128]{1,0:T(8,128)(2,1)S(1)} %pad_maximum_fusion.2), channel_id=1, source_target_pairs={{0,1},{1,0},{2,3},{3,2},{4,5},{5,4},{6,7},{7,6},{8,9},{9,8},{10,11... | collective-permute-start | bytes 282632 | tf_op jit(solution)/shard_map/ppermute | solution.py:259
  22.4 6.0 %collective-permute-start.4 = (bf16[368,128]{1,0:T(8,128)(2,1)S(1)}, bf16[368,128]{1,0:T(8,128)(2,1)S(1)}, u32[]{:S(2)}, u32[]{:S(2)}) collective-permute-start(bf16[368,128]{1,0:T(8,128)(2,1)S(1)} %pad_maximum_fusion), channel_id=1, source_target_pairs={{0,3},{1,2},{2,1},{3,0},{4,7},{5,6},{6,5},{7,4},{8,11},{9,10},{10,... | collective-permute-start | bytes 282632 | tf_op jit(solution)/shard_map/ppermute | solution.py:259
  28.6 6.8 %copy-start.9 = (f32[16,576]{1,0:T(8,128)}, f32[16,576]{1,0:T(8,128)S(1)}, u32[]{:S(2)}) copy-start(f32[16,576]{1,0:T(8,128)S(1)} %constant_dynamic-update-slice_fusion) | copy-start | bytes 110596
  28.6 6.8 %collective-permute-start.7 = (bf16[72,128]{1,0:T(8,128)(2,1)S(1)}, bf16[72,128]{1,0:T(8,128)(2,1)S(1)}, u32[]{:S(2)}, u32[]{:S(2)}) collective-permute-start(bf16[72,128]{1,0:T(8,128)(2,1)S(1)} %get-tuple-element.52), channel_id=1, source_target_pairs={{0,24},{4,28},{8,16},{12,20},{16,8},{20,12},{24,0},{28,4},{1,25},{... | collective-permute-start | bytes 55304 | tf_op jit(solution)/shard_map/ppermute | solution.py:262
  32.3 3.8 %collective-permute-start.9 = (bf16[72,128]{1,0:T(8,128)(2,1)S(1)}, bf16[72,128]{1,0:T(8,128)(2,1)S(1)}, u32[]{:S(2)}, u32[]{:S(2)}) collective-permute-start(bf16[72,128]{1,0:T(8,128)(2,1)S(1)} %get-tuple-element.53), channel_id=1, source_target_pairs={{0,8},{4,12},{8,0},{12,4},{16,24},{20,28},{24,16},{28,20},{1,9},{5... | collective-permute-start | bytes 55304 | tf_op jit(solution)/shard_map/ppermute | solution.py:262
  32.3 4.7 %collective-permute-start.8 = (bf16[72,128]{1,0:T(8,128)(2,1)S(1)}, bf16[72,128]{1,0:T(8,128)(2,1)S(1)}, u32[]{:S(2)}, u32[]{:S(2)}) collective-permute-start(bf16[72,128]{1,0:T(8,128)(2,1)S(1)} %get-tuple-element.54), channel_id=1, source_target_pairs={{0,16},{4,20},{8,24},{12,28},{16,0},{20,4},{24,8},{28,12},{1,17},{... | collective-permute-start | bytes 55304 | tf_op jit(solution)/shard_map/ppermute | solution.py:262

commit v3 on v2

--- a/solution.py
+++ b/solution.py
@@ -41,6 +41,14 @@
     key_pos = lax.broadcasted_iota(jnp.int32, mask_ref.shape, 0)
     row = lax.broadcasted_iota(jnp.int32, mask_ref.shape, 1)
     mask_ref[...] = jnp.where(key_pos * heads <= row, 1.0, 0.0)
+
+
+def partial_softmax(keys_ref, at, q_ref, qr_ref, up_ref):
+    latent = q_ref.shape[1]
+    logits = dot(keys_ref[:, :latent], q_ref[at, :], NT) + dot(
+        keys_ref[:, latent:], qr_ref[at, :], NT
+    )
+    return logits, dot(keys_ref[:, :latent], up_ref[at, :], NT) * SIGMA
 
 
 def early_kernel(
@@ -82,10 +90,7 @@
 
     for i in range(rows // STEP):
         at = pl.ds(i * STEP, STEP)
-        logits = dot(keys_ref[:, :latent], q_ref[at, :], NT) + dot(
-            keys_ref[:, latent:], qr_ref[at, :], NT
-        )
-        dprob = dot(keys_ref[:, :latent], up_ref[at, :], NT)
+        logits, dprob = partial_softmax(keys_ref, at, q_ref, qr_ref, up_ref)
         key_pos = lax.broadcasted_iota(jnp.int32, (tok, STEP), 0)
         seen = (mask_ref[:, at] > 0.5) & (key_pos < live)
         own = jnp.where(seen, logits[shard:], -jnp.inf)
@@ -98,7 +103,32 @@
         stat_ref[0:1, at] = top
         stat_ref[1:2, at] = jnp.sum(expo, axis=0, keepdims=True)
         stat_ref[2:3, at] = jnp.sum(expo * dprob, axis=0, keepdims=True)
-        stat_ref[3:4, at] = jnp.where(row_pos < live, SIGMA, 0.0)
+        stat_ref[3:4, at] = jnp.where(row_pos < live, 1.0, 0.0)
+
+
+def middle_kernel(scale_ref, q_ref, up_ref, qr_ref, stat_ref, *refs):
+    shard_refs = refs[:-4]
+    expo_ref, dprob_ref, out_ref, keys_ref = refs[-4:]
+    rows, latent = q_ref.shape
+    shard = shard_refs[0].shape[1]
+    for d, ref in enumerate(shard_refs):
+        put_keys(keys_ref, d * shard, latent, scaled_rows(ref[...], scale_ref[...]))
+    for i in range(rows // STEP):
+        at = pl.ds(i * STEP, STEP)
+        logits, dprob = partial_softmax(keys_ref, at, q_ref, qr_ref, up_ref)
+        before = stat_ref[0:1, at]
+        top = jnp.maximum(before, jnp.max(logits, axis=0, keepdims=True))
+        expo = jnp.exp2((logits - top) * EXP_SCALE)
+        again = jnp.exp2((before - top) * EXP_SCALE)
+        expo_ref[:, at] = expo
+        dprob_ref[:, at] = dprob
+        out_ref[0:1, at] = top
+        out_ref[1:2, at] = stat_ref[1:2, at] * again + jnp.sum(expo, axis=0, keepdims=True)
+        out_ref[2:3, at] = stat_ref[2:3, at] * again + jnp.sum(
+            expo * dprob, axis=0, keepdims=True
+        )
+        out_ref[3:4, at] = stat_ref[3:4, at]
+        out_ref[4:5, at] = before
 
 
 def keys_kernel(
@@ -108,62 +138,64 @@
     q_ref,
     up_ref,
     qr_ref,
-    expo_ref,
-    dprob_ref,
+    expo_a,
+    dprob_a,
+    keys_a,
+    expo_b,
+    dprob_b,
+    keys_b,
     stat_ref,
-    early_ref,
     *refs,
 ):
-    shard_refs = refs[: n_seq - 1]
-    mine_ref, theirs_ref, span_out, ds_ref, keys_ref, t_scr = refs[n_seq - 1 :]
+    shard_refs = refs[:-7]
+    mine_ref, theirs_ref, span_out, ds_ref, keys_ref, p_scr, keys_c = refs[-7:]
     rows, latent = q_ref.shape
-    full, shard = shard_refs[0].shape
+    full = scale_ref.shape[1]
+    shard = shard_refs[0].shape[1]
     rope = full - latent
     prompt = shard * n_seq
-    tok = early_ref.shape[0] - shard
+    tok = keys_a.shape[0] - shard
     my_resp = lax.axis_index("resp")
     my_seq = lax.axis_index("seq")
     odd = (my_resp % 2) == 1
 
+    middle = slice(shard, shard + keys_b.shape[0])
+    late = slice(middle.stop, prompt)
     scale = scale_ref[...]
-    keys_ref[:shard] = early_ref[:shard]
-    keys_ref[prompt:] = early_ref[shard:]
-    for d in range(1, n_seq):
-        value = shard_refs[d - 1][...]
-        if d < n_seq - 1:
-            other = shard_refs[(d - 1) ^ 1][...]
-            value = jnp.where(odd, other, value)
-        put_keys(keys_ref, d * shard, latent, scaled_rows(value, scale))
-
-    late = slice(shard, prompt)
+    for d, ref in enumerate(shard_refs):
+        put_keys(keys_c, d * shard, latent, scaled_rows(ref[...], scale))
+    keys_ref[:shard] = keys_a[:shard]
+    keys_ref[middle] = keys_b[...]
+    keys_ref[late] = keys_c[...]
+    keys_ref[prompt:] = keys_a[shard:]
+
     for i in range(rows // STEP):
         at = pl.ds(i * STEP, STEP)
-        logits = dot(keys_ref[late, :latent], q_ref[at, :], NT) + dot(
-            keys_ref[late, latent:], qr_ref[at, :], NT
-        )
-        dprob = dot(keys_ref[late, :latent], up_ref[at, :], NT)
-        early_top = stat_ref[0:1, at]
-        top = jnp.maximum(early_top, jnp.max(logits, axis=0, keepdims=True))
+        logits, dprob = partial_softmax(keys_c, at, q_ref, qr_ref, up_ref)
+        before = stat_ref[0:1, at]
+        top = jnp.maximum(before, jnp.max(logits, axis=0, keepdims=True))
         expo = jnp.exp2((logits - top) * EXP_SCALE)
-        again = jnp.exp2((early_top - top) * EXP_SCALE)
+        again = jnp.exp2((before - top) * EXP_SCALE)
         total = stat_ref[1:2, at] * again + jnp.sum(expo, axis=0, keepdims=True)
         weighed = stat_ref[2:3, at] * again + jnp.sum(expo * dprob, axis=0, keepdims=True)
         inverse = 1.0 / total
         delta = weighed * inverse
         factor = inverse * stat_ref[3:4, at]
         probs = expo * factor
-        t_scr[late, at] = probs.astype(BF16)
+        p_scr[late, at] = probs.astype(BF16)
         ds_ref[late, at] = (probs * (dprob - delta)).astype(BF16)
-        probs = expo_ref[:, at] * (factor * again)
-        dscore = probs * (dprob_ref[:, at] - delta)
-        t_scr[:shard, at] = probs[:shard].astype(BF16)
+        probs = expo_b[:, at] * (factor * again)
+        p_scr[middle, at] = probs.astype(BF16)
+        ds_ref[middle, at] = (probs * (dprob_b[:, at] - delta)).astype(BF16)
+        first = jnp.exp2((stat_ref[4:5, at] - top) * EXP_SCALE)
+        probs = expo_a[:, at] * (factor * first)
+        dscore = probs * (dprob_a[:, at] - delta)
+        p_scr[:shard, at] = probs[:shard].astype(BF16)
         ds_ref[:shard, at] = dscore[:shard].astype(BF16)
-        t_scr[prompt:, at] = probs[shard:].astype(BF16)
+        p_scr[prompt:, at] = probs[shard:].astype(BF16)
         ds_ref[prompt:, at] = dscore[shard:].astype(BF16)
 
-    grad_latent = dot(ds_ref[...], q_ref[...], NN) + dot(t_scr[...], up_ref[...], NN) * (
-        1.0 / SIGMA
-    )
+    grad_latent = dot(ds_ref[...], q_ref[...], NN) + dot(p_scr[...], up_ref[...], NN)
     grad_rope = dot(ds_ref[...], qr_ref[...], NN)
 
     piece = tok // n_seq
@@ -180,16 +212,25 @@
     cols = full // n_resp
     my_pair = my_resp // 2
     scale_twice = jnp.concatenate([scale[:, latent:]] * 2, axis=1)
-    for d in range(n_seq):
-        at = slice(d * shard, (d + 1) * shard)
+    pairs = n_seq // 2 - 1
+    for slot in range(n_seq):
+        at = slice(slot * shard, (slot + 1) * shard)
         lat = (grad_latent[at] * scale[:, :latent]).T
         rot = (grad_rope[at] * scale_twice).T
         whole = jnp.concatenate([lat, rot[:rope] + rot[rope:]], axis=0)
         for z in range(n_resp // 2):
             even_part = whole[2 * z * cols : (2 * z + 1) * cols]
             odd_part = whole[(2 * z + 1) * cols : (2 * z + 2) * cols]
-            mine_ref[d, z ^ my_pair] = jnp.where(odd, odd_part, even_part).astype(BF16)
-            theirs_ref[d, z ^ my_pair] = jnp.where(odd, even_part, odd_part).astype(BF16)
+            mine = jnp.where(odd, odd_part, even_part).astype(BF16)
+            theirs = jnp.where(odd, even_part, odd_part).astype(BF16)
+            if slot in (0, n_seq - 1):
+                d = slot
+            elif slot <= pairs:
+                d = 2 * slot - 1 + my_resp % 2
+            else:
+                d = 2 * (slot - pairs) - my_resp % 2
+            mine_ref[d, z ^ my_pair] = mine
+            theirs_ref[d, z ^ my_pair] = theirs
 
 
 def query_kernel(heads, first, count, ds_ref, keys_ref, *refs):
@@ -271,7 +312,6 @@
 
     prompt_t = prompt_cache.T
     fetched = [by_core(prompt_t, d) for d in range(1, n_seq - 1, 2)]
-    last = over_seq(prompt_t, n_seq - 1)
 
     scale_row = channel_scale.reshape(1, full)
     smem = pl.BlockSpec(memory_space=pltpu.SMEM)
@@ -287,6 +327,8 @@
         ),
         name="mask",
     )()
+    again, mask = lax.optimization_barrier((prompt_t, mask))
+    last = over_seq(again, n_seq - 1)
     q_turned, expo, dprob, stats, early_keys = pl.pallas_call(
         functools.partial(early_kernel, heads),
         out_shape=(
@@ -318,10 +360,25 @@
     )
 
     fetched, stats = lax.optimization_barrier((fetched, stats))
-    shards = []
-    for value in fetched:
-        shards += [value, over_resp(value, 1)]
-    shards.append(last)
+    swapped = [over_resp(value, 1) for value in fetched]
+    middle = shard * len(fetched)
+    expo_b, dprob_b, stats, middle_keys = pl.pallas_call(
+        middle_kernel,
+        out_shape=(
+            shape((middle, rows), F32),
+            shape((middle, rows), F32),
+            shape((8, rows), F32),
+            shape((middle, width)),
+        ),
+        in_specs=[vmem] * (5 + len(fetched)),
+        out_specs=(vmem,) * 4,
+        compiler_params=pltpu.CompilerParams(vmem_limit_bytes=24 * MIB),
+        cost_estimate=pl.CostEstimate(
+            flops=2 * middle * rows * 2 * latent, bytes_accessed=4 * rows * latent, transcendentals=0
+        ),
+        name="middle",
+    )(scale_row, q_rows, up_rows, q_turned, stats, *fetched)
+
     mine, theirs, span, dscore, keys_all = pl.pallas_call(
         functools.partial(keys_kernel, n_resp, n_seq),
         out_shape=(
@@ -331,15 +388,32 @@
             shape((keys, rows)),
             shape((keys, width)),
         ),
-        in_specs=[vmem] * (7 + n_seq),
+        in_specs=[vmem] * (12 + len(swapped)),
         out_specs=(vmem,) * 5,
-        scratch_shapes=[pltpu.VMEM((keys, rows), BF16)],
+        scratch_shapes=[
+            pltpu.VMEM((keys, rows), BF16),
+            pltpu.VMEM((shard * (len(swapped) + 1), width), BF16),
+        ],
         compiler_params=pltpu.CompilerParams(vmem_limit_bytes=24 * MIB),
         cost_estimate=pl.CostEstimate(
             flops=2 * keys * rows * 3 * latent, bytes_accessed=4 * rows * latent, transcendentals=0
         ),
         name="keys",
-    )(scale_row, q_rows, up_rows, q_turned, expo, dprob, stats, early_keys, *shards)
+    )(
+        scale_row,
+        q_rows,
+        up_rows,
+        q_turned,
+        expo,
+        dprob,
+        early_keys,
+        expo_b,
+        dprob_b,
+        middle_keys,
+        stats,
+        *swapped,
+        last,
+    )
 
     steps = tok // 16
 
@@ -372,7 +446,7 @@
         d: over_seq(jnp.concatenate([held[d].reshape(-1, 2 * rope), span[d]], axis=0), d)
         for d in range(n_seq - 1, 0, -1)
     }
-    half = (steps + 1) // 2
+    half = (3 * steps + 3) // 4
     partly = queries(0, half, dscore, keys_all, ())
     split = pairs * cols * shard // (2 * rope)
     block = summed[0].reshape(pairs, cols, shard)

time: 37.8 us -> 36.5 us (0.966)
  waiting for transfers between devices: 8.9 us -> 6.81 us
  Pallas kernels: 14 us -> 14.7 us
    ppermute x1, starting transfers between devices: 0.54 us -> 3 us  [by_core(): return lax.ppermute(x, ('resp', 'seq'), moves)]
    ppermute x1, waiting for transfers between devices: 2.37 us -> 0.01 us  [by_core(): return lax.ppermute(x, ('resp', 'seq'), moves)]
    ppermute x4, starting transfers between devices: 7.63 us -> 5.33 us  [over_seq(): return lax.ppermute(x, 'seq', [(i, i ^ d) for i in range(n_seq)])]
    pallas_call x0 -> x1, Pallas kernels: none -> 1.64 us  [on_device(): pl.pallas_call(middle_kernel, out_shape=(shape((middle, rows), F32), shap...]
    pallas_call x1, Pallas kernels: 6.53 us -> 5.58 us  [on_device(): pl.pallas_call(functools.partial(keys_kernel, n_resp, n_seq), out_shape=(...]
    ppermute x4, waiting for transfers between devices: 2.18 us -> 2.96 us  [over_seq(): return lax.ppermute(x, 'seq', [(i, i ^ d) for i in range(n_seq)])]
    ppermute x5, waiting for transfers between devices: 4.36 us -> 3.85 us  [over_resp(): return lax.ppermute(x, 'resp', [(i, i ^ d) for i in range(n_resp)])]
  transfers between devices with their start and end apart: 10 -> 10, of which waited for: 7 -> 5; matrix products, arithmetic and copies ran while one was open for 0% -> 0% of each run, Pallas kernels for 20% -> 25%
where the time goes in v3:
time: 36.5 us; the launch traced here: 36.3 us
  Pallas kernels  14.7 us (40%)
  starting transfers between devices  12.9 us (35%)
  waiting for transfers between devices  6.81 us (19%)
  between operations  0.97 us (3%)
  other arithmetic  0.79 us (2%)
    pallas_call x1, Pallas kernels, on_device(): pl.pallas_call(functools.partial(keys_kernel, n_resp, n_seq), out_shape=(...  5.58 us
    ppermute x4, starting transfers between devices, over_seq(): return lax.ppermute(x, 'seq', [(i, i ^ d) for i in range(n_seq)])  5.33 us
    ppermute x5, starting transfers between devices, over_resp(): return lax.ppermute(x, 'resp', [(i, i ^ d) for i in range(n_resp)])  4.59 us
    pallas_call x2, Pallas kernels, queries(): pl.pallas_call(functools.partial(query_kernel, heads, first, count), out_...  4.56 us
    ppermute x5, waiting for transfers between devices, over_resp(): return lax.ppermute(x, 'resp', [(i, i ^ d) for i in range(n_resp)])  3.85 us
    ppermute x1, starting transfers between devices, by_core(): return lax.ppermute(x, ('resp', 'seq'), moves)  3 us
    ppermute x4, waiting for transfers between devices, over_seq(): return lax.ppermute(x, 'seq', [(i, i ^ d) for i in range(n_seq)])  2.96 us
    pallas_call x1, Pallas kernels, on_device(): pl.pallas_call(functools.partial(early_kernel, heads), out_shape=(shape((...  2.9 us
  transfers between devices with their start and end apart: 10, of which 5 were waited for; matrix products, arithmetic and copies ran while one was open for 0% of the time, Pallas kernels for 25%

profile of v3, /device:TPU:0, one launch (start us, length us, event | category | flops | bytes accessed | tf_op | source)
XLA Modules:
  0.0 36.3 jit_solution(6355452186188277948)
XLA Ops:
  0.6 0.0 copy-start.3
  0.6 0.0 copy-start.8
  0.7 3.0 %collective-permute-start = (bf16[576,128]{1,0:T(8,128)(2,1)}, bf16[576,128]{1,0:T(8,128)(2,1)S(1)}, u32[]{:S(2)}, u32[]{:S(2)}) collective-permute-start(bf16[576,128]{1,0:T(8,128)(2,1)} %bitcast.55), channel_id=1, source_target_pairs={{0,1},{1,0},{2,3},{3,2},{4,6},{5,7},{6,4},{7,5},{8,9},{9,8},{10,11... | collective-permute-start | bytes 442376 | tf_op jit(solution)/shard_map/ppermute | solution.py:311
  3.8 0.0 copy-done.3
  3.8 1.7 %collective-permute-start.2 = (bf16[576,128]{1,0:T(8,128)(2,1)S(1)}, bf16[576,128]{1,0:T(8,128)(2,1)S(1)}, u32[]{:S(2)}, u32[]{:S(2)}) collective-permute-start(bf16[576,128]{1,0:T(8,128)(2,1)S(1)} %bitcast.56), channel_id=1, source_target_pairs={{0,3},{1,2},{2,1},{3,0},{4,7},{5,6},{6,5},{7,4},{8,11},{9,10},{10,... | collective-permute-start | bytes 442376 | tf_op jit(solution)/shard_map/ppermute | solution.py:300
  5.4 0.0 copy-done.8
  5.5 2.9 %early.1 = (bf16[2048,128]{1,0:T(8,128)(2,1)S(1)}, f32[192,2048]{1,0:T(8,128)S(1)}, f32[192,2048]{1,0:T(8,128)S(1)}, f32[8,2048]{1,0:T(8,128)S(1)}, bf16[192,640]{1,0:T(8,128)(2,1)S(1)}) custom-call(s32[16]{0:T(128)S(1)} %copy-done.5, s32[8]{0:T(128)S(1)} %copy-done.6, s32[8]{0:T(128)S(1)} %copy-done.7, f32[64,2048]{1,0:T(8,128)S(1)} %mask.1.mask_ref, ...), custom_call_target="tpu_custom_call" | custom-call | flops 805306368 | bytes 4194304 | tf_op jit(solution)/shard_map/early/pallas_call | solution.py:332
  8.4 0.0 collective-permute-done.refs_0_
  8.4 0.1 collective-permute-start.1
  8.5 1.6 %middle.1 = (f32[128,2048]{1,0:T(8,128)S(1)}, f32[128,2048]{1,0:T(8,128)S(1)}, f32[8,2048]{1,0:T(8,128)S(1)}, bf16[128,640]{1,0:T(8,128)(2,1)S(1)}) custom-call(f32[1,576]{1,0:T(1,128)S(1)} %reshape.49.scale_ref, bf16[2048,512]{1,0:T(8,128)(2,1)S(1)} %bitcast.50, bf16[2048,512]{1,0:T(8,128)(2,1)S(1)} %bitcast.53, ...), custom_call_target="tpu_custom_call" | custom-call | flops 536870912 | bytes 4194304 | tf_op jit(solution)/shard_map/middle/pallas_call | solution.py:365
  10.1 1.5 %collective-permute-done.2.refs_1_ = bf16[576,128]{1,0:T(8,128)(2,1)S(1)} collective-permute-done((bf16[576,128]{1,0:T(8,128)(2,1)S(1)}, bf16[576,128]{1,0:T(8,128)(2,1)S(1)}, u32[]{:S(2)}, u32[]{:S(2)}) %collective-permute-start.2) | collective-permute-done | bytes 147488 | tf_op jit(solution)/shard_map/ppermute | solution.py:300
  11.7 0.0 collective-permute-done.1.refs_0_
  11.7 5.6 %keys.1 = (bf16[4,4,72,128]{3,2,1,0:T(8,128)(2,1)S(1)}, bf16[4,4,72,128]{3,2,1,0:T(8,128)(2,1)S(1)}, bf16[4,80,128]{2,1,0:T(8,128)(2,1)S(1)}, bf16[576,2048]{1,0:T(8,128)(2,1)S(1)}, bf16[576,640]{1,0:T(8,128)(2,1)S(1)}) custom-call(f32[1,576]{1,0:T(1,128)S(1)} %reshape.49.scale_ref, bf16[2048,512]{1,0:T(8,128)(2,1)S(1)} %bitcast.51, ...), custom_call_target="tpu_custom_call" | custom-call | flops 3623878656 | bytes 4194304 | tf_op jit(solution)/shard_map/keys/pallas_call | solution.py:382
  17.3 0.1 collective-permute-start.3
  17.4 1.6 %collective-permute-done.3 = bf16[4,4,72,128]{3,2,1,0:T(8,128)(2,1)S(1)} collective-permute-done((bf16[4,4,72,128]{3,2,1,0:T(8,128)(2,1)S(1)}, bf16[4,4,72,128]{3,2,1,0:T(8,128)(2,1)S(1)}, u32[]{:S(2)}, u32[]{:S(2)}) %collective-permute-start.3) | collective-permute-done | bytes 294944 | tf_op jit(solution)/shard_map/ppermute | solution.py:303
  18.9 0.1 convert_add_fusion
  19.0 0.9 %collective-permute-start.5 = (bf16[368,128]{1,0:T(8,128)(2,1)S(1)}, bf16[368,128]{1,0:T(8,128)(2,1)S(1)}, u32[]{:S(2)}, u32[]{:S(2)}) collective-permute-start(bf16[368,128]{1,0:T(8,128)(2,1)S(1)} %pad_maximum_fusion.1), channel_id=1, source_target_pairs={{0,2},{1,3},{2,0},{3,1},{4,6},{5,7},{6,4},{7,5},{8,10},{9,11},{10,... | collective-permute-start | bytes 282632 | tf_op jit(solution)/shard_map/ppermute | solution.py:300
  19.9 1.6 %collective-permute-start.6 = (bf16[368,128]{1,0:T(8,128)(2,1)S(1)}, bf16[368,128]{1,0:T(8,128)(2,1)S(1)}, u32[]{:S(2)}, u32[]{:S(2)}) collective-permute-start(bf16[368,128]{1,0:T(8,128)(2,1)S(1)} %pad_maximum_fusion.2), channel_id=1, source_target_pairs={{0,1},{1,0},{2,3},{3,2},{4,5},{5,4},{6,7},{7,6},{8,9},{9,8},{10,11... | collective-permute-start | bytes 282632 | tf_op jit(solution)/shard_map/ppermute | solution.py:300
  21.5 1.3 %collective-permute-start.4 = (bf16[368,128]{1,0:T(8,128)(2,1)S(1)}, bf16[368,128]{1,0:T(8,128)(2,1)S(1)}, u32[]{:S(2)}, u32[]{:S(2)}) collective-permute-start(bf16[368,128]{1,0:T(8,128)(2,1)S(1)} %pad_maximum_fusion), channel_id=1, source_target_pairs={{0,3},{1,2},{2,1},{3,0},{4,7},{5,6},{6,5},{7,4},{8,11},{9,10},{10,... | collective-permute-start | bytes 282632 | tf_op jit(solution)/shard_map/ppermute | solution.py:300
  22.7 3.0 %queries.2 = (bf16[2048,512]{1,0:T(8,128)(2,1)}, bf16[64,2048]{1,0:T(8,128)(2,1)}) custom-call(bf16[576,2048]{1,0:T(8,128)(2,1)S(1)} %get-tuple-element.47.ds_ref, bf16[576,640]{1,0:T(8,128)(2,1)S(1)} %get-tuple-element.48.keys_ref), custom_call_target="tpu_custom_call" | custom-call | flops 1132462080 | bytes 1572864 | tf_op jit(solution)/shard_map/queries/pallas_call | solution.py:421
  25.7 0.0 collective-permute-done.5
  25.8 0.0 collective-permute-done.6
  25.8 1.4 %collective-permute-done.4 = bf16[368,128]{1,0:T(8,128)(2,1)S(1)} collective-permute-done((bf16[368,128]{1,0:T(8,128)(2,1)S(1)}, bf16[368,128]{1,0:T(8,128)(2,1)S(1)}, u32[]{:S(2)}, u32[]{:S(2)}) %collective-permute-start.4) | collective-permute-done | bytes 94240 | tf_op jit(solution)/shard_map/ppermute | solution.py:300
  27.4 0.0 copy-start.9
  27.4 3.7 %collective-permute-start.7 = (bf16[72,128]{1,0:T(8,128)(2,1)S(1)}, bf16[72,128]{1,0:T(8,128)(2,1)S(1)}, u32[]{:S(2)}, u32[]{:S(2)}) collective-permute-start(bf16[72,128]{1,0:T(8,128)(2,1)S(1)} %get-tuple-element.64), channel_id=1, source_target_pairs={{0,24},{4,28},{8,16},{12,20},{16,8},{20,12},{24,0},{28,4},{1,25},{... | collective-permute-start | bytes 55304 | tf_op jit(solution)/shard_map/ppermute | solution.py:303
  31.0 0.0 collective-permute-start.9
  31.0 0.8 %collective-permute-start.8 = (bf16[72,128]{1,0:T(8,128)(2,1)S(1)}, bf16[72,128]{1,0:T(8,128)(2,1)S(1)}, u32[]{:S(2)}, u32[]{:S(2)}) collective-permute-start(bf16[72,128]{1,0:T(8,128)(2,1)S(1)} %get-tuple-element.66), channel_id=1, source_target_pairs={{0,16},{4,20},{8,24},{12,28},{16,0},{20,4},{24,8},{28,12},{1,17},{... | collective-permute-start | bytes 55304 | tf_op jit(solution)/shard_map/ppermute | solution.py:303
  31.8 1.6 %queries.3 = (bf16[2048,512]{1,0:T(8,128)(2,1)}, bf16[64,2048]{1,0:T(8,128)(2,1)}) custom-call(bf16[576,2048]{1,0:T(8,128)(2,1)S(1)} %get-tuple-element.47.ds_ref, bf16[576,640]{1,0:T(8,128)(2,1)S(1)} %get-tuple-element.48.keys_ref, bf16[2048,512]{1,0:T(8,128)(2,1)} %get-tuple-element.49.refs_0_, ...), custom_call_target="tpu_custom_call", output_to_operand_aliasing={{0}: (2, {}), {1}: (3, {})} | custom-call | flops 377487360 | bytes 524288 | tf_op jit(solution)/shard_map/queries/pallas_call | solution.py:421
  33.4 0.0 collective-permute-done.7
  33.4 1.4 %collective-permute-done.9 = bf16[72,128]{1,0:T(8,128)(2,1)S(1)} collective-permute-done((bf16[72,128]{1,0:T(8,128)(2,1)S(1)}, bf16[72,128]{1,0:T(8,128)(2,1)S(1)}, u32[]{:S(2)}, u32[]{:S(2)}) %collective-permute-start.9) | collective-permute-done | bytes 18464 | tf_op jit(solution)/shard_map/ppermute | solution.py:303
  34.8 0.9 %collective-permute-done.8 = bf16[72,128]{1,0:T(8,128)(2,1)S(1)} collective-permute-done((bf16[72,128]{1,0:T(8,128)(2,1)S(1)}, bf16[72,128]{1,0:T(8,128)(2,1)S(1)}, u32[]{:S(2)}, u32[]{:S(2)}) %collective-permute-start.8) | collective-permute-done | bytes 18464 | tf_op jit(solution)/shard_map/ppermute | solution.py:303
  35.7 0.6 %fusion.8 = f32[128,72]{0,1:T(8,128)} fusion(f32[4,72,128]{2,1,0:T(8,128)S(1)} %get-tuple-element.55, bf16[72,128]{1,0:T(8,128)(2,1)S(1)} %collective-permute-done.9, bf16[72,128]{1,0:T(8,128)(2,1)S(1)} %collective-permute-done.8, bf16[72,128]{1,0:T(8,128)(2,1)S(1)} %collective-permute-done.7), kind=kLoop, calls=%fused_computation.15 | loop fusion | flops 55296 | bytes 129024 | tf_op jit(solution)/shard_map/transpose | solution.py:464
  (33 shorter events, 0.2 us)
Async XLA Ops:
  0.6 3.1 %copy-start.3 = (bf16[128,576]{0,1:T(8,128)(2,1)S(1)}, bf16[128,576]{0,1:T(8,128)(2,1)}, u32[]{:S(2)}) copy-start(bf16[128,576]{0,1:T(8,128)(2,1)} %param.9) | copy-start | bytes 442372
  0.6 4.8 %copy-start.8 = (f32[576]{0:T(1024)S(1)}, f32[576]{0:T(1024)}, u32[]{:S(2)}) copy-start(f32[576]{0:T(1024)} %param.10) | copy-start | bytes 6916
  0.7 4.8 %copy-start = (bf16[64,32,512]{2,1,0:T(8,128)(2,1)S(1)}, bf16[64,32,512]{2,1,0:T(8,128)(2,1)}, u32[]{:S(2)}) copy-start(bf16[64,32,512]{2,1,0:T(8,128)(2,1)} %param.12) | copy-start | bytes 6291460
  0.7 4.8 %copy-start.1 = (bf16[64,32,512]{2,1,0:T(8,128)(2,1)S(1)}, bf16[64,32,512]{2,1,0:T(8,128)(2,1)}, u32[]{:S(2)}) copy-start(bf16[64,32,512]{2,1,0:T(8,128)(2,1)} %param.14) | copy-start | bytes 6291460
  0.7 4.8 %copy-start.2 = (bf16[64,2048]{1,0:T(8,128)(2,1)S(1)}, bf16[64,2048]{1,0:T(8,128)(2,1)}, u32[]{:S(2)}) copy-start(bf16[64,2048]{1,0:T(8,128)(2,1)} %qrope_v.1) | copy-start | bytes 786436
  0.7 4.8 %copy-start.4 = (bf16[64,576]{1,0:T(8,128)(2,1)S(1)}, bf16[64,576]{1,0:T(8,128)(2,1)}, u32[]{:S(2)}) copy-start(bf16[64,576]{1,0:T(8,128)(2,1)} %span_ref.1) | copy-start | bytes 221188
  0.7 4.8 %copy-start.5 = (s32[16]{0:T(128)S(1)}, s32[16]{0:T(128)}, u32[]{:S(2)}) copy-start(s32[16]{0:T(128)} %length_s.1) | copy-start | bytes 196
  0.7 4.8 %copy-start.6 = (s32[8]{0:T(128)S(1)}, s32[8]{0:T(128)}, u32[]{:S(2)}) copy-start(s32[8]{0:T(128)} %response_s.1) | copy-start | bytes 100
  0.7 4.8 %copy-start.7 = (s32[8]{0:T(128)S(1)}, s32[8]{0:T(128)}, u32[]{:S(2)}) copy-start(s32[8]{0:T(128)} %index_s.1) | copy-start | bytes 100
  0.7 7.7 %collective-permute-start = (bf16[576,128]{1,0:T(8,128)(2,1)}, bf16[576,128]{1,0:T(8,128)(2,1)S(1)}, u32[]{:S(2)}, u32[]{:S(2)}) collective-permute-start(bf16[576,128]{1,0:T(8,128)(2,1)} %bitcast.55), channel_id=1, source_target_pairs={{0,1},{1,0},{2,3},{3,2},{4,6},{5,7},{6,4},{7,5},{8,9},{9,8},{10,11... | collective-permute-start | bytes 442376 | tf_op jit(solution)/shard_map/ppermute | solution.py:311
  3.8 7.9 %collective-permute-start.2 = (bf16[576,128]{1,0:T(8,128)(2,1)S(1)}, bf16[576,128]{1,0:T(8,128)(2,1)S(1)}, u32[]{:S(2)}, u32[]{:S(2)}) collective-permute-start(bf16[576,128]{1,0:T(8,128)(2,1)S(1)} %bitcast.56), channel_id=1, source_target_pairs={{0,3},{1,2},{2,1},{3,0},{4,7},{5,6},{6,5},{7,4},{8,11},{9,10},{10,... | collective-permute-start | bytes 442376 | tf_op jit(solution)/shard_map/ppermute | solution.py:300
  8.4 3.2 %collective-permute-start.1 = (bf16[576,128]{1,0:T(8,128)(2,1)S(1)}, bf16[576,128]{1,0:T(8,128)(2,1)S(1)}, u32[]{:S(2)}, u32[]{:S(2)}) collective-permute-start(bf16[576,128]{1,0:T(8,128)(2,1)S(1)} %collective-permute-done.refs_0_), channel_id=1, source_target_pairs={{0,4},{4,0},{8,12},{12,8},{16,20},{20,16},{24,28},{28,24},{1,5},{5... | collective-permute-start | bytes 442376 | tf_op jit(solution)/shard_map/ppermute | solution.py:303
  17.3 1.6 %collective-permute-start.3 = (bf16[4,4,72,128]{3,2,1,0:T(8,128)(2,1)S(1)}, bf16[4,4,72,128]{3,2,1,0:T(8,128)(2,1)S(1)}, u32[]{:S(2)}, u32[]{:S(2)}) collective-permute-start(bf16[4,4,72,128]{3,2,1,0:T(8,128)(2,1)S(1)} %get-tuple-element.43), channel_id=1, source_target_pairs={{0,4},{4,0},{8,12},{12,8},{16,20},{20,16},{24,28},{28,24},{1,5},{5... | collective-permute-start | bytes 884744 | tf_op jit(solution)/shard_map/ppermute | solution.py:303
  19.0 6.7 %collective-permute-start.5 = (bf16[368,128]{1,0:T(8,128)(2,1)S(1)}, bf16[368,128]{1,0:T(8,128)(2,1)S(1)}, u32[]{:S(2)}, u32[]{:S(2)}) collective-permute-start(bf16[368,128]{1,0:T(8,128)(2,1)S(1)} %pad_maximum_fusion.1), channel_id=1, source_target_pairs={{0,2},{1,3},{2,0},{3,1},{4,6},{5,7},{6,4},{7,5},{8,10},{9,11},{10,... | collective-permute-start | bytes 282632 | tf_op jit(solution)/shard_map/ppermute | solution.py:300
  19.9 5.9 %collective-permute-start.6 = (bf16[368,128]{1,0:T(8,128)(2,1)S(1)}, bf16[368,128]{1,0:T(8,128)(2,1)S(1)}, u32[]{:S(2)}, u32[]{:S(2)}) collective-permute-start(bf16[368,128]{1,0:T(8,128)(2,1)S(1)} %pad_maximum_fusion.2), channel_id=1, source_target_pairs={{0,1},{1,0},{2,3},{3,2},{4,5},{5,4},{6,7},{7,6},{8,9},{9,8},{10,11... | collective-permute-start | bytes 282632 | tf_op jit(solution)/shard_map/ppermute | solution.py:300
  21.5 5.8 %collective-permute-start.4 = (bf16[368,128]{1,0:T(8,128)(2,1)S(1)}, bf16[368,128]{1,0:T(8,128)(2,1)S(1)}, u32[]{:S(2)}, u32[]{:S(2)}) collective-permute-start(bf16[368,128]{1,0:T(8,128)(2,1)S(1)} %pad_maximum_fusion), channel_id=1, source_target_pairs={{0,3},{1,2},{2,1},{3,0},{4,7},{5,6},{6,5},{7,4},{8,11},{9,10},{10,... | collective-permute-start | bytes 282632 | tf_op jit(solution)/shard_map/ppermute | solution.py:300
  27.4 6.0 %copy-start.9 = (f32[16,576]{1,0:T(8,128)}, f32[16,576]{1,0:T(8,128)S(1)}, u32[]{:S(2)}) copy-start(f32[16,576]{1,0:T(8,128)S(1)} %constant_dynamic-update-slice_fusion) | copy-start | bytes 110596
  27.4 6.0 %collective-permute-start.7 = (bf16[72,128]{1,0:T(8,128)(2,1)S(1)}, bf16[72,128]{1,0:T(8,128)(2,1)S(1)}, u32[]{:S(2)}, u32[]{:S(2)}) collective-permute-start(bf16[72,128]{1,0:T(8,128)(2,1)S(1)} %get-tuple-element.64), channel_id=1, source_target_pairs={{0,24},{4,28},{8,16},{12,20},{16,8},{20,12},{24,0},{28,4},{1,25},{... | collective-permute-start | bytes 55304 | tf_op jit(solution)/shard_map/ppermute | solution.py:303
  31.0 3.8 %collective-permute-start.9 = (bf16[72,128]{1,0:T(8,128)(2,1)S(1)}, bf16[72,128]{1,0:T(8,128)(2,1)S(1)}, u32[]{:S(2)}, u32[]{:S(2)}) collective-permute-start(bf16[72,128]{1,0:T(8,128)(2,1)S(1)} %get-tuple-element.65), channel_id=1, source_target_pairs={{0,8},{4,12},{8,0},{12,4},{16,24},{20,28},{24,16},{28,20},{1,9},{5... | collective-permute-start | bytes 55304 | tf_op jit(solution)/shard_map/ppermute | solution.py:303
  31.0 4.7 %collective-permute-start.8 = (bf16[72,128]{1,0:T(8,128)(2,1)S(1)}, bf16[72,128]{1,0:T(8,128)(2,1)S(1)}, u32[]{:S(2)}, u32[]{:S(2)}) collective-permute-start(bf16[72,128]{1,0:T(8,128)(2,1)S(1)} %get-tuple-element.66), channel_id=1, source_target_pairs={{0,16},{4,20},{8,24},{12,28},{16,0},{20,4},{24,8},{28,12},{1,17},{... | collective-permute-start | bytes 55304 | tf_op jit(solution)/shard_map/ppermute | solution.py:303

commit v4 on v3

--- a/solution.py
+++ b/solution.py
@@ -231,6 +231,19 @@
                 d = 2 * (slot - pairs) - my_resp % 2
             mine_ref[d, z ^ my_pair] = mine
             theirs_ref[d, z ^ my_pair] = theirs
+
+
+def sum_kernel(mine_ref, theirs_ref, span_ref, own_ref, *pay_refs):
+    pairs, cols, lanes = mine_ref.shape[1:]
+    for d in range(len(pay_refs) + 1):
+        for z in range(pairs):
+            total = mine_ref[d, z].astype(F32) + theirs_ref[d, z].astype(F32)
+            if d == 0:
+                own_ref[z] = total
+            else:
+                pay_refs[d - 1][pl.ds(z * cols, cols), :] = total.astype(BF16)
+        if d:
+            pay_refs[d - 1][pl.ds(pairs * cols, span_ref.shape[1]), :] = span_ref[d]
 
 
 def query_kernel(heads, first, count, ds_ref, keys_ref, *refs):
@@ -440,20 +453,32 @@
             name="queries",
         )(dscore, keys_all, *before)
 
-    summed = mine.astype(F32) + over_resp(theirs, 1).astype(F32)
-    held = summed.astype(BF16).reshape(n_seq, pairs * cols, shard)
-    moved = {
-        d: over_seq(jnp.concatenate([held[d].reshape(-1, 2 * rope), span[d]], axis=0), d)
-        for d in range(n_seq - 1, 0, -1)
-    }
+    theirs = over_resp(theirs, 1)
+    farthest = mine[-1].astype(F32) + theirs[-1].astype(F32)
+    farthest = jnp.concatenate(
+        [farthest.astype(BF16).reshape(-1, 2 * rope), span[-1]], axis=0
+    )
+    moved = [over_seq(farthest, n_seq - 1)]
+    block, *pays = pl.pallas_call(
+        sum_kernel,
+        out_shape=[shape((pairs, cols, shard), F32)]
+        + [shape((pairs * cols + span_rows, shard))] * (n_seq - 2),
+        in_specs=[vmem] * 3,
+        out_specs=[vmem] * (n_seq - 1),
+        compiler_params=pltpu.CompilerParams(vmem_limit_bytes=8 * MIB),
+        cost_estimate=pl.CostEstimate(
+            flops=keys * rows * width, bytes_accessed=4 * keys * width, transcendentals=0
+        ),
+        name="sums",
+    )(mine, theirs, span)
+    moved += [over_seq(pay, d + 1) for d, pay in enumerate(pays)]
     half = (3 * steps + 3) // 4
     partly = queries(0, half, dscore, keys_all, ())
-    split = pairs * cols * shard // (2 * rope)
-    block = summed[0].reshape(pairs, cols, shard)
+    split = pairs * cols
     own = span[0].astype(F32)
-    for d in moved:
-        block = block + moved[d][:split].reshape(pairs, cols, shard).astype(F32)
-        own = own + moved[d][split:].astype(F32)
+    for x in moved:
+        block = block + x[:split].reshape(pairs, cols, shard).astype(F32)
+        own = own + x[split:].astype(F32)
     block_half = block.astype(BF16)
     block_half, dscore, keys_all = lax.optimization_barrier((block_half, dscore, keys_all))
     arrived = [over_resp(block_half[d], 2 * d) for d in range(pairs - 1, 0, -1)]

time: 36.5 us -> 35.9 us (0.984)
  waiting for transfers between devices: 6.81 us -> 6.41 us
    ppermute x4, waiting for transfers between devices: 2.96 us -> 2.56 us  [over_seq(): return lax.ppermute(x, 'seq', [(i, i ^ d) for i in range(n_seq)])]
  transfers between devices with their start and end apart: 10 -> 10, of which waited for: 5 -> 6; matrix products, arithmetic and copies ran while one was open for 0% -> 0% of each run, Pallas kernels for 25% -> 26%
where the time goes in v4:
time: 35.9 us; the launch traced here: 35.8 us
  Pallas kernels  14.8 us (41%)
  starting transfers between devices  12.9 us (36%)
  waiting for transfers between devices  6.41 us (18%)
  between operations  0.95 us (3%)
  other arithmetic  0.72 us (2%)
    pallas_call x1, Pallas kernels, on_device(): pl.pallas_call(functools.partial(keys_kernel, n_resp, n_seq), out_shape=(...  5.58 us
    ppermute x4, starting transfers between devices, over_seq(): return lax.ppermute(x, 'seq', [(i, i ^ d) for i in range(n_seq)])  5.28 us
    ppermute x5, starting transfers between devices, over_resp(): return lax.ppermute(x, 'resp', [(i, i ^ d) for i in range(n_resp)])  4.59 us
    pallas_call x2, Pallas kernels, queries(): pl.pallas_call(functools.partial(query_kernel, heads, first, count), out_...  4.57 us
    ppermute x5, waiting for transfers between devices, over_resp(): return lax.ppermute(x, 'resp', [(i, i ^ d) for i in range(n_resp)])  3.84 us
    ppermute x1, starting transfers between devices, by_core(): return lax.ppermute(x, ('resp', 'seq'), moves)  3 us
    pallas_call x1, Pallas kernels, on_device(): pl.pallas_call(functools.partial(early_kernel, heads), out_shape=(shape((...  2.86 us
    ppermute x4, waiting for transfers between devices, over_seq(): return lax.ppermute(x, 'seq', [(i, i ^ d) for i in range(n_seq)])  2.56 us
  transfers between devices with their start and end apart: 10, of which 6 were waited for; matrix products, arithmetic and copies ran while one was open for 0% of the time, Pallas kernels for 26%

profile of v4, /device:TPU:0, one launch (start us, length us, event | category | flops | bytes accessed | tf_op | source)
XLA Modules:
  0.0 35.8 jit_solution(12072337119304267445)
XLA Ops:
  0.6 0.0 copy-start.3
  0.6 0.0 copy-start.8
  0.7 0.0 copy-start
  0.7 0.0 copy-start.1
  0.7 3.0 %collective-permute-start = (bf16[576,128]{1,0:T(8,128)(2,1)}, bf16[576,128]{1,0:T(8,128)(2,1)S(1)}, u32[]{:S(2)}, u32[]{:S(2)}) collective-permute-start(bf16[576,128]{1,0:T(8,128)(2,1)} %bitcast.40), channel_id=1, source_target_pairs={{0,1},{1,0},{2,3},{3,2},{4,6},{5,7},{6,4},{7,5},{8,9},{9,8},{10,11... | collective-permute-start | bytes 442376 | tf_op jit(solution)/shard_map/ppermute | solution.py:324
  3.8 1.7 %collective-permute-start.2 = (bf16[576,128]{1,0:T(8,128)(2,1)S(1)}, bf16[576,128]{1,0:T(8,128)(2,1)S(1)}, u32[]{:S(2)}, u32[]{:S(2)}) collective-permute-start(bf16[576,128]{1,0:T(8,128)(2,1)S(1)} %bitcast.41), channel_id=1, source_target_pairs={{0,3},{1,2},{2,1},{3,0},{4,7},{5,6},{6,5},{7,4},{8,11},{9,10},{10,... | collective-permute-start | bytes 442376 | tf_op jit(solution)/shard_map/ppermute | solution.py:313
  5.5 2.9 %early.1 = (bf16[2048,128]{1,0:T(8,128)(2,1)S(1)}, f32[192,2048]{1,0:T(8,128)S(1)}, f32[192,2048]{1,0:T(8,128)S(1)}, f32[8,2048]{1,0:T(8,128)S(1)}, bf16[192,640]{1,0:T(8,128)(2,1)S(1)}) custom-call(s32[16]{0:T(128)S(1)} %copy-done.5, s32[8]{0:T(128)S(1)} %copy-done.6, s32[8]{0:T(128)S(1)} %copy-done.7, f32[64,2048]{1,0:T(8,128)S(1)} %mask.1.mask_ref, ...), custom_call_target="tpu_custom_call" | custom-call | flops 805306368 | bytes 4194304 | tf_op jit(solution)/shard_map/early/pallas_call | solution.py:345
  8.4 0.0 collective-permute-done.refs_0_
  8.4 0.1 collective-permute-start.1
  8.5 1.6 %middle.1 = (f32[128,2048]{1,0:T(8,128)S(1)}, f32[128,2048]{1,0:T(8,128)S(1)}, f32[8,2048]{1,0:T(8,128)S(1)}, bf16[128,640]{1,0:T(8,128)(2,1)S(1)}) custom-call(f32[1,576]{1,0:T(1,128)S(1)} %reshape.49.scale_ref, bf16[2048,512]{1,0:T(8,128)(2,1)S(1)} %bitcast.35, bf16[2048,512]{1,0:T(8,128)(2,1)S(1)} %bitcast.38, ...), custom_call_target="tpu_custom_call" | custom-call | flops 536870912 | bytes 4194304 | tf_op jit(solution)/shard_map/middle/pallas_call | solution.py:378
  10.1 1.6 %collective-permute-done.2.refs_1_ = bf16[576,128]{1,0:T(8,128)(2,1)S(1)} collective-permute-done((bf16[576,128]{1,0:T(8,128)(2,1)S(1)}, bf16[576,128]{1,0:T(8,128)(2,1)S(1)}, u32[]{:S(2)}, u32[]{:S(2)}) %collective-permute-start.2) | collective-permute-done | bytes 147488 | tf_op jit(solution)/shard_map/ppermute | solution.py:313
  11.7 0.0 collective-permute-done.1.refs_0_
  11.7 5.6 %keys.1 = (bf16[4,4,72,128]{3,2,1,0:T(8,128)(2,1)S(1)}, bf16[4,4,72,128]{3,2,1,0:T(8,128)(2,1)S(1)}, bf16[4,80,128]{2,1,0:T(8,128)(2,1)S(1)}, bf16[576,2048]{1,0:T(8,128)(2,1)S(1)}, bf16[576,640]{1,0:T(8,128)(2,1)S(1)}) custom-call(f32[1,576]{1,0:T(1,128)S(1)} %reshape.49.scale_ref, bf16[2048,512]{1,0:T(8,128)(2,1)S(1)} %bitcast.36, ...), custom_call_target="tpu_custom_call" | custom-call | flops 3623878656 | bytes 4194304 | tf_op jit(solution)/shard_map/keys/pallas_call | solution.py:395
  17.3 0.1 collective-permute-start.3
  17.3 1.6 %collective-permute-done.3.theirs_ref = bf16[4,4,72,128]{3,2,1,0:T(8,128)(2,1)S(1)} collective-permute-done((bf16[4,4,72,128]{3,2,1,0:T(8,128)(2,1)S(1)}, bf16[4,4,72,128]{3,2,1,0:T(8,128)(2,1)S(1)}, u32[]{:S(2)}, u32[]{:S(2)}) %collective-permute-start.3) | collective-permute-done | bytes 294944 | tf_op jit(solution)/shard_map/ppermute | solution.py:316
  18.9 1.8 %collective-permute-start.4 = (bf16[368,128]{1,0:T(8,128)(2,1)S(1)}, bf16[368,128]{1,0:T(8,128)(2,1)S(1)}, u32[]{:S(2)}, u32[]{:S(2)}) collective-permute-start(bf16[368,128]{1,0:T(8,128)(2,1)S(1)} %pad_maximum_fusion), channel_id=1, source_target_pairs={{0,3},{1,2},{2,1},{3,0},{4,7},{5,6},{6,5},{7,4},{8,11},{9,10},{10,... | collective-permute-start | bytes 282632 | tf_op jit(solution)/shard_map/ppermute | solution.py:313
  20.7 0.1 sums.1
  20.8 0.6 %collective-permute-start.5 = (bf16[368,128]{1,0:T(8,128)(2,1)S(1)}, bf16[368,128]{1,0:T(8,128)(2,1)S(1)}, u32[]{:S(2)}, u32[]{:S(2)}) collective-permute-start(bf16[368,128]{1,0:T(8,128)(2,1)S(1)} %get-tuple-element.49), channel_id=1, source_target_pairs={{0,1},{1,0},{2,3},{3,2},{4,5},{5,4},{6,7},{7,6},{8,9},{9,8},{10,11... | collective-permute-start | bytes 282632 | tf_op jit(solution)/shard_map/ppermute | solution.py:313
  21.4 1.2 %collective-permute-start.6 = (bf16[368,128]{1,0:T(8,128)(2,1)S(1)}, bf16[368,128]{1,0:T(8,128)(2,1)S(1)}, u32[]{:S(2)}, u32[]{:S(2)}) collective-permute-start(bf16[368,128]{1,0:T(8,128)(2,1)S(1)} %get-tuple-element.50), channel_id=1, source_target_pairs={{0,2},{1,3},{2,0},{3,1},{4,6},{5,7},{6,4},{7,5},{8,10},{9,11},{10,... | collective-permute-start | bytes 282632 | tf_op jit(solution)/shard_map/ppermute | solution.py:313
  22.6 3.0 %queries.2 = (bf16[2048,512]{1,0:T(8,128)(2,1)}, bf16[64,2048]{1,0:T(8,128)(2,1)}) custom-call(bf16[576,2048]{1,0:T(8,128)(2,1)S(1)} %get-tuple-element.53.ds_ref, bf16[576,640]{1,0:T(8,128)(2,1)S(1)} %get-tuple-element.54.keys_ref), custom_call_target="tpu_custom_call" | custom-call | flops 1132462080 | bytes 1572864 | tf_op jit(solution)/shard_map/queries/pallas_call | solution.py:434
  25.6 0.0 collective-permute-done.4
  25.7 0.6 %collective-permute-done.5 = bf16[368,128]{1,0:T(8,128)(2,1)S(1)} collective-permute-done((bf16[368,128]{1,0:T(8,128)(2,1)S(1)}, bf16[368,128]{1,0:T(8,128)(2,1)S(1)}, u32[]{:S(2)}, u32[]{:S(2)}) %collective-permute-start.5) | collective-permute-done | bytes 94240 | tf_op jit(solution)/shard_map/ppermute | solution.py:313
  26.2 0.4 %collective-permute-done.6 = bf16[368,128]{1,0:T(8,128)(2,1)S(1)} collective-permute-done((bf16[368,128]{1,0:T(8,128)(2,1)S(1)}, bf16[368,128]{1,0:T(8,128)(2,1)S(1)}, u32[]{:S(2)}, u32[]{:S(2)}) %collective-permute-start.6) | collective-permute-done | bytes 94240 | tf_op jit(solution)/shard_map/ppermute | solution.py:313
  26.8 0.0 copy-start.9
  26.8 3.7 %collective-permute-start.7 = (bf16[72,128]{1,0:T(8,128)(2,1)S(1)}, bf16[72,128]{1,0:T(8,128)(2,1)S(1)}, u32[]{:S(2)}, u32[]{:S(2)}) collective-permute-start(bf16[72,128]{1,0:T(8,128)(2,1)S(1)} %get-tuple-element.62), channel_id=1, source_target_pairs={{0,24},{4,28},{8,16},{12,20},{16,8},{20,12},{24,0},{28,4},{1,25},{... | collective-permute-start | bytes 55304 | tf_op jit(solution)/shard_map/ppermute | solution.py:316
  30.5 0.0 collective-permute-start.9
  30.5 0.8 %collective-permute-start.8 = (bf16[72,128]{1,0:T(8,128)(2,1)S(1)}, bf16[72,128]{1,0:T(8,128)(2,1)S(1)}, u32[]{:S(2)}, u32[]{:S(2)}) collective-permute-start(bf16[72,128]{1,0:T(8,128)(2,1)S(1)} %get-tuple-element.64), channel_id=1, source_target_pairs={{0,16},{4,20},{8,24},{12,28},{16,0},{20,4},{24,8},{28,12},{1,17},{... | collective-permute-start | bytes 55304 | tf_op jit(solution)/shard_map/ppermute | solution.py:316
  31.3 1.6 %queries.3 = (bf16[2048,512]{1,0:T(8,128)(2,1)}, bf16[64,2048]{1,0:T(8,128)(2,1)}) custom-call(bf16[576,2048]{1,0:T(8,128)(2,1)S(1)} %get-tuple-element.53.ds_ref, bf16[576,640]{1,0:T(8,128)(2,1)S(1)} %get-tuple-element.54.keys_ref, bf16[2048,512]{1,0:T(8,128)(2,1)} %get-tuple-element.55.refs_0_, ...), custom_call_target="tpu_custom_call", output_to_operand_aliasing={{0}: (2, {}), {1}: (3, {})} | custom-call | flops 377487360 | bytes 524288 | tf_op jit(solution)/shard_map/queries/pallas_call | solution.py:434
  32.9 0.0 collective-permute-done.7
  32.9 1.4 %collective-permute-done.9 = bf16[72,128]{1,0:T(8,128)(2,1)S(1)} collective-permute-done((bf16[72,128]{1,0:T(8,128)(2,1)S(1)}, bf16[72,128]{1,0:T(8,128)(2,1)S(1)}, u32[]{:S(2)}, u32[]{:S(2)}) %collective-permute-start.9) | collective-permute-done | bytes 18464 | tf_op jit(solution)/shard_map/ppermute | solution.py:316
  34.3 0.9 %collective-permute-done.8 = bf16[72,128]{1,0:T(8,128)(2,1)S(1)} collective-permute-done((bf16[72,128]{1,0:T(8,128)(2,1)S(1)}, bf16[72,128]{1,0:T(8,128)(2,1)S(1)}, u32[]{:S(2)}, u32[]{:S(2)}) %collective-permute-start.8) | collective-permute-done | bytes 18464 | tf_op jit(solution)/shard_map/ppermute | solution.py:316
  35.2 0.6 %fusion.5 = f32[128,72]{0,1:T(8,128)} fusion(f32[4,72,128]{2,1,0:T(8,128)S(1)} %get-tuple-element.61, bf16[72,128]{1,0:T(8,128)(2,1)S(1)} %collective-permute-done.9, bf16[72,128]{1,0:T(8,128)(2,1)S(1)} %collective-permute-done.8, bf16[72,128]{1,0:T(8,128)(2,1)S(1)} %collective-permute-done.7), kind=kLoop, calls=%fused_computation.12 | loop fusion | flops 55296 | bytes 129024 | tf_op jit(solution)/shard_map/transpose | solution.py:489
  (31 shorter events, 0.2 us)
Async XLA Ops:
  0.6 3.1 %copy-start.3 = (bf16[128,576]{0,1:T(8,128)(2,1)S(1)}, bf16[128,576]{0,1:T(8,128)(2,1)}, u32[]{:S(2)}) copy-start(bf16[128,576]{0,1:T(8,128)(2,1)} %param.9) | copy-start | bytes 442372
  0.6 4.8 %copy-start.8 = (f32[576]{0:T(1024)S(1)}, f32[576]{0:T(1024)}, u32[]{:S(2)}) copy-start(f32[576]{0:T(1024)} %param.10) | copy-start | bytes 6916
  0.7 4.8 %copy-start = (bf16[64,32,512]{2,1,0:T(8,128)(2,1)S(1)}, bf16[64,32,512]{2,1,0:T(8,128)(2,1)}, u32[]{:S(2)}) copy-start(bf16[64,32,512]{2,1,0:T(8,128)(2,1)} %param.12) | copy-start | bytes 6291460
  0.7 4.8 %copy-start.1 = (bf16[64,32,512]{2,1,0:T(8,128)(2,1)S(1)}, bf16[64,32,512]{2,1,0:T(8,128)(2,1)}, u32[]{:S(2)}) copy-start(bf16[64,32,512]{2,1,0:T(8,128)(2,1)} %param.14) | copy-start | bytes 6291460
  0.7 4.8 %copy-start.2 = (bf16[64,2048]{1,0:T(8,128)(2,1)S(1)}, bf16[64,2048]{1,0:T(8,128)(2,1)}, u32[]{:S(2)}) copy-start(bf16[64,2048]{1,0:T(8,128)(2,1)} %qrope_v.1) | copy-start | bytes 786436
  0.7 4.8 %copy-start.4 = (bf16[64,576]{1,0:T(8,128)(2,1)S(1)}, bf16[64,576]{1,0:T(8,128)(2,1)}, u32[]{:S(2)}) copy-start(bf16[64,576]{1,0:T(8,128)(2,1)} %span_ref.1) | copy-start | bytes 221188
  0.7 4.8 %copy-start.5 = (s32[16]{0:T(128)S(1)}, s32[16]{0:T(128)}, u32[]{:S(2)}) copy-start(s32[16]{0:T(128)} %length_s.1) | copy-start | bytes 196
  0.7 4.8 %copy-start.6 = (s32[8]{0:T(128)S(1)}, s32[8]{0:T(128)}, u32[]{:S(2)}) copy-start(s32[8]{0:T(128)} %response_s.1) | copy-start | bytes 100
  0.7 4.8 %copy-start.7 = (s32[8]{0:T(128)S(1)}, s32[8]{0:T(128)}, u32[]{:S(2)}) copy-start(s32[8]{0:T(128)} %index_s.1) | copy-start | bytes 100
  0.7 7.7 %collective-permute-start = (bf16[576,128]{1,0:T(8,128)(2,1)}, bf16[576,128]{1,0:T(8,128)(2,1)S(1)}, u32[]{:S(2)}, u32[]{:S(2)}) collective-permute-start(bf16[576,128]{1,0:T(8,128)(2,1)} %bitcast.40), channel_id=1, source_target_pairs={{0,1},{1,0},{2,3},{3,2},{4,6},{5,7},{6,4},{7,5},{8,9},{9,8},{10,11... | collective-permute-start | bytes 442376 | tf_op jit(solution)/shard_map/ppermute | solution.py:324
  3.8 7.9 %collective-permute-start.2 = (bf16[576,128]{1,0:T(8,128)(2,1)S(1)}, bf16[576,128]{1,0:T(8,128)(2,1)S(1)}, u32[]{:S(2)}, u32[]{:S(2)}) collective-permute-start(bf16[576,128]{1,0:T(8,128)(2,1)S(1)} %bitcast.41), channel_id=1, source_target_pairs={{0,3},{1,2},{2,1},{3,0},{4,7},{5,6},{6,5},{7,4},{8,11},{9,10},{10,... | collective-permute-start | bytes 442376 | tf_op jit(solution)/shard_map/ppermute | solution.py:313
  8.4 3.3 %collective-permute-start.1 = (bf16[576,128]{1,0:T(8,128)(2,1)S(1)}, bf16[576,128]{1,0:T(8,128)(2,1)S(1)}, u32[]{:S(2)}, u32[]{:S(2)}) collective-permute-start(bf16[576,128]{1,0:T(8,128)(2,1)S(1)} %collective-permute-done.refs_0_), channel_id=1, source_target_pairs={{0,4},{4,0},{8,12},{12,8},{16,20},{20,16},{24,28},{28,24},{1,5},{5... | collective-permute-start | bytes 442376 | tf_op jit(solution)/shard_map/ppermute | solution.py:316
  17.3 1.6 %collective-permute-start.3 = (bf16[4,4,72,128]{3,2,1,0:T(8,128)(2,1)S(1)}, bf16[4,4,72,128]{3,2,1,0:T(8,128)(2,1)S(1)}, u32[]{:S(2)}, u32[]{:S(2)}) collective-permute-start(bf16[4,4,72,128]{3,2,1,0:T(8,128)(2,1)S(1)} %get-tuple-element.46), channel_id=1, source_target_pairs={{0,4},{4,0},{8,12},{12,8},{16,20},{20,16},{24,28},{28,24},{1,5},{5... | collective-permute-start | bytes 884744 | tf_op jit(solution)/shard_map/ppermute | solution.py:316
  18.9 6.7 %collective-permute-start.4 = (bf16[368,128]{1,0:T(8,128)(2,1)S(1)}, bf16[368,128]{1,0:T(8,128)(2,1)S(1)}, u32[]{:S(2)}, u32[]{:S(2)}) collective-permute-start(bf16[368,128]{1,0:T(8,128)(2,1)S(1)} %pad_maximum_fusion), channel_id=1, source_target_pairs={{0,3},{1,2},{2,1},{3,0},{4,7},{5,6},{6,5},{7,4},{8,11},{9,10},{10,... | collective-permute-start | bytes 282632 | tf_op jit(solution)/shard_map/ppermute | solution.py:313
  20.8 5.4 %collective-permute-start.5 = (bf16[368,128]{1,0:T(8,128)(2,1)S(1)}, bf16[368,128]{1,0:T(8,128)(2,1)S(1)}, u32[]{:S(2)}, u32[]{:S(2)}) collective-permute-start(bf16[368,128]{1,0:T(8,128)(2,1)S(1)} %get-tuple-element.49), channel_id=1, source_target_pairs={{0,1},{1,0},{2,3},{3,2},{4,5},{5,4},{6,7},{7,6},{8,9},{9,8},{10,11... | collective-permute-start | bytes 282632 | tf_op jit(solution)/shard_map/ppermute | solution.py:313
  21.4 5.3 %collective-permute-start.6 = (bf16[368,128]{1,0:T(8,128)(2,1)S(1)}, bf16[368,128]{1,0:T(8,128)(2,1)S(1)}, u32[]{:S(2)}, u32[]{:S(2)}) collective-permute-start(bf16[368,128]{1,0:T(8,128)(2,1)S(1)} %get-tuple-element.50), channel_id=1, source_target_pairs={{0,2},{1,3},{2,0},{3,1},{4,6},{5,7},{6,4},{7,5},{8,10},{9,11},{10,... | collective-permute-start | bytes 282632 | tf_op jit(solution)/shard_map/ppermute | solution.py:313
  26.8 6.1 %copy-start.9 = (f32[16,576]{1,0:T(8,128)}, f32[16,576]{1,0:T(8,128)S(1)}, u32[]{:S(2)}) copy-start(f32[16,576]{1,0:T(8,128)S(1)} %constant_dynamic-update-slice_fusion) | copy-start | bytes 110596
  26.8 6.0 %collective-permute-start.7 = (bf16[72,128]{1,0:T(8,128)(2,1)S(1)}, bf16[72,128]{1,0:T(8,128)(2,1)S(1)}, u32[]{:S(2)}, u32[]{:S(2)}) collective-permute-start(bf16[72,128]{1,0:T(8,128)(2,1)S(1)} %get-tuple-element.62), channel_id=1, source_target_pairs={{0,24},{4,28},{8,16},{12,20},{16,8},{20,12},{24,0},{28,4},{1,25},{... | collective-permute-start | bytes 55304 | tf_op jit(solution)/shard_map/ppermute | solution.py:316
  30.5 3.8 %collective-permute-start.9 = (bf16[72,128]{1,0:T(8,128)(2,1)S(1)}, bf16[72,128]{1,0:T(8,128)(2,1)S(1)}, u32[]{:S(2)}, u32[]{:S(2)}) collective-permute-start(bf16[72,128]{1,0:T(8,128)(2,1)S(1)} %get-tuple-element.63), channel_id=1, source_target_pairs={{0,8},{4,12},{8,0},{12,4},{16,24},{20,28},{24,16},{28,20},{1,9},{5... | collective-permute-start | bytes 55304 | tf_op jit(solution)/shard_map/ppermute | solution.py:316
  30.5 4.7 %collective-permute-start.8 = (bf16[72,128]{1,0:T(8,128)(2,1)S(1)}, bf16[72,128]{1,0:T(8,128)(2,1)S(1)}, u32[]{:S(2)}, u32[]{:S(2)}) collective-permute-start(bf16[72,128]{1,0:T(8,128)(2,1)S(1)} %get-tuple-element.64), channel_id=1, source_target_pairs={{0,16},{4,20},{8,24},{12,28},{16,0},{20,4},{24,8},{28,12},{1,17},{... | collective-permute-start | bytes 55304 | tf_op jit(solution)/shard_map/ppermute | solution.py:316

commit v5 on v4

--- a/solution.py
+++ b/solution.py
@@ -147,8 +147,8 @@
     stat_ref,
     *refs,
 ):
-    shard_refs = refs[:-7]
-    mine_ref, theirs_ref, span_out, ds_ref, keys_ref, p_scr, keys_c = refs[-7:]
+    shard_refs = refs[:-8]
+    mine_ref, theirs_ref, far_ref, span_out, ds_ref, keys_ref, p_scr, keys_c = refs[-8:]
     rows, latent = q_ref.shape
     full = scale_ref.shape[1]
     shard = shard_refs[0].shape[1]
@@ -230,7 +230,10 @@
             else:
                 d = 2 * (slot - pairs) - my_resp % 2
             mine_ref[d, z ^ my_pair] = mine
-            theirs_ref[d, z ^ my_pair] = theirs
+            if slot == n_seq - 1:
+                far_ref[z ^ my_pair] = theirs
+            else:
+                theirs_ref[d, z ^ my_pair] = theirs
 
 
 def sum_kernel(mine_ref, theirs_ref, span_ref, own_ref, *pay_refs):
@@ -246,18 +249,18 @@
             pay_refs[d - 1][pl.ds(pairs * cols, span_ref.shape[1]), :] = span_ref[d]
 
 
-def query_kernel(heads, first, count, ds_ref, keys_ref, *refs):
-    out_hbm, rope_hbm, out_v, rope_v, rope_scr, out_sems, rope_sems = refs[-7:]
+def query_kernel(
+    heads, ds_ref, keys_ref, out_hbm, rope_hbm, out_v, rope_v, rope_scr, out_sems, rope_sems
+):
     latent = out_v.shape[1]
     rope = (keys_ref.shape[1] - latent) // 2
     step = 16 * heads
     low = low_half((16, 2 * rope), rope)
     copies = []
-    for i in range(count):
-        at = pl.ds((first + i) * step, step)
-        here = pl.ds(i * step, step)
-        out_v[here, :] = dot(ds_ref[:, at], keys_ref[:, :latent], TN).astype(BF16)
-        copies.append(pltpu.make_async_copy(out_v.at[here], out_hbm.at[at], out_sems.at[i]))
+    for i in range(out_v.shape[0] // step):
+        at = pl.ds(i * step, step)
+        out_v[at, :] = dot(ds_ref[:, at], keys_ref[:, :latent], TN).astype(BF16)
+        copies.append(pltpu.make_async_copy(out_v.at[at], out_hbm.at[at], out_sems.at[i]))
         copies[-1].start()
         rope_scr[...] = dot(ds_ref[:, at], keys_ref[:, latent:], TN)
         for j in range(heads // 2):
@@ -269,7 +272,7 @@
         copies.append(
             pltpu.make_async_copy(
                 rope_v.at[pl.ds(i * 16, 16)],
-                rope_hbm.at[pl.ds((first + i) * 16, 16)],
+                rope_hbm.at[pl.ds(i * 16, 16)],
                 rope_sems.at[i],
             )
         )
@@ -392,17 +395,18 @@
         name="middle",
     )(scale_row, q_rows, up_rows, q_turned, stats, *fetched)
 
-    mine, theirs, span, dscore, keys_all = pl.pallas_call(
+    mine, theirs, far, span, dscore, keys_all = pl.pallas_call(
         functools.partial(keys_kernel, n_resp, n_seq),
         out_shape=(
             shape((n_seq, pairs, cols, shard)),
-            shape((n_seq, pairs, cols, shard)),
+            shape((n_seq - 1, pairs, cols, shard)),
+            shape((pairs, cols, shard)),
             shape((n_seq, span_rows, 2 * rope)),
             shape((keys, rows)),
             shape((keys, width)),
         ),
         in_specs=[vmem] * (12 + len(swapped)),
-        out_specs=(vmem,) * 5,
+        out_specs=(vmem,) * 6,
         scratch_shapes=[
             pltpu.VMEM((keys, rows), BF16),
             pltpu.VMEM((shard * (len(swapped) + 1), width), BF16),
@@ -430,31 +434,29 @@
 
     steps = tok // 16
 
-    def queries(first, count, dscore, keys_all, before):
+    def queries(dscore, keys_all):
         return pl.pallas_call(
-            functools.partial(query_kernel, heads, first, count),
+            functools.partial(query_kernel, heads),
             out_shape=(shape((rows, latent)), shape((tok, heads * rope))),
-            in_specs=[vmem] * 2 + [hbm] * len(before),
+            in_specs=[vmem] * 2,
             out_specs=(hbm,) * 2,
             scratch_shapes=[
-                pltpu.VMEM((count * 16 * heads, latent), BF16),
-                pltpu.VMEM((count * 16, heads * rope), BF16),
+                pltpu.VMEM((rows, latent), BF16),
+                pltpu.VMEM((tok, heads * rope), BF16),
                 pltpu.VMEM((16 * heads, 2 * rope), F32),
-                pltpu.SemaphoreType.DMA((count,)),
-                pltpu.SemaphoreType.DMA((count,)),
+                pltpu.SemaphoreType.DMA((steps,)),
+                pltpu.SemaphoreType.DMA((steps,)),
             ],
-            input_output_aliases={2: 0, 3: 1} if before else {},
             compiler_params=pltpu.CompilerParams(vmem_limit_bytes=16 * MIB),
             cost_estimate=pl.CostEstimate(
-                flops=2 * keys * count * 16 * heads * width,
-                bytes_accessed=count * 32 * heads * latent,
-                transcendentals=0,
+                flops=2 * keys * rows * width, bytes_accessed=2 * rows * width, transcendentals=0
             ),
             name="queries",
-        )(dscore, keys_all, *before)
-
+        )(dscore, keys_all)
+
+    far = over_resp(far, 1)
     theirs = over_resp(theirs, 1)
-    farthest = mine[-1].astype(F32) + theirs[-1].astype(F32)
+    farthest = mine[-1].astype(F32) + far.astype(F32)
     farthest = jnp.concatenate(
         [farthest.astype(BF16).reshape(-1, 2 * rope), span[-1]], axis=0
     )
@@ -472,17 +474,14 @@
         name="sums",
     )(mine, theirs, span)
     moved += [over_seq(pay, d + 1) for d, pay in enumerate(pays)]
-    half = (3 * steps + 3) // 4
-    partly = queries(0, half, dscore, keys_all, ())
+    grad_latent, grad_rope = queries(dscore, keys_all)
     split = pairs * cols
     own = span[0].astype(F32)
     for x in moved:
         block = block + x[:split].reshape(pairs, cols, shard).astype(F32)
         own = own + x[split:].astype(F32)
     block_half = block.astype(BF16)
-    block_half, dscore, keys_all = lax.optimization_barrier((block_half, dscore, keys_all))
     arrived = [over_resp(block_half[d], 2 * d) for d in range(pairs - 1, 0, -1)]
-    grad_latent, grad_rope = queries(half, steps - half, dscore, keys_all, partly)
     total = block[0]
     for x in arrived:
         total = total + x.astype(F32)

time: 35.9 us -> 35.6 us (level)
  Pallas kernels: 14.8 us -> 13.9 us
  starting transfers between devices: 12.9 us -> 13.4 us
    pallas_call x2 -> x1, Pallas kernels: 4.57 us -> 3.73 us  [queries(): pl.pallas_call(functools.partial(query_kernel, heads), out_shape=(shape((...]
    ppermute x4, waiting for transfers between devices: 2.56 us -> 1.81 us  [over_seq(): return lax.ppermute(x, 'seq', [(i, i ^ d) for i in range(n_seq)])]
    ppermute x5 -> x6, waiting for transfers between devices: 3.84 us -> 4.55 us  [over_resp(): return lax.ppermute(x, 'resp', [(i, i ^ d) for i in range(n_resp)])]
    ppermute x5 -> x6, starting transfers between devices: 4.59 us -> 5.08 us  [over_resp(): return lax.ppermute(x, 'resp', [(i, i ^ d) for i in range(n_resp)])]
  transfers between devices with their start and end apart: 10 -> 11, of which waited for: 6 -> 6; matrix products, arithmetic and copies ran while one was open for 0% -> 0% of each run, Pallas kernels for 26% -> 24%
where the time goes in v5:
time: 35.6 us; the launch traced here: 35.4 us
  Pallas kernels  13.9 us (39%)
  starting transfers between devices  13.4 us (38%)
  waiting for transfers between devices  6.36 us (18%)
  between operations  0.94 us (3%)
  other arithmetic  0.72 us (2%)
    pallas_call x1, Pallas kernels, on_device(): pl.pallas_call(functools.partial(keys_kernel, n_resp, n_seq), out_shape=(...  5.58 us
    ppermute x4, starting transfers between devices, over_seq(): return lax.ppermute(x, 'seq', [(i, i ^ d) for i in range(n_seq)])  5.28 us
    ppermute x6, starting transfers between devices, over_resp(): return lax.ppermute(x, 'resp', [(i, i ^ d) for i in range(n_resp)])  5.08 us
    ppermute x6, waiting for transfers between devices, over_resp(): return lax.ppermute(x, 'resp', [(i, i ^ d) for i in range(n_resp)])  4.55 us
    pallas_call x1, Pallas kernels, queries(): pl.pallas_call(functools.partial(query_kernel, heads), out_shape=(shape((...  3.73 us
    ppermute x1, starting transfers between devices, by_core(): return lax.ppermute(x, ('resp', 'seq'), moves)  3 us
    pallas_call x1, Pallas kernels, on_device(): pl.pallas_call(functools.partial(early_kernel, heads), out_shape=(shape((...  2.9 us
    ppermute x4, waiting for transfers between devices, over_seq(): return lax.ppermute(x, 'seq', [(i, i ^ d) for i in range(n_seq)])  1.81 us
  transfers between devices with their start and end apart: 11, of which 6 were waited for; matrix products, arithmetic and copies ran while one was open for 0% of the time, Pallas kernels for 24%

profile of v5, /device:TPU:0, one launch (start us, length us, event | category | flops | bytes accessed | tf_op | source)
XLA Modules:
  0.0 35.4 jit_solution(8049248901674681355)
XLA Ops:
  0.6 0.0 copy-start.3
  0.6 0.0 copy-start.8
  0.7 3.0 %collective-permute-start = (bf16[576,128]{1,0:T(8,128)(2,1)}, bf16[576,128]{1,0:T(8,128)(2,1)S(1)}, u32[]{:S(2)}, u32[]{:S(2)}) collective-permute-start(bf16[576,128]{1,0:T(8,128)(2,1)} %bitcast.43), channel_id=1, source_target_pairs={{0,1},{1,0},{2,3},{3,2},{4,6},{5,7},{6,4},{7,5},{8,9},{9,8},{10,11... | collective-permute-start | bytes 442376 | tf_op jit(solution)/shard_map/ppermute | solution.py:327
  3.8 0.0 copy-done.3
  3.8 1.7 %collective-permute-start.2 = (bf16[576,128]{1,0:T(8,128)(2,1)S(1)}, bf16[576,128]{1,0:T(8,128)(2,1)S(1)}, u32[]{:S(2)}, u32[]{:S(2)}) collective-permute-start(bf16[576,128]{1,0:T(8,128)(2,1)S(1)} %bitcast.44), channel_id=1, source_target_pairs={{0,3},{1,2},{2,1},{3,0},{4,7},{5,6},{6,5},{7,4},{8,11},{9,10},{10,... | collective-permute-start | bytes 442376 | tf_op jit(solution)/shard_map/ppermute | solution.py:316
  5.5 2.9 %early.1 = (bf16[2048,128]{1,0:T(8,128)(2,1)S(1)}, f32[192,2048]{1,0:T(8,128)S(1)}, f32[192,2048]{1,0:T(8,128)S(1)}, f32[8,2048]{1,0:T(8,128)S(1)}, bf16[192,640]{1,0:T(8,128)(2,1)S(1)}) custom-call(s32[16]{0:T(128)S(1)} %copy-done.5, s32[8]{0:T(128)S(1)} %copy-done.6, s32[8]{0:T(128)S(1)} %copy-done.7, f32[64,2048]{1,0:T(8,128)S(1)} %mask.1.mask_ref, ...), custom_call_target="tpu_custom_call" | custom-call | flops 805306368 | bytes 4194304 | tf_op jit(solution)/shard_map/early/pallas_call | solution.py:348
  8.4 0.0 collective-permute-done.refs_0_
  8.4 0.1 collective-permute-start.1
  8.5 1.6 %middle.1 = (f32[128,2048]{1,0:T(8,128)S(1)}, f32[128,2048]{1,0:T(8,128)S(1)}, f32[8,2048]{1,0:T(8,128)S(1)}, bf16[128,640]{1,0:T(8,128)(2,1)S(1)}) custom-call(f32[1,576]{1,0:T(1,128)S(1)} %reshape.47.scale_ref, bf16[2048,512]{1,0:T(8,128)(2,1)S(1)} %bitcast.38, bf16[2048,512]{1,0:T(8,128)(2,1)S(1)} %bitcast.41, ...), custom_call_target="tpu_custom_call" | custom-call | flops 536870912 | bytes 4194304 | tf_op jit(solution)/shard_map/middle/pallas_call | solution.py:381
  10.1 1.5 %collective-permute-done.2.refs_1_ = bf16[576,128]{1,0:T(8,128)(2,1)S(1)} collective-permute-done((bf16[576,128]{1,0:T(8,128)(2,1)S(1)}, bf16[576,128]{1,0:T(8,128)(2,1)S(1)}, u32[]{:S(2)}, u32[]{:S(2)}) %collective-permute-start.2) | collective-permute-done | bytes 147488 | tf_op jit(solution)/shard_map/ppermute | solution.py:316
  11.7 0.0 collective-permute-done.1.refs_0_
  11.7 5.6 %keys.1 = (bf16[4,4,72,128]{3,2,1,0:T(8,128)(2,1)S(1)}, bf16[3,4,72,128]{3,2,1,0:T(8,128)(2,1)S(1)}, bf16[4,72,128]{2,1,0:T(8,128)(2,1)S(1)}, bf16[4,80,128]{2,1...) custom-call(f32[1,576]{1,0:T(1,128)S(1)} %reshape.47.scale_ref, ...), custom_call_target="tpu_custom_call" | custom-call | flops 3623878656 | bytes 4194304 | tf_op jit(solution)/shard_map/keys/pallas_call | solution.py:398
  17.3 0.1 collective-permute-start.4
  17.3 0.5 %collective-permute-start.3 = (bf16[3,4,72,128]{3,2,1,0:T(8,128)(2,1)S(1)}, bf16[3,4,72,128]{3,2,1,0:T(8,128)(2,1)S(1)}, u32[]{:S(2)}, u32[]{:S(2)}) collective-permute-start(bf16[3,4,72,128]{3,2,1,0:T(8,128)(2,1)S(1)} %get-tuple-element.46), channel_id=1, source_target_pairs={{0,4},{4,0},{8,12},{12,8},{16,20},{20,16},{24,28},{28,24},{1,5},{5... | collective-permute-start | bytes 663560 | tf_op jit(solution)/shard_map/ppermute | solution.py:319
  17.8 0.8 %collective-permute-done.4 = bf16[4,72,128]{2,1,0:T(8,128)(2,1)S(1)} collective-permute-done((bf16[4,72,128]{2,1,0:T(8,128)(2,1)S(1)}, bf16[4,72,128]{2,1,0:T(8,128)(2,1)S(1)}, u32[]{:S(2)}, u32[]{:S(2)}) %collective-permute-start.4) | collective-permute-done | bytes 73760 | tf_op jit(solution)/shard_map/ppermute | solution.py:319
  18.6 1.8 %collective-permute-start.5 = (bf16[368,128]{1,0:T(8,128)(2,1)S(1)}, bf16[368,128]{1,0:T(8,128)(2,1)S(1)}, u32[]{:S(2)}, u32[]{:S(2)}) collective-permute-start(bf16[368,128]{1,0:T(8,128)(2,1)S(1)} %pad_maximum_fusion), channel_id=1, source_target_pairs={{0,3},{1,2},{2,1},{3,0},{4,7},{5,6},{6,5},{7,4},{8,11},{9,10},{10,... | collective-permute-start | bytes 282632 | tf_op jit(solution)/shard_map/ppermute | solution.py:316
  20.4 0.0 collective-permute-done.3.theirs_ref
  20.4 0.1 sums.1
  20.5 0.6 %collective-permute-start.6 = (bf16[368,128]{1,0:T(8,128)(2,1)S(1)}, bf16[368,128]{1,0:T(8,128)(2,1)S(1)}, u32[]{:S(2)}, u32[]{:S(2)}) collective-permute-start(bf16[368,128]{1,0:T(8,128)(2,1)S(1)} %get-tuple-element.50), channel_id=1, source_target_pairs={{0,1},{1,0},{2,3},{3,2},{4,5},{5,4},{6,7},{7,6},{8,9},{9,8},{10,11... | collective-permute-start | bytes 282632 | tf_op jit(solution)/shard_map/ppermute | solution.py:316
  21.1 1.2 %collective-permute-start.7 = (bf16[368,128]{1,0:T(8,128)(2,1)S(1)}, bf16[368,128]{1,0:T(8,128)(2,1)S(1)}, u32[]{:S(2)}, u32[]{:S(2)}) collective-permute-start(bf16[368,128]{1,0:T(8,128)(2,1)S(1)} %get-tuple-element.51), channel_id=1, source_target_pairs={{0,2},{1,3},{2,0},{3,1},{4,6},{5,7},{6,4},{7,5},{8,10},{9,11},{10,... | collective-permute-start | bytes 282632 | tf_op jit(solution)/shard_map/ppermute | solution.py:316
  22.3 3.7 %queries.1 = (bf16[2048,512]{1,0:T(8,128)(2,1)}, bf16[64,2048]{1,0:T(8,128)(2,1)}) custom-call(bf16[576,2048]{1,0:T(8,128)(2,1)S(1)} %get-tuple-element.41.ds_ref, bf16[576,640]{1,0:T(8,128)(2,1)S(1)} %get-tuple-element.42.keys_ref), custom_call_target="tpu_custom_call" | custom-call | flops 1509949440 | bytes 2621440 | tf_op jit(solution)/shard_map/queries/pallas_call | solution.py:438
  26.0 0.0 collective-permute-done.5
  26.1 0.0 collective-permute-done.6
  26.1 0.3 collective-permute-done.7
  26.5 3.7 %collective-permute-start.8 = (bf16[72,128]{1,0:T(8,128)(2,1)S(1)}, bf16[72,128]{1,0:T(8,128)(2,1)S(1)}, u32[]{:S(2)}, u32[]{:S(2)}) collective-permute-start(bf16[72,128]{1,0:T(8,128)(2,1)S(1)} %get-tuple-element.54), channel_id=1, source_target_pairs={{0,24},{4,28},{8,16},{12,20},{16,8},{20,12},{24,0},{28,4},{1,25},{... | collective-permute-start | bytes 55304 | tf_op jit(solution)/shard_map/ppermute | solution.py:319
  30.1 0.0 collective-permute-start.10
  30.1 0.8 %collective-permute-start.9 = (bf16[72,128]{1,0:T(8,128)(2,1)S(1)}, bf16[72,128]{1,0:T(8,128)(2,1)S(1)}, u32[]{:S(2)}, u32[]{:S(2)}) collective-permute-start(bf16[72,128]{1,0:T(8,128)(2,1)S(1)} %get-tuple-element.56), channel_id=1, source_target_pairs={{0,16},{4,20},{8,24},{12,28},{16,0},{20,4},{24,8},{28,12},{1,17},{... | collective-permute-start | bytes 55304 | tf_op jit(solution)/shard_map/ppermute | solution.py:319
  31.0 0.0 copy-start.9
  31.0 1.1 %collective-permute-done.8 = bf16[72,128]{1,0:T(8,128)(2,1)S(1)} collective-permute-done((bf16[72,128]{1,0:T(8,128)(2,1)S(1)}, bf16[72,128]{1,0:T(8,128)(2,1)S(1)}, u32[]{:S(2)}, u32[]{:S(2)}) %collective-permute-start.8) | collective-permute-done | bytes 18464 | tf_op jit(solution)/shard_map/ppermute | solution.py:319
  32.1 1.8 %collective-permute-done.10 = bf16[72,128]{1,0:T(8,128)(2,1)S(1)} collective-permute-done((bf16[72,128]{1,0:T(8,128)(2,1)S(1)}, bf16[72,128]{1,0:T(8,128)(2,1)S(1)}, u32[]{:S(2)}, u32[]{:S(2)}) %collective-permute-start.10) | collective-permute-done | bytes 18464 | tf_op jit(solution)/shard_map/ppermute | solution.py:319
  33.9 0.9 %collective-permute-done.9 = bf16[72,128]{1,0:T(8,128)(2,1)S(1)} collective-permute-done((bf16[72,128]{1,0:T(8,128)(2,1)S(1)}, bf16[72,128]{1,0:T(8,128)(2,1)S(1)}, u32[]{:S(2)}, u32[]{:S(2)}) %collective-permute-start.9) | collective-permute-done | bytes 18464 | tf_op jit(solution)/shard_map/ppermute | solution.py:319
  34.8 0.6 %fusion.6 = f32[128,72]{0,1:T(8,128)} fusion(f32[4,72,128]{2,1,0:T(8,128)S(1)} %get-tuple-element.53, bf16[72,128]{1,0:T(8,128)(2,1)S(1)} %collective-permute-done.10, bf16[72,128]{1,0:T(8,128)(2,1)S(1)} %collective-permute-done.9, bf16[72,128]{1,0:T(8,128)(2,1)S(1)} %collective-permute-done.8), kind=kLoop, calls=%fused_computation.13 | loop fusion | flops 55296 | bytes 129024 | tf_op jit(solution)/shard_map/transpose | solution.py:488
  (32 shorter events, 0.2 us)
Async XLA Ops:
  0.6 3.1 %copy-start.3 = (bf16[128,576]{0,1:T(8,128)(2,1)S(1)}, bf16[128,576]{0,1:T(8,128)(2,1)}, u32[]{:S(2)}) copy-start(bf16[128,576]{0,1:T(8,128)(2,1)} %param.9) | copy-start | bytes 442372
  0.6 4.8 %copy-start.8 = (f32[576]{0:T(1024)S(1)}, f32[576]{0:T(1024)}, u32[]{:S(2)}) copy-start(f32[576]{0:T(1024)} %param.10) | copy-start | bytes 6916
  0.7 4.8 %copy-start = (bf16[64,32,512]{2,1,0:T(8,128)(2,1)S(1)}, bf16[64,32,512]{2,1,0:T(8,128)(2,1)}, u32[]{:S(2)}) copy-start(bf16[64,32,512]{2,1,0:T(8,128)(2,1)} %param.12) | copy-start | bytes 6291460
  0.7 4.8 %copy-start.1 = (bf16[64,32,512]{2,1,0:T(8,128)(2,1)S(1)}, bf16[64,32,512]{2,1,0:T(8,128)(2,1)}, u32[]{:S(2)}) copy-start(bf16[64,32,512]{2,1,0:T(8,128)(2,1)} %param.14) | copy-start | bytes 6291460
  0.7 4.8 %copy-start.2 = (bf16[64,2048]{1,0:T(8,128)(2,1)S(1)}, bf16[64,2048]{1,0:T(8,128)(2,1)}, u32[]{:S(2)}) copy-start(bf16[64,2048]{1,0:T(8,128)(2,1)} %qrope_v.1) | copy-start | bytes 786436
  0.7 4.8 %copy-start.4 = (bf16[64,576]{1,0:T(8,128)(2,1)S(1)}, bf16[64,576]{1,0:T(8,128)(2,1)}, u32[]{:S(2)}) copy-start(bf16[64,576]{1,0:T(8,128)(2,1)} %span_ref.1) | copy-start | bytes 221188
  0.7 4.8 %copy-start.5 = (s32[16]{0:T(128)S(1)}, s32[16]{0:T(128)}, u32[]{:S(2)}) copy-start(s32[16]{0:T(128)} %length_s.1) | copy-start | bytes 196
  0.7 4.8 %copy-start.6 = (s32[8]{0:T(128)S(1)}, s32[8]{0:T(128)}, u32[]{:S(2)}) copy-start(s32[8]{0:T(128)} %response_s.1) | copy-start | bytes 100
  0.7 4.8 %copy-start.7 = (s32[8]{0:T(128)S(1)}, s32[8]{0:T(128)}, u32[]{:S(2)}) copy-start(s32[8]{0:T(128)} %index_s.1) | copy-start | bytes 100
  0.7 7.7 %collective-permute-start = (bf16[576,128]{1,0:T(8,128)(2,1)}, bf16[576,128]{1,0:T(8,128)(2,1)S(1)}, u32[]{:S(2)}, u32[]{:S(2)}) collective-permute-start(bf16[576,128]{1,0:T(8,128)(2,1)} %bitcast.43), channel_id=1, source_target_pairs={{0,1},{1,0},{2,3},{3,2},{4,6},{5,7},{6,4},{7,5},{8,9},{9,8},{10,11... | collective-permute-start | bytes 442376 | tf_op jit(solution)/shard_map/ppermute | solution.py:327
  3.8 7.9 %collective-permute-start.2 = (bf16[576,128]{1,0:T(8,128)(2,1)S(1)}, bf16[576,128]{1,0:T(8,128)(2,1)S(1)}, u32[]{:S(2)}, u32[]{:S(2)}) collective-permute-start(bf16[576,128]{1,0:T(8,128)(2,1)S(1)} %bitcast.44), channel_id=1, source_target_pairs={{0,3},{1,2},{2,1},{3,0},{4,7},{5,6},{6,5},{7,4},{8,11},{9,10},{10,... | collective-permute-start | bytes 442376 | tf_op jit(solution)/shard_map/ppermute | solution.py:316
  8.4 3.2 %collective-permute-start.1 = (bf16[576,128]{1,0:T(8,128)(2,1)S(1)}, bf16[576,128]{1,0:T(8,128)(2,1)S(1)}, u32[]{:S(2)}, u32[]{:S(2)}) collective-permute-start(bf16[576,128]{1,0:T(8,128)(2,1)S(1)} %collective-permute-done.refs_0_), channel_id=1, source_target_pairs={{0,4},{4,0},{8,12},{12,8},{16,20},{20,16},{24,28},{28,24},{1,5},{5... | collective-permute-start | bytes 442376 | tf_op jit(solution)/shard_map/ppermute | solution.py:319
  17.3 1.3 %collective-permute-start.4 = (bf16[4,72,128]{2,1,0:T(8,128)(2,1)S(1)}, bf16[4,72,128]{2,1,0:T(8,128)(2,1)S(1)}, u32[]{:S(2)}, u32[]{:S(2)}) collective-permute-start(bf16[4,72,128]{2,1,0:T(8,128)(2,1)S(1)} %get-tuple-element.49), channel_id=1, source_target_pairs={{0,4},{4,0},{8,12},{12,8},{16,20},{20,16},{24,28},{28,24},{1,5},{5... | collective-permute-start | bytes 221192 | tf_op jit(solution)/shard_map/ppermute | solution.py:319
  17.3 3.1 %collective-permute-start.3 = (bf16[3,4,72,128]{3,2,1,0:T(8,128)(2,1)S(1)}, bf16[3,4,72,128]{3,2,1,0:T(8,128)(2,1)S(1)}, u32[]{:S(2)}, u32[]{:S(2)}) collective-permute-start(bf16[3,4,72,128]{3,2,1,0:T(8,128)(2,1)S(1)} %get-tuple-element.46), channel_id=1, source_target_pairs={{0,4},{4,0},{8,12},{12,8},{16,20},{20,16},{24,28},{28,24},{1,5},{5... | collective-permute-start | bytes 663560 | tf_op jit(solution)/shard_map/ppermute | solution.py:319
  18.6 7.4 %collective-permute-start.5 = (bf16[368,128]{1,0:T(8,128)(2,1)S(1)}, bf16[368,128]{1,0:T(8,128)(2,1)S(1)}, u32[]{:S(2)}, u32[]{:S(2)}) collective-permute-start(bf16[368,128]{1,0:T(8,128)(2,1)S(1)} %pad_maximum_fusion), channel_id=1, source_target_pairs={{0,3},{1,2},{2,1},{3,0},{4,7},{5,6},{6,5},{7,4},{8,11},{9,10},{10,... | collective-permute-start | bytes 282632 | tf_op jit(solution)/shard_map/ppermute | solution.py:316
  20.5 5.6 %collective-permute-start.6 = (bf16[368,128]{1,0:T(8,128)(2,1)S(1)}, bf16[368,128]{1,0:T(8,128)(2,1)S(1)}, u32[]{:S(2)}, u32[]{:S(2)}) collective-permute-start(bf16[368,128]{1,0:T(8,128)(2,1)S(1)} %get-tuple-element.50), channel_id=1, source_target_pairs={{0,1},{1,0},{2,3},{3,2},{4,5},{5,4},{6,7},{7,6},{8,9},{9,8},{10,11... | collective-permute-start | bytes 282632 | tf_op jit(solution)/shard_map/ppermute | solution.py:316
  21.1 5.3 %collective-permute-start.7 = (bf16[368,128]{1,0:T(8,128)(2,1)S(1)}, bf16[368,128]{1,0:T(8,128)(2,1)S(1)}, u32[]{:S(2)}, u32[]{:S(2)}) collective-permute-start(bf16[368,128]{1,0:T(8,128)(2,1)S(1)} %get-tuple-element.51), channel_id=1, source_target_pairs={{0,2},{1,3},{2,0},{3,1},{4,6},{5,7},{6,4},{7,5},{8,10},{9,11},{10,... | collective-permute-start | bytes 282632 | tf_op jit(solution)/shard_map/ppermute | solution.py:316
  26.5 5.6 %collective-permute-start.8 = (bf16[72,128]{1,0:T(8,128)(2,1)S(1)}, bf16[72,128]{1,0:T(8,128)(2,1)S(1)}, u32[]{:S(2)}, u32[]{:S(2)}) collective-permute-start(bf16[72,128]{1,0:T(8,128)(2,1)S(1)} %get-tuple-element.54), channel_id=1, source_target_pairs={{0,24},{4,28},{8,16},{12,20},{16,8},{20,12},{24,0},{28,4},{1,25},{... | collective-permute-start | bytes 55304 | tf_op jit(solution)/shard_map/ppermute | solution.py:319
  30.1 3.8 %collective-permute-start.10 = (bf16[72,128]{1,0:T(8,128)(2,1)S(1)}, bf16[72,128]{1,0:T(8,128)(2,1)S(1)}, u32[]{:S(2)}, u32[]{:S(2)}) collective-permute-start(bf16[72,128]{1,0:T(8,128)(2,1)S(1)} %get-tuple-element.55), channel_id=1, source_target_pairs={{0,8},{4,12},{8,0},{12,4},{16,24},{20,28},{24,16},{28,20},{1,9},{5... | collective-permute-start | bytes 55304 | tf_op jit(solution)/shard_map/ppermute | solution.py:319
  30.1 4.7 %collective-permute-start.9 = (bf16[72,128]{1,0:T(8,128)(2,1)S(1)}, bf16[72,128]{1,0:T(8,128)(2,1)S(1)}, u32[]{:S(2)}, u32[]{:S(2)}) collective-permute-start(bf16[72,128]{1,0:T(8,128)(2,1)S(1)} %get-tuple-element.56), channel_id=1, source_target_pairs={{0,16},{4,20},{8,24},{12,28},{16,0},{20,4},{24,8},{28,12},{1,17},{... | collective-permute-start | bytes 55304 | tf_op jit(solution)/shard_map/ppermute | solution.py:319
  31.0 4.4 %copy-start.9 = (f32[16,576]{1,0:T(8,128)}, f32[16,576]{1,0:T(8,128)S(1)}, u32[]{:S(2)}) copy-start(f32[16,576]{1,0:T(8,128)S(1)} %constant_dynamic-update-slice_fusion) | copy-start | bytes 110596

commit v6 on v5

--- a/solution.py
+++ b/solution.py
@@ -237,16 +237,17 @@
 
 
 def sum_kernel(mine_ref, theirs_ref, span_ref, own_ref, *pay_refs):
-    pairs, cols, lanes = mine_ref.shape[1:]
+    pairs = mine_ref.shape[1]
     for d in range(len(pay_refs) + 1):
-        for z in range(pairs):
-            total = mine_ref[d, z].astype(F32) + theirs_ref[d, z].astype(F32)
-            if d == 0:
-                own_ref[z] = total
-            else:
-                pay_refs[d - 1][pl.ds(z * cols, cols), :] = total.astype(BF16)
-        if d:
-            pay_refs[d - 1][pl.ds(pairs * cols, span_ref.shape[1]), :] = span_ref[d]
+        totals = [
+            mine_ref[d, z].astype(F32) + theirs_ref[d, z].astype(F32) for z in range(pairs)
+        ]
+        if d == 0:
+            for z in range(pairs):
+                own_ref[z] = totals[z]
+        else:
+            totals.append(span_ref[d].astype(F32))
+            pay_refs[d - 1][...] = jnp.concatenate(totals, axis=0).astype(BF16)
 
 
 def query_kernel(

time: 35.6 us -> 35.6 us (level)
  no operation moved by 1% of the time
where the time goes in v6:
time: 35.6 us; the launch traced here: 35.4 us
  Pallas kernels  13.9 us (39%)
  starting transfers between devices  13.4 us (38%)
  waiting for transfers between devices  6.35 us (18%)
  between operations  0.94 us (3%)
  other arithmetic  0.72 us (2%)
    pallas_call x1, Pallas kernels, on_device(): pl.pallas_call(functools.partial(keys_kernel, n_resp, n_seq), out_shape=(...  5.58 us
    ppermute x4, starting transfers between devices, over_seq(): return lax.ppermute(x, 'seq', [(i, i ^ d) for i in range(n_seq)])  5.28 us
    ppermute x6, starting transfers between devices, over_resp(): return lax.ppermute(x, 'resp', [(i, i ^ d) for i in range(n_resp)])  5.08 us
    ppermute x6, waiting for transfers between devices, over_resp(): return lax.ppermute(x, 'resp', [(i, i ^ d) for i in range(n_resp)])  4.55 us
    pallas_call x1, Pallas kernels, queries(): pl.pallas_call(functools.partial(query_kernel, heads), out_shape=(shape((...  3.73 us
    ppermute x1, starting transfers between devices, by_core(): return lax.ppermute(x, ('resp', 'seq'), moves)  3 us
    pallas_call x1, Pallas kernels, on_device(): pl.pallas_call(functools.partial(early_kernel, heads), out_shape=(shape((...  2.9 us
    ppermute x4, waiting for transfers between devices, over_seq(): return lax.ppermute(x, 'seq', [(i, i ^ d) for i in range(n_seq)])  1.8 us
  transfers between devices with their start and end apart: 11, of which 6 were waited for; matrix products, arithmetic and copies ran while one was open for 0% of the time, Pallas kernels for 24%

profile of v6, /device:TPU:0, one launch (start us, length us, event | category | flops | bytes accessed | tf_op | source)
XLA Modules:
  0.0 35.4 jit_solution(11602580568425485155)
XLA Ops:
  0.6 0.0 copy-start.3
  0.6 0.0 copy-start.8
  0.7 3.0 %collective-permute-start = (bf16[576,128]{1,0:T(8,128)(2,1)}, bf16[576,128]{1,0:T(8,128)(2,1)S(1)}, u32[]{:S(2)}, u32[]{:S(2)}) collective-permute-start(bf16[576,128]{1,0:T(8,128)(2,1)} %bitcast.43), channel_id=1, source_target_pairs={{0,1},{1,0},{2,3},{3,2},{4,6},{5,7},{6,4},{7,5},{8,9},{9,8},{10,11... | collective-permute-start | bytes 442376 | tf_op jit(solution)/shard_map/ppermute | solution.py:328
  3.8 0.0 copy-done.3
  3.8 1.7 %collective-permute-start.2 = (bf16[576,128]{1,0:T(8,128)(2,1)S(1)}, bf16[576,128]{1,0:T(8,128)(2,1)S(1)}, u32[]{:S(2)}, u32[]{:S(2)}) collective-permute-start(bf16[576,128]{1,0:T(8,128)(2,1)S(1)} %bitcast.44), channel_id=1, source_target_pairs={{0,3},{1,2},{2,1},{3,0},{4,7},{5,6},{6,5},{7,4},{8,11},{9,10},{10,... | collective-permute-start | bytes 442376 | tf_op jit(solution)/shard_map/ppermute | solution.py:317
  5.5 2.9 %early.1 = (bf16[2048,128]{1,0:T(8,128)(2,1)S(1)}, f32[192,2048]{1,0:T(8,128)S(1)}, f32[192,2048]{1,0:T(8,128)S(1)}, f32[8,2048]{1,0:T(8,128)S(1)}, bf16[192,640]{1,0:T(8,128)(2,1)S(1)}) custom-call(s32[16]{0:T(128)S(1)} %copy-done.5, s32[8]{0:T(128)S(1)} %copy-done.6, s32[8]{0:T(128)S(1)} %copy-done.7, f32[64,2048]{1,0:T(8,128)S(1)} %mask.1.mask_ref, ...), custom_call_target="tpu_custom_call" | custom-call | flops 805306368 | bytes 4194304 | tf_op jit(solution)/shard_map/early/pallas_call | solution.py:349
  8.4 0.0 collective-permute-done.refs_0_
  8.4 0.1 collective-permute-start.1
  8.5 1.6 %middle.1 = (f32[128,2048]{1,0:T(8,128)S(1)}, f32[128,2048]{1,0:T(8,128)S(1)}, f32[8,2048]{1,0:T(8,128)S(1)}, bf16[128,640]{1,0:T(8,128)(2,1)S(1)}) custom-call(f32[1,576]{1,0:T(1,128)S(1)} %reshape.47.scale_ref, bf16[2048,512]{1,0:T(8,128)(2,1)S(1)} %bitcast.38, bf16[2048,512]{1,0:T(8,128)(2,1)S(1)} %bitcast.41, ...), custom_call_target="tpu_custom_call" | custom-call | flops 536870912 | bytes 4194304 | tf_op jit(solution)/shard_map/middle/pallas_call | solution.py:382
  10.1 1.5 %collective-permute-done.2.refs_1_ = bf16[576,128]{1,0:T(8,128)(2,1)S(1)} collective-permute-done((bf16[576,128]{1,0:T(8,128)(2,1)S(1)}, bf16[576,128]{1,0:T(8,128)(2,1)S(1)}, u32[]{:S(2)}, u32[]{:S(2)}) %collective-permute-start.2) | collective-permute-done | bytes 147488 | tf_op jit(solution)/shard_map/ppermute | solution.py:317
  11.7 0.0 collective-permute-done.1.refs_0_
  11.7 5.6 %keys.1 = (bf16[4,4,72,128]{3,2,1,0:T(8,128)(2,1)S(1)}, bf16[3,4,72,128]{3,2,1,0:T(8,128)(2,1)S(1)}, bf16[4,72,128]{2,1,0:T(8,128)(2,1)S(1)}, bf16[4,80,128]{2,1...) custom-call(f32[1,576]{1,0:T(1,128)S(1)} %reshape.47.scale_ref, ...), custom_call_target="tpu_custom_call" | custom-call | flops 3623878656 | bytes 4194304 | tf_op jit(solution)/shard_map/keys/pallas_call | solution.py:399
  17.3 0.1 collective-permute-start.4
  17.3 0.5 %collective-permute-start.3 = (bf16[3,4,72,128]{3,2,1,0:T(8,128)(2,1)S(1)}, bf16[3,4,72,128]{3,2,1,0:T(8,128)(2,1)S(1)}, u32[]{:S(2)}, u32[]{:S(2)}) collective-permute-start(bf16[3,4,72,128]{3,2,1,0:T(8,128)(2,1)S(1)} %get-tuple-element.46), channel_id=1, source_target_pairs={{0,4},{4,0},{8,12},{12,8},{16,20},{20,16},{24,28},{28,24},{1,5},{5... | collective-permute-start | bytes 663560 | tf_op jit(solution)/shard_map/ppermute | solution.py:320
  17.8 0.8 %collective-permute-done.4 = bf16[4,72,128]{2,1,0:T(8,128)(2,1)S(1)} collective-permute-done((bf16[4,72,128]{2,1,0:T(8,128)(2,1)S(1)}, bf16[4,72,128]{2,1,0:T(8,128)(2,1)S(1)}, u32[]{:S(2)}, u32[]{:S(2)}) %collective-permute-start.4) | collective-permute-done | bytes 73760 | tf_op jit(solution)/shard_map/ppermute | solution.py:320
  18.6 1.8 %collective-permute-start.5 = (bf16[368,128]{1,0:T(8,128)(2,1)S(1)}, bf16[368,128]{1,0:T(8,128)(2,1)S(1)}, u32[]{:S(2)}, u32[]{:S(2)}) collective-permute-start(bf16[368,128]{1,0:T(8,128)(2,1)S(1)} %pad_maximum_fusion), channel_id=1, source_target_pairs={{0,3},{1,2},{2,1},{3,0},{4,7},{5,6},{6,5},{7,4},{8,11},{9,10},{10,... | collective-permute-start | bytes 282632 | tf_op jit(solution)/shard_map/ppermute | solution.py:317
  20.4 0.0 collective-permute-done.3.theirs_ref
  20.4 0.1 sums.1
  20.5 0.6 %collective-permute-start.6 = (bf16[368,128]{1,0:T(8,128)(2,1)S(1)}, bf16[368,128]{1,0:T(8,128)(2,1)S(1)}, u32[]{:S(2)}, u32[]{:S(2)}) collective-permute-start(bf16[368,128]{1,0:T(8,128)(2,1)S(1)} %get-tuple-element.50), channel_id=1, source_target_pairs={{0,1},{1,0},{2,3},{3,2},{4,5},{5,4},{6,7},{7,6},{8,9},{9,8},{10,11... | collective-permute-start | bytes 282632 | tf_op jit(solution)/shard_map/ppermute | solution.py:317
  21.1 1.2 %collective-permute-start.7 = (bf16[368,128]{1,0:T(8,128)(2,1)S(1)}, bf16[368,128]{1,0:T(8,128)(2,1)S(1)}, u32[]{:S(2)}, u32[]{:S(2)}) collective-permute-start(bf16[368,128]{1,0:T(8,128)(2,1)S(1)} %get-tuple-element.51), channel_id=1, source_target_pairs={{0,2},{1,3},{2,0},{3,1},{4,6},{5,7},{6,4},{7,5},{8,10},{9,11},{10,... | collective-permute-start | bytes 282632 | tf_op jit(solution)/shard_map/ppermute | solution.py:317
  22.3 3.7 %queries.1 = (bf16[2048,512]{1,0:T(8,128)(2,1)}, bf16[64,2048]{1,0:T(8,128)(2,1)}) custom-call(bf16[576,2048]{1,0:T(8,128)(2,1)S(1)} %get-tuple-element.41.ds_ref, bf16[576,640]{1,0:T(8,128)(2,1)S(1)} %get-tuple-element.42.keys_ref), custom_call_target="tpu_custom_call" | custom-call | flops 1509949440 | bytes 2621440 | tf_op jit(solution)/shard_map/queries/pallas_call | solution.py:439
  26.1 0.0 collective-permute-done.5
  26.1 0.0 collective-permute-done.6
  26.1 0.3 collective-permute-done.7
  26.5 3.7 %collective-permute-start.8 = (bf16[72,128]{1,0:T(8,128)(2,1)S(1)}, bf16[72,128]{1,0:T(8,128)(2,1)S(1)}, u32[]{:S(2)}, u32[]{:S(2)}) collective-permute-start(bf16[72,128]{1,0:T(8,128)(2,1)S(1)} %get-tuple-element.54), channel_id=1, source_target_pairs={{0,24},{4,28},{8,16},{12,20},{16,8},{20,12},{24,0},{28,4},{1,25},{... | collective-permute-start | bytes 55304 | tf_op jit(solution)/shard_map/ppermute | solution.py:320
  30.1 0.0 collective-permute-start.10
  30.1 0.8 %collective-permute-start.9 = (bf16[72,128]{1,0:T(8,128)(2,1)S(1)}, bf16[72,128]{1,0:T(8,128)(2,1)S(1)}, u32[]{:S(2)}, u32[]{:S(2)}) collective-permute-start(bf16[72,128]{1,0:T(8,128)(2,1)S(1)} %get-tuple-element.56), channel_id=1, source_target_pairs={{0,16},{4,20},{8,24},{12,28},{16,0},{20,4},{24,8},{28,12},{1,17},{... | collective-permute-start | bytes 55304 | tf_op jit(solution)/shard_map/ppermute | solution.py:320
  31.0 0.0 copy-start.9
  31.0 1.1 %collective-permute-done.8 = bf16[72,128]{1,0:T(8,128)(2,1)S(1)} collective-permute-done((bf16[72,128]{1,0:T(8,128)(2,1)S(1)}, bf16[72,128]{1,0:T(8,128)(2,1)S(1)}, u32[]{:S(2)}, u32[]{:S(2)}) %collective-permute-start.8) | collective-permute-done | bytes 18464 | tf_op jit(solution)/shard_map/ppermute | solution.py:320
  32.1 1.8 %collective-permute-done.10 = bf16[72,128]{1,0:T(8,128)(2,1)S(1)} collective-permute-done((bf16[72,128]{1,0:T(8,128)(2,1)S(1)}, bf16[72,128]{1,0:T(8,128)(2,1)S(1)}, u32[]{:S(2)}, u32[]{:S(2)}) %collective-permute-start.10) | collective-permute-done | bytes 18464 | tf_op jit(solution)/shard_map/ppermute | solution.py:320
  33.9 0.9 %collective-permute-done.9 = bf16[72,128]{1,0:T(8,128)(2,1)S(1)} collective-permute-done((bf16[72,128]{1,0:T(8,128)(2,1)S(1)}, bf16[72,128]{1,0:T(8,128)(2,1)S(1)}, u32[]{:S(2)}, u32[]{:S(2)}) %collective-permute-start.9) | collective-permute-done | bytes 18464 | tf_op jit(solution)/shard_map/ppermute | solution.py:320
  34.8 0.6 %fusion.6 = f32[128,72]{0,1:T(8,128)} fusion(f32[4,72,128]{2,1,0:T(8,128)S(1)} %get-tuple-element.53, bf16[72,128]{1,0:T(8,128)(2,1)S(1)} %collective-permute-done.10, bf16[72,128]{1,0:T(8,128)(2,1)S(1)} %collective-permute-done.9, bf16[72,128]{1,0:T(8,128)(2,1)S(1)} %collective-permute-done.8), kind=kLoop, calls=%fused_computation.13 | loop fusion | flops 55296 | bytes 129024 | tf_op jit(solution)/shard_map/transpose | solution.py:489
  (32 shorter events, 0.2 us)
Async XLA Ops:
  0.6 3.1 %copy-start.3 = (bf16[128,576]{0,1:T(8,128)(2,1)S(1)}, bf16[128,576]{0,1:T(8,128)(2,1)}, u32[]{:S(2)}) copy-start(bf16[128,576]{0,1:T(8,128)(2,1)} %param.9) | copy-start | bytes 442372
  0.6 4.8 %copy-start.8 = (f32[576]{0:T(1024)S(1)}, f32[576]{0:T(1024)}, u32[]{:S(2)}) copy-start(f32[576]{0:T(1024)} %param.10) | copy-start | bytes 6916
  0.7 4.8 %copy-start = (bf16[64,32,512]{2,1,0:T(8,128)(2,1)S(1)}, bf16[64,32,512]{2,1,0:T(8,128)(2,1)}, u32[]{:S(2)}) copy-start(bf16[64,32,512]{2,1,0:T(8,128)(2,1)} %param.12) | copy-start | bytes 6291460
  0.7 4.8 %copy-start.1 = (bf16[64,32,512]{2,1,0:T(8,128)(2,1)S(1)}, bf16[64,32,512]{2,1,0:T(8,128)(2,1)}, u32[]{:S(2)}) copy-start(bf16[64,32,512]{2,1,0:T(8,128)(2,1)} %param.14) | copy-start | bytes 6291460
  0.7 4.8 %copy-start.2 = (bf16[64,2048]{1,0:T(8,128)(2,1)S(1)}, bf16[64,2048]{1,0:T(8,128)(2,1)}, u32[]{:S(2)}) copy-start(bf16[64,2048]{1,0:T(8,128)(2,1)} %qrope_v.1) | copy-start | bytes 786436
  0.7 4.8 %copy-start.4 = (bf16[64,576]{1,0:T(8,128)(2,1)S(1)}, bf16[64,576]{1,0:T(8,128)(2,1)}, u32[]{:S(2)}) copy-start(bf16[64,576]{1,0:T(8,128)(2,1)} %span_ref.1) | copy-start | bytes 221188
  0.7 4.8 %copy-start.5 = (s32[16]{0:T(128)S(1)}, s32[16]{0:T(128)}, u32[]{:S(2)}) copy-start(s32[16]{0:T(128)} %length_s.1) | copy-start | bytes 196
  0.7 4.8 %copy-start.6 = (s32[8]{0:T(128)S(1)}, s32[8]{0:T(128)}, u32[]{:S(2)}) copy-start(s32[8]{0:T(128)} %response_s.1) | copy-start | bytes 100
  0.7 4.8 %copy-start.7 = (s32[8]{0:T(128)S(1)}, s32[8]{0:T(128)}, u32[]{:S(2)}) copy-start(s32[8]{0:T(128)} %index_s.1) | copy-start | bytes 100
  0.7 7.7 %collective-permute-start = (bf16[576,128]{1,0:T(8,128)(2,1)}, bf16[576,128]{1,0:T(8,128)(2,1)S(1)}, u32[]{:S(2)}, u32[]{:S(2)}) collective-permute-start(bf16[576,128]{1,0:T(8,128)(2,1)} %bitcast.43), channel_id=1, source_target_pairs={{0,1},{1,0},{2,3},{3,2},{4,6},{5,7},{6,4},{7,5},{8,9},{9,8},{10,11... | collective-permute-start | bytes 442376 | tf_op jit(solution)/shard_map/ppermute | solution.py:328
  3.8 7.9 %collective-permute-start.2 = (bf16[576,128]{1,0:T(8,128)(2,1)S(1)}, bf16[576,128]{1,0:T(8,128)(2,1)S(1)}, u32[]{:S(2)}, u32[]{:S(2)}) collective-permute-start(bf16[576,128]{1,0:T(8,128)(2,1)S(1)} %bitcast.44), channel_id=1, source_target_pairs={{0,3},{1,2},{2,1},{3,0},{4,7},{5,6},{6,5},{7,4},{8,11},{9,10},{10,... | collective-permute-start | bytes 442376 | tf_op jit(solution)/shard_map/ppermute | solution.py:317
  8.4 3.2 %collective-permute-start.1 = (bf16[576,128]{1,0:T(8,128)(2,1)S(1)}, bf16[576,128]{1,0:T(8,128)(2,1)S(1)}, u32[]{:S(2)}, u32[]{:S(2)}) collective-permute-start(bf16[576,128]{1,0:T(8,128)(2,1)S(1)} %collective-permute-done.refs_0_), channel_id=1, source_target_pairs={{0,4},{4,0},{8,12},{12,8},{16,20},{20,16},{24,28},{28,24},{1,5},{5... | collective-permute-start | bytes 442376 | tf_op jit(solution)/shard_map/ppermute | solution.py:320
  17.3 1.3 %collective-permute-start.4 = (bf16[4,72,128]{2,1,0:T(8,128)(2,1)S(1)}, bf16[4,72,128]{2,1,0:T(8,128)(2,1)S(1)}, u32[]{:S(2)}, u32[]{:S(2)}) collective-permute-start(bf16[4,72,128]{2,1,0:T(8,128)(2,1)S(1)} %get-tuple-element.49), channel_id=1, source_target_pairs={{0,4},{4,0},{8,12},{12,8},{16,20},{20,16},{24,28},{28,24},{1,5},{5... | collective-permute-start | bytes 221192 | tf_op jit(solution)/shard_map/ppermute | solution.py:320
  17.3 3.1 %collective-permute-start.3 = (bf16[3,4,72,128]{3,2,1,0:T(8,128)(2,1)S(1)}, bf16[3,4,72,128]{3,2,1,0:T(8,128)(2,1)S(1)}, u32[]{:S(2)}, u32[]{:S(2)}) collective-permute-start(bf16[3,4,72,128]{3,2,1,0:T(8,128)(2,1)S(1)} %get-tuple-element.46), channel_id=1, source_target_pairs={{0,4},{4,0},{8,12},{12,8},{16,20},{20,16},{24,28},{28,24},{1,5},{5... | collective-permute-start | bytes 663560 | tf_op jit(solution)/shard_map/ppermute | solution.py:320
  18.6 7.4 %collective-permute-start.5 = (bf16[368,128]{1,0:T(8,128)(2,1)S(1)}, bf16[368,128]{1,0:T(8,128)(2,1)S(1)}, u32[]{:S(2)}, u32[]{:S(2)}) collective-permute-start(bf16[368,128]{1,0:T(8,128)(2,1)S(1)} %pad_maximum_fusion), channel_id=1, source_target_pairs={{0,3},{1,2},{2,1},{3,0},{4,7},{5,6},{6,5},{7,4},{8,11},{9,10},{10,... | collective-permute-start | bytes 282632 | tf_op jit(solution)/shard_map/ppermute | solution.py:317
  20.5 5.6 %collective-permute-start.6 = (bf16[368,128]{1,0:T(8,128)(2,1)S(1)}, bf16[368,128]{1,0:T(8,128)(2,1)S(1)}, u32[]{:S(2)}, u32[]{:S(2)}) collective-permute-start(bf16[368,128]{1,0:T(8,128)(2,1)S(1)} %get-tuple-element.50), channel_id=1, source_target_pairs={{0,1},{1,0},{2,3},{3,2},{4,5},{5,4},{6,7},{7,6},{8,9},{9,8},{10,11... | collective-permute-start | bytes 282632 | tf_op jit(solution)/shard_map/ppermute | solution.py:317
  21.1 5.3 %collective-permute-start.7 = (bf16[368,128]{1,0:T(8,128)(2,1)S(1)}, bf16[368,128]{1,0:T(8,128)(2,1)S(1)}, u32[]{:S(2)}, u32[]{:S(2)}) collective-permute-start(bf16[368,128]{1,0:T(8,128)(2,1)S(1)} %get-tuple-element.51), channel_id=1, source_target_pairs={{0,2},{1,3},{2,0},{3,1},{4,6},{5,7},{6,4},{7,5},{8,10},{9,11},{10,... | collective-permute-start | bytes 282632 | tf_op jit(solution)/shard_map/ppermute | solution.py:317
  26.5 5.6 %collective-permute-start.8 = (bf16[72,128]{1,0:T(8,128)(2,1)S(1)}, bf16[72,128]{1,0:T(8,128)(2,1)S(1)}, u32[]{:S(2)}, u32[]{:S(2)}) collective-permute-start(bf16[72,128]{1,0:T(8,128)(2,1)S(1)} %get-tuple-element.54), channel_id=1, source_target_pairs={{0,24},{4,28},{8,16},{12,20},{16,8},{20,12},{24,0},{28,4},{1,25},{... | collective-permute-start | bytes 55304 | tf_op jit(solution)/shard_map/ppermute | solution.py:320
  30.1 3.8 %collective-permute-start.10 = (bf16[72,128]{1,0:T(8,128)(2,1)S(1)}, bf16[72,128]{1,0:T(8,128)(2,1)S(1)}, u32[]{:S(2)}, u32[]{:S(2)}) collective-permute-start(bf16[72,128]{1,0:T(8,128)(2,1)S(1)} %get-tuple-element.55), channel_id=1, source_target_pairs={{0,8},{4,12},{8,0},{12,4},{16,24},{20,28},{24,16},{28,20},{1,9},{5... | collective-permute-start | bytes 55304 | tf_op jit(solution)/shard_map/ppermute | solution.py:320
  30.1 4.7 %collective-permute-start.9 = (bf16[72,128]{1,0:T(8,128)(2,1)S(1)}, bf16[72,128]{1,0:T(8,128)(2,1)S(1)}, u32[]{:S(2)}, u32[]{:S(2)}) collective-permute-start(bf16[72,128]{1,0:T(8,128)(2,1)S(1)} %get-tuple-element.56), channel_id=1, source_target_pairs={{0,16},{4,20},{8,24},{12,28},{16,0},{20,4},{24,8},{28,12},{1,17},{... | collective-permute-start | bytes 55304 | tf_op jit(solution)/shard_map/ppermute | solution.py:320
  31.0 4.4 %copy-start.9 = (f32[16,576]{1,0:T(8,128)}, f32[16,576]{1,0:T(8,128)S(1)}, u32[]{:S(2)}) copy-start(f32[16,576]{1,0:T(8,128)S(1)} %constant_dynamic-update-slice_fusion) | copy-start | bytes 110596

commit v7 on v6

--- a/solution.py
+++ b/solution.py
@@ -482,7 +482,8 @@
         block = block + x[:split].reshape(pairs, cols, shard).astype(F32)
         own = own + x[split:].astype(F32)
     block_half = block.astype(BF16)
-    arrived = [over_resp(block_half[d], 2 * d) for d in range(pairs - 1, 0, -1)]
+    order = sorted(range(1, pairs), key=lambda d: (d != pairs // 2, d))
+    arrived = [over_resp(block_half[d], 2 * d) for d in order]
     total = block[0]
     for x in arrived:
         total = total + x.astype(F32)

time: 35.6 us -> 35.5 us (level)
  transfers between devices with their start and end apart: 11 -> 11, of which waited for: 6 -> 5; matrix products, arithmetic and copies ran while one was open for 0% -> 0% of each run, Pallas kernels for 24% -> 24%
where the time goes in v7:
time: 35.5 us; the launch traced here: 35.3 us
  Pallas kernels  13.9 us (39%)
  starting transfers between devices  13.1 us (37%)
  waiting for transfers between devices  6.46 us (18%)
  between operations  0.94 us (3%)
  other arithmetic  0.72 us (2%)
    pallas_call x1, Pallas kernels, on_device(): pl.pallas_call(functools.partial(keys_kernel, n_resp, n_seq), out_shape=(...  5.58 us
    ppermute x4, starting transfers between devices, over_seq(): return lax.ppermute(x, 'seq', [(i, i ^ d) for i in range(n_seq)])  5.28 us
    ppermute x6, starting transfers between devices, over_resp(): return lax.ppermute(x, 'resp', [(i, i ^ d) for i in range(n_resp)])  4.86 us
    ppermute x6, waiting for transfers between devices, over_resp(): return lax.ppermute(x, 'resp', [(i, i ^ d) for i in range(n_resp)])  4.65 us
    pallas_call x1, Pallas kernels, queries(): pl.pallas_call(functools.partial(query_kernel, heads), out_shape=(shape((...  3.73 us
    ppermute x1, starting transfers between devices, by_core(): return lax.ppermute(x, ('resp', 'seq'), moves)  3 us
    pallas_call x1, Pallas kernels, on_device(): pl.pallas_call(functools.partial(early_kernel, heads), out_shape=(shape((...  2.9 us
    ppermute x4, waiting for transfers between devices, over_seq(): return lax.ppermute(x, 'seq', [(i, i ^ d) for i in range(n_seq)])  1.8 us
  transfers between devices with their start and end apart: 11, of which 5 were waited for; matrix products, arithmetic and copies ran while one was open for 0% of the time, Pallas kernels for 24%

profile of v7, /device:TPU:0, one launch (start us, length us, event | category | flops | bytes accessed | tf_op | source)
XLA Modules:
  0.0 35.3 jit_solution(6252679453668415780)
XLA Ops:
  0.6 0.0 copy-start.3
  0.6 0.0 copy-start.8
  0.7 0.0 copy-start
  0.7 3.0 %collective-permute-start = (bf16[576,128]{1,0:T(8,128)(2,1)}, bf16[576,128]{1,0:T(8,128)(2,1)S(1)}, u32[]{:S(2)}, u32[]{:S(2)}) collective-permute-start(bf16[576,128]{1,0:T(8,128)(2,1)} %bitcast.43), channel_id=1, source_target_pairs={{0,1},{1,0},{2,3},{3,2},{4,6},{5,7},{6,4},{7,5},{8,9},{9,8},{10,11... | collective-permute-start | bytes 442376 | tf_op jit(solution)/shard_map/ppermute | solution.py:328
  3.8 1.7 %collective-permute-start.2 = (bf16[576,128]{1,0:T(8,128)(2,1)S(1)}, bf16[576,128]{1,0:T(8,128)(2,1)S(1)}, u32[]{:S(2)}, u32[]{:S(2)}) collective-permute-start(bf16[576,128]{1,0:T(8,128)(2,1)S(1)} %bitcast.44), channel_id=1, source_target_pairs={{0,3},{1,2},{2,1},{3,0},{4,7},{5,6},{6,5},{7,4},{8,11},{9,10},{10,... | collective-permute-start | bytes 442376 | tf_op jit(solution)/shard_map/ppermute | solution.py:317
  5.5 2.9 %early.1 = (bf16[2048,128]{1,0:T(8,128)(2,1)S(1)}, f32[192,2048]{1,0:T(8,128)S(1)}, f32[192,2048]{1,0:T(8,128)S(1)}, f32[8,2048]{1,0:T(8,128)S(1)}, bf16[192,640]{1,0:T(8,128)(2,1)S(1)}) custom-call(s32[16]{0:T(128)S(1)} %copy-done.5, s32[8]{0:T(128)S(1)} %copy-done.6, s32[8]{0:T(128)S(1)} %copy-done.7, f32[64,2048]{1,0:T(8,128)S(1)} %mask.1.mask_ref, ...), custom_call_target="tpu_custom_call" | custom-call | flops 805306368 | bytes 4194304 | tf_op jit(solution)/shard_map/early/pallas_call | solution.py:349
  8.4 0.0 collective-permute-done.refs_0_
  8.4 0.1 collective-permute-start.1
  8.5 1.6 %middle.1 = (f32[128,2048]{1,0:T(8,128)S(1)}, f32[128,2048]{1,0:T(8,128)S(1)}, f32[8,2048]{1,0:T(8,128)S(1)}, bf16[128,640]{1,0:T(8,128)(2,1)S(1)}) custom-call(f32[1,576]{1,0:T(1,128)S(1)} %reshape.47.scale_ref, bf16[2048,512]{1,0:T(8,128)(2,1)S(1)} %bitcast.38, bf16[2048,512]{1,0:T(8,128)(2,1)S(1)} %bitcast.41, ...), custom_call_target="tpu_custom_call" | custom-call | flops 536870912 | bytes 4194304 | tf_op jit(solution)/shard_map/middle/pallas_call | solution.py:382
  10.1 1.5 %collective-permute-done.2.refs_1_ = bf16[576,128]{1,0:T(8,128)(2,1)S(1)} collective-permute-done((bf16[576,128]{1,0:T(8,128)(2,1)S(1)}, bf16[576,128]{1,0:T(8,128)(2,1)S(1)}, u32[]{:S(2)}, u32[]{:S(2)}) %collective-permute-start.2) | collective-permute-done | bytes 147488 | tf_op jit(solution)/shard_map/ppermute | solution.py:317
  11.7 0.0 collective-permute-done.1.refs_0_
  11.7 5.6 %keys.1 = (bf16[4,4,72,128]{3,2,1,0:T(8,128)(2,1)S(1)}, bf16[3,4,72,128]{3,2,1,0:T(8,128)(2,1)S(1)}, bf16[4,72,128]{2,1,0:T(8,128)(2,1)S(1)}, bf16[4,80,128]{2,1...) custom-call(f32[1,576]{1,0:T(1,128)S(1)} %reshape.47.scale_ref, ...), custom_call_target="tpu_custom_call" | custom-call | flops 3623878656 | bytes 4194304 | tf_op jit(solution)/shard_map/keys/pallas_call | solution.py:399
  17.3 0.1 collective-permute-start.4
  17.3 0.5 %collective-permute-start.3 = (bf16[3,4,72,128]{3,2,1,0:T(8,128)(2,1)S(1)}, bf16[3,4,72,128]{3,2,1,0:T(8,128)(2,1)S(1)}, u32[]{:S(2)}, u32[]{:S(2)}) collective-permute-start(bf16[3,4,72,128]{3,2,1,0:T(8,128)(2,1)S(1)} %get-tuple-element.46), channel_id=1, source_target_pairs={{0,4},{4,0},{8,12},{12,8},{16,20},{20,16},{24,28},{28,24},{1,5},{5... | collective-permute-start | bytes 663560 | tf_op jit(solution)/shard_map/ppermute | solution.py:320
  17.8 0.8 %collective-permute-done.4 = bf16[4,72,128]{2,1,0:T(8,128)(2,1)S(1)} collective-permute-done((bf16[4,72,128]{2,1,0:T(8,128)(2,1)S(1)}, bf16[4,72,128]{2,1,0:T(8,128)(2,1)S(1)}, u32[]{:S(2)}, u32[]{:S(2)}) %collective-permute-start.4) | collective-permute-done | bytes 73760 | tf_op jit(solution)/shard_map/ppermute | solution.py:320
  18.6 1.8 %collective-permute-start.5 = (bf16[368,128]{1,0:T(8,128)(2,1)S(1)}, bf16[368,128]{1,0:T(8,128)(2,1)S(1)}, u32[]{:S(2)}, u32[]{:S(2)}) collective-permute-start(bf16[368,128]{1,0:T(8,128)(2,1)S(1)} %pad_maximum_fusion), channel_id=1, source_target_pairs={{0,3},{1,2},{2,1},{3,0},{4,7},{5,6},{6,5},{7,4},{8,11},{9,10},{10,... | collective-permute-start | bytes 282632 | tf_op jit(solution)/shard_map/ppermute | solution.py:317
  20.4 0.0 collective-permute-done.3.theirs_ref
  20.4 0.1 sums.1
  20.5 0.6 %collective-permute-start.6 = (bf16[368,128]{1,0:T(8,128)(2,1)S(1)}, bf16[368,128]{1,0:T(8,128)(2,1)S(1)}, u32[]{:S(2)}, u32[]{:S(2)}) collective-permute-start(bf16[368,128]{1,0:T(8,128)(2,1)S(1)} %get-tuple-element.50), channel_id=1, source_target_pairs={{0,1},{1,0},{2,3},{3,2},{4,5},{5,4},{6,7},{7,6},{8,9},{9,8},{10,11... | collective-permute-start | bytes 282632 | tf_op jit(solution)/shard_map/ppermute | solution.py:317
  21.1 1.2 %collective-permute-start.7 = (bf16[368,128]{1,0:T(8,128)(2,1)S(1)}, bf16[368,128]{1,0:T(8,128)(2,1)S(1)}, u32[]{:S(2)}, u32[]{:S(2)}) collective-permute-start(bf16[368,128]{1,0:T(8,128)(2,1)S(1)} %get-tuple-element.51), channel_id=1, source_target_pairs={{0,2},{1,3},{2,0},{3,1},{4,6},{5,7},{6,4},{7,5},{8,10},{9,11},{10,... | collective-permute-start | bytes 282632 | tf_op jit(solution)/shard_map/ppermute | solution.py:317
  22.3 3.7 %queries.1 = (bf16[2048,512]{1,0:T(8,128)(2,1)}, bf16[64,2048]{1,0:T(8,128)(2,1)}) custom-call(bf16[576,2048]{1,0:T(8,128)(2,1)S(1)} %get-tuple-element.41.ds_ref, bf16[576,640]{1,0:T(8,128)(2,1)S(1)} %get-tuple-element.42.keys_ref), custom_call_target="tpu_custom_call" | custom-call | flops 1509949440 | bytes 2621440 | tf_op jit(solution)/shard_map/queries/pallas_call | solution.py:439
  26.1 0.0 collective-permute-done.5
  26.1 0.0 collective-permute-done.6
  26.1 0.3 collective-permute-done.7
  26.5 2.7 %collective-permute-start.8 = (bf16[72,128]{1,0:T(8,128)(2,1)S(1)}, bf16[72,128]{1,0:T(8,128)(2,1)S(1)}, u32[]{:S(2)}, u32[]{:S(2)}) collective-permute-start(bf16[72,128]{1,0:T(8,128)(2,1)S(1)} %get-tuple-element.54), channel_id=1, source_target_pairs={{0,16},{4,20},{8,24},{12,28},{16,0},{20,4},{24,8},{28,12},{1,17},{... | collective-permute-start | bytes 55304 | tf_op jit(solution)/shard_map/ppermute | solution.py:320
  29.1 1.3 %collective-permute-start.10 = (bf16[72,128]{1,0:T(8,128)(2,1)S(1)}, bf16[72,128]{1,0:T(8,128)(2,1)S(1)}, u32[]{:S(2)}, u32[]{:S(2)}) collective-permute-start(bf16[72,128]{1,0:T(8,128)(2,1)S(1)} %get-tuple-element.55), channel_id=1, source_target_pairs={{0,24},{4,28},{8,16},{12,20},{16,8},{20,12},{24,0},{28,4},{1,25},{... | collective-permute-start | bytes 55304 | tf_op jit(solution)/shard_map/ppermute | solution.py:320
  30.5 0.2 collective-permute-start.9
  30.8 0.0 copy-start.9
  30.8 0.4 %collective-permute-done.8 = bf16[72,128]{1,0:T(8,128)(2,1)S(1)} collective-permute-done((bf16[72,128]{1,0:T(8,128)(2,1)S(1)}, bf16[72,128]{1,0:T(8,128)(2,1)S(1)}, u32[]{:S(2)}, u32[]{:S(2)}) %collective-permute-start.8) | collective-permute-done | bytes 18464 | tf_op jit(solution)/shard_map/ppermute | solution.py:320
  31.2 3.5 %collective-permute-done.10 = bf16[72,128]{1,0:T(8,128)(2,1)S(1)} collective-permute-done((bf16[72,128]{1,0:T(8,128)(2,1)S(1)}, bf16[72,128]{1,0:T(8,128)(2,1)S(1)}, u32[]{:S(2)}, u32[]{:S(2)}) %collective-permute-start.10) | collective-permute-done | bytes 18464 | tf_op jit(solution)/shard_map/ppermute | solution.py:320
  34.7 0.0 collective-permute-done.9
  34.7 0.6 %fusion.6 = f32[128,72]{0,1:T(8,128)} fusion(f32[4,72,128]{2,1,0:T(8,128)S(1)} %get-tuple-element.53, bf16[72,128]{1,0:T(8,128)(2,1)S(1)} %collective-permute-done.10, bf16[72,128]{1,0:T(8,128)(2,1)S(1)} %collective-permute-done.9, bf16[72,128]{1,0:T(8,128)(2,1)S(1)} %collective-permute-done.8), kind=kLoop, calls=%fused_computation.13 | loop fusion | flops 55296 | bytes 129024 | tf_op jit(solution)/shard_map/transpose | solution.py:490
  (32 shorter events, 0.2 us)
Async XLA Ops:
  0.6 3.1 %copy-start.3 = (bf16[128,576]{0,1:T(8,128)(2,1)S(1)}, bf16[128,576]{0,1:T(8,128)(2,1)}, u32[]{:S(2)}) copy-start(bf16[128,576]{0,1:T(8,128)(2,1)} %param.9) | copy-start | bytes 442372
  0.6 4.8 %copy-start.8 = (f32[576]{0:T(1024)S(1)}, f32[576]{0:T(1024)}, u32[]{:S(2)}) copy-start(f32[576]{0:T(1024)} %param.10) | copy-start | bytes 6916
  0.7 4.8 %copy-start = (bf16[64,32,512]{2,1,0:T(8,128)(2,1)S(1)}, bf16[64,32,512]{2,1,0:T(8,128)(2,1)}, u32[]{:S(2)}) copy-start(bf16[64,32,512]{2,1,0:T(8,128)(2,1)} %param.12) | copy-start | bytes 6291460
  0.7 4.8 %copy-start.1 = (bf16[64,32,512]{2,1,0:T(8,128)(2,1)S(1)}, bf16[64,32,512]{2,1,0:T(8,128)(2,1)}, u32[]{:S(2)}) copy-start(bf16[64,32,512]{2,1,0:T(8,128)(2,1)} %param.14) | copy-start | bytes 6291460
  0.7 4.8 %copy-start.2 = (bf16[64,2048]{1,0:T(8,128)(2,1)S(1)}, bf16[64,2048]{1,0:T(8,128)(2,1)}, u32[]{:S(2)}) copy-start(bf16[64,2048]{1,0:T(8,128)(2,1)} %qrope_v.1) | copy-start | bytes 786436
  0.7 4.8 %copy-start.4 = (bf16[64,576]{1,0:T(8,128)(2,1)S(1)}, bf16[64,576]{1,0:T(8,128)(2,1)}, u32[]{:S(2)}) copy-start(bf16[64,576]{1,0:T(8,128)(2,1)} %span_ref.1) | copy-start | bytes 221188
  0.7 4.8 %copy-start.5 = (s32[16]{0:T(128)S(1)}, s32[16]{0:T(128)}, u32[]{:S(2)}) copy-start(s32[16]{0:T(128)} %length_s.1) | copy-start | bytes 196
  0.7 4.8 %copy-start.6 = (s32[8]{0:T(128)S(1)}, s32[8]{0:T(128)}, u32[]{:S(2)}) copy-start(s32[8]{0:T(128)} %response_s.1) | copy-start | bytes 100
  0.7 4.8 %copy-start.7 = (s32[8]{0:T(128)S(1)}, s32[8]{0:T(128)}, u32[]{:S(2)}) copy-start(s32[8]{0:T(128)} %index_s.1) | copy-start | bytes 100
  0.7 7.7 %collective-permute-start = (bf16[576,128]{1,0:T(8,128)(2,1)}, bf16[576,128]{1,0:T(8,128)(2,1)S(1)}, u32[]{:S(2)}, u32[]{:S(2)}) collective-permute-start(bf16[576,128]{1,0:T(8,128)(2,1)} %bitcast.43), channel_id=1, source_target_pairs={{0,1},{1,0},{2,3},{3,2},{4,6},{5,7},{6,4},{7,5},{8,9},{9,8},{10,11... | collective-permute-start | bytes 442376 | tf_op jit(solution)/shard_map/ppermute | solution.py:328
  3.8 7.9 %collective-permute-start.2 = (bf16[576,128]{1,0:T(8,128)(2,1)S(1)}, bf16[576,128]{1,0:T(8,128)(2,1)S(1)}, u32[]{:S(2)}, u32[]{:S(2)}) collective-permute-start(bf16[576,128]{1,0:T(8,128)(2,1)S(1)} %bitcast.44), channel_id=1, source_target_pairs={{0,3},{1,2},{2,1},{3,0},{4,7},{5,6},{6,5},{7,4},{8,11},{9,10},{10,... | collective-permute-start | bytes 442376 | tf_op jit(solution)/shard_map/ppermute | solution.py:317
  8.4 3.2 %collective-permute-start.1 = (bf16[576,128]{1,0:T(8,128)(2,1)S(1)}, bf16[576,128]{1,0:T(8,128)(2,1)S(1)}, u32[]{:S(2)}, u32[]{:S(2)}) collective-permute-start(bf16[576,128]{1,0:T(8,128)(2,1)S(1)} %collective-permute-done.refs_0_), channel_id=1, source_target_pairs={{0,4},{4,0},{8,12},{12,8},{16,20},{20,16},{24,28},{28,24},{1,5},{5... | collective-permute-start | bytes 442376 | tf_op jit(solution)/shard_map/ppermute | solution.py:320
  17.3 1.3 %collective-permute-start.4 = (bf16[4,72,128]{2,1,0:T(8,128)(2,1)S(1)}, bf16[4,72,128]{2,1,0:T(8,128)(2,1)S(1)}, u32[]{:S(2)}, u32[]{:S(2)}) collective-permute-start(bf16[4,72,128]{2,1,0:T(8,128)(2,1)S(1)} %get-tuple-element.49), channel_id=1, source_target_pairs={{0,4},{4,0},{8,12},{12,8},{16,20},{20,16},{24,28},{28,24},{1,5},{5... | collective-permute-start | bytes 221192 | tf_op jit(solution)/shard_map/ppermute | solution.py:320
  17.3 3.1 %collective-permute-start.3 = (bf16[3,4,72,128]{3,2,1,0:T(8,128)(2,1)S(1)}, bf16[3,4,72,128]{3,2,1,0:T(8,128)(2,1)S(1)}, u32[]{:S(2)}, u32[]{:S(2)}) collective-permute-start(bf16[3,4,72,128]{3,2,1,0:T(8,128)(2,1)S(1)} %get-tuple-element.46), channel_id=1, source_target_pairs={{0,4},{4,0},{8,12},{12,8},{16,20},{20,16},{24,28},{28,24},{1,5},{5... | collective-permute-start | bytes 663560 | tf_op jit(solution)/shard_map/ppermute | solution.py:320
  18.6 7.4 %collective-permute-start.5 = (bf16[368,128]{1,0:T(8,128)(2,1)S(1)}, bf16[368,128]{1,0:T(8,128)(2,1)S(1)}, u32[]{:S(2)}, u32[]{:S(2)}) collective-permute-start(bf16[368,128]{1,0:T(8,128)(2,1)S(1)} %pad_maximum_fusion), channel_id=1, source_target_pairs={{0,3},{1,2},{2,1},{3,0},{4,7},{5,6},{6,5},{7,4},{8,11},{9,10},{10,... | collective-permute-start | bytes 282632 | tf_op jit(solution)/shard_map/ppermute | solution.py:317
  20.5 5.6 %collective-permute-start.6 = (bf16[368,128]{1,0:T(8,128)(2,1)S(1)}, bf16[368,128]{1,0:T(8,128)(2,1)S(1)}, u32[]{:S(2)}, u32[]{:S(2)}) collective-permute-start(bf16[368,128]{1,0:T(8,128)(2,1)S(1)} %get-tuple-element.50), channel_id=1, source_target_pairs={{0,1},{1,0},{2,3},{3,2},{4,5},{5,4},{6,7},{7,6},{8,9},{9,8},{10,11... | collective-permute-start | bytes 282632 | tf_op jit(solution)/shard_map/ppermute | solution.py:317
  21.1 5.3 %collective-permute-start.7 = (bf16[368,128]{1,0:T(8,128)(2,1)S(1)}, bf16[368,128]{1,0:T(8,128)(2,1)S(1)}, u32[]{:S(2)}, u32[]{:S(2)}) collective-permute-start(bf16[368,128]{1,0:T(8,128)(2,1)S(1)} %get-tuple-element.51), channel_id=1, source_target_pairs={{0,2},{1,3},{2,0},{3,1},{4,6},{5,7},{6,4},{7,5},{8,10},{9,11},{10,... | collective-permute-start | bytes 282632 | tf_op jit(solution)/shard_map/ppermute | solution.py:317
  26.5 4.7 %collective-permute-start.8 = (bf16[72,128]{1,0:T(8,128)(2,1)S(1)}, bf16[72,128]{1,0:T(8,128)(2,1)S(1)}, u32[]{:S(2)}, u32[]{:S(2)}) collective-permute-start(bf16[72,128]{1,0:T(8,128)(2,1)S(1)} %get-tuple-element.54), channel_id=1, source_target_pairs={{0,16},{4,20},{8,24},{12,28},{16,0},{20,4},{24,8},{28,12},{1,17},{... | collective-permute-start | bytes 55304 | tf_op jit(solution)/shard_map/ppermute | solution.py:320
  29.1 5.6 %collective-permute-start.10 = (bf16[72,128]{1,0:T(8,128)(2,1)S(1)}, bf16[72,128]{1,0:T(8,128)(2,1)S(1)}, u32[]{:S(2)}, u32[]{:S(2)}) collective-permute-start(bf16[72,128]{1,0:T(8,128)(2,1)S(1)} %get-tuple-element.55), channel_id=1, source_target_pairs={{0,24},{4,28},{8,16},{12,20},{16,8},{20,12},{24,0},{28,4},{1,25},{... | collective-permute-start | bytes 55304 | tf_op jit(solution)/shard_map/ppermute | solution.py:320
  30.5 4.2 %collective-permute-start.9 = (bf16[72,128]{1,0:T(8,128)(2,1)S(1)}, bf16[72,128]{1,0:T(8,128)(2,1)S(1)}, u32[]{:S(2)}, u32[]{:S(2)}) collective-permute-start(bf16[72,128]{1,0:T(8,128)(2,1)S(1)} %get-tuple-element.56), channel_id=1, source_target_pairs={{0,8},{4,12},{8,0},{12,4},{16,24},{20,28},{24,16},{28,20},{1,9},{5... | collective-permute-start | bytes 55304 | tf_op jit(solution)/shard_map/ppermute | solution.py:320
  30.8 4.5 %copy-start.9 = (f32[16,576]{1,0:T(8,128)}, f32[16,576]{1,0:T(8,128)S(1)}, u32[]{:S(2)}) copy-start(f32[16,576]{1,0:T(8,128)S(1)} %constant_dynamic-update-slice_fusion) | copy-start | bytes 110596
